TPU v7x, 256 devices: a whole 4x4x8 slice. The times are simulated.
256 devices in a mesh: row: 16 (over y_hi, z), col: 16 (over x, y_lo, core).
Axes of the slice: x: 4, y: 4 (y_hi: 2, y_lo: 2; y = y_hi * 2 + y_lo), z: 8, core: 2. Of those that a mesh axis runs over, the one named last changes fastest.
Arguments:
- covariance: bfloat16 [8192, 131072], P('row', 'col'), may hold values from -6 to 6
- operator_rows: bfloat16 [512, 131072], P('row', 'col'), may hold values from -0.015625 to 0.015625
- row_index: int32 [512], replicated, may hold values from 0 to 511, each once
Outputs:
- cross_cov: bfloat16 [8192, 512], P(('row', 'col'))
Inputs may be any that keep to these rules, and one draw needn't show every extreme that they name: `row_index`: each stored row is named by exactly one observation.
All inputs are finite; a program needn't handle non-finite values.
Results may differ from a plain program's by a relative error of at most 0.0015.
Values may be sent and summed in bfloat16 or wider, within the bound.
No kernel may reach another device: no remote copies, remote signals or barrier semaphores. Data moves between devices by JAX's collectives and lax.ppermute only.
A program may use at most 64 MiB of HBM per device.

v0:
```python
import jax
import jax.numpy as jnp
from jax import lax
from jax.sharding import PartitionSpec as P


def pick_rows(shard_rows, first, row_index):
    height = shard_rows.shape[0]
    offset = row_index - first
    inside = (offset >= 0) & (offset < height)
    picked = jnp.take(shard_rows, jnp.clip(offset, 0, height - 1), axis=0)
    return jnp.where(inside[:, None], picked.astype(jnp.float32), 0.0)


def on_device(covariance, operator_rows, row_index):
    first_own = lax.axis_index("row") * operator_rows.shape[0]
    masked = pick_rows(operator_rows, first_own, row_index)
    selected = lax.psum(masked.astype(jnp.bfloat16), "row").astype(jnp.float32)
    selected = selected.astype(jnp.bfloat16)
    partial_sums = jnp.einsum("rk,ok->ro", covariance, selected, preferred_element_type=jnp.float32)
    summed = lax.psum_scatter(partial_sums, "col", scatter_dimension=0, tiled=True)
    return summed.astype(jnp.bfloat16)


def solution(mesh):
    in_specs = (P("row", "col"), P("row", "col"), P())
    out_specs = P(("row", "col"), None)
    return jax.shard_map(
        on_device, mesh=mesh, in_specs=in_specs, out_specs=out_specs, check_vma=False
    )
```

profile of v0, /device:TPU:1, one launch (start us, length us, event | category | flops | bytes accessed | tf_op | source)
XLA Modules:
  0.0 313.5 jit_solution(16465811440026535792)
XLA Ops:
  6.5 0.0 copy-start
  6.5 0.0 all-reduce.2.cloned.1.call-start
  6.5 0.7 compare_and_fusion
  7.3 0.3 copy-done
  7.6 7.8 %gather_fusion = bf16[512,8192]{1,0:T(8,128)(2,1)} fusion(bf16[32,8192]{1,0:T(8,128)(2,1)S(1)} %copy-done, s32[1024]{0:T(1024)S(1)} %pad_clamp_fusion), kind=kCustom, calls=%fused_computation | custom fusion | bytes 16779264 | tf_op jit(solution)/shard_map/jit(_take)/gather | solution.py:11
  15.4 12.5 %select_convert_fusion = bf16[512,8192]{1,0:T(8,128)(2,1)} fusion(bf16[512,8192]{1,0:T(8,128)(2,1)} %gather_fusion, pred[512]{0:T(512)(128)(4,1)S(1)} %get-tuple-element.5, pred[512]{0:T(512)(128)(4,1)S(1)} %get-tuple-element.7), kind=kLoop, calls=%fused_computation.1 | loop fusion | flops 16777216 | bytes 16778240 | tf_op jit(solution)/shard_map/convert_element_type | solution.py:18
  27.9 0.0 all-reduce.2.cloned.1.call-update
  27.9 0.0 reduce-scatter.4.cloned.1.call-start
  28.0 209.2 %all-reduce.2.cloned.1.call-done = bf16[512,8192]{1,0:T(8,128)(2,1)} async-done(((bf16[512,8192]{1,0:T(8,128)(2,1)}), bf16[512,8192]{1,0:T(8,128)(2,1)}) %all-reduce.2.cloned.1.call-update) | async-done | bytes 8388624 | tf_op jit(solution)/shard_map/psum | solution.py:18
  237.1 9.5 %convolution_bitcast_fusion = f32[512,512]{0,1:T(8,128)S(1)} fusion(bf16[512,8192]{1,0:T(8,128)(2,1)} %all-reduce.2.cloned.1.call-done, bf16[512,8192]{1,0:T(8,128)(2,1)} %param.3), kind=kOutput, calls=%fused_computation.2 | convolution fusion | flops 4294967296 | bytes 17825792 | tf_op jit(solution)/shard_map/rk,ok->ro/dot_general | solution.py:20
  246.6 1.3 copy.7
  247.9 0.0 reduce-scatter.4.cloned.1.call-update
  248.0 57.2 %reduce-scatter.4.cloned.1.call-done = f32[32,512]{1,0:T(8,128)} async-done(((f32[512,512]{1,0:T(8,128)}), f32[32,512]{1,0:T(8,128)}) %reduce-scatter.4.cloned.1.call-update) | async-done | bytes 65552 | tf_op jit(solution)/shard_map/reduce_scatter | solution.py:21
  305.2 1.5 convert_element_type.13
  (1 shorter events, 0.0 us)
Async XLA Ops:
  6.5 1.1 copy-start
  6.5 230.6 %all-reduce.2.cloned.1.call-start = ((), (), s32[]{:S(2)}) async-start(), calls=%async_computation.1 | async-start | bytes 16777216 | tf_op jit(solution)/shard_map/psum | solution.py:18
  27.9 277.2 %reduce-scatter.4.cloned.1.call-start = ((), (), s32[]{:S(2)}) async-start(), calls=%async_computation.2 | async-start | bytes 1114112 | tf_op jit(solution)/shard_map/reduce_scatter | solution.py:21
Sparse Core Ops, SparseCore 0:
  28.0 209.0 all-reduce.1
  248.1 57.0 reduce-scatter.3
where the time goes:
time: 316 us; the launch traced here: 313 us
  waiting for transfers between devices  266 us (84%)
  other arithmetic  14.7 us (5%)
  between operations  13.4 us (4%)
  matrix products  9.5 us (3%)
  local copies, waits for them, and re-layouts  9.4 us (3%)
    psum x1, waiting for transfers between devices, on_device(): selected = lax.psum(masked.astype(jnp.bfloat16), 'row').astype(jnp.float32)  209 us
    reduce_scatter x1, waiting for transfers between devices, on_device(): lax.psum_scatter(partial_sums, 'col', scatter_dimension=0, tiled=True)  57.2 us
    convert_element_type x1, other arithmetic, on_device(): selected = lax.psum(masked.astype(jnp.bfloat16), 'row').astype(jnp.float32)  12.5 us
    dot_general x1, matrix products, on_device(): jnp.einsum('rk,ok->ro', covariance, selected, preferred_element_type=jnp....  9.5 us
    gather x1, local copies, waits for them, and re-layouts, pick_rows(): picked = jnp.take(shard_rows, jnp.clip(offset, 0, height - 1), axis=0)  7.79 us
  transfers between devices with their start and end apart: 2, of which 2 were waited for; matrix products, arithmetic and copies ran while one was open for 0% of the time, Pallas kernels for 0%

commit v1 on v0

v1 whole, which is shorter than its diff:
```python
import functools

import jax
import jax.numpy as jnp
import numpy as np
from jax import lax
from jax.experimental import pallas as pl
from jax.experimental.pallas import tpu as pltpu
from jax.sharding import PartitionSpec as P

BOTH = ("row", "col")
XS, YS, ZS, CORES = 4, 4, 8, 2
UNIT = 16
STEP_K = 1024


def index_of(x, y, z, core):
    return ((y // 2) * ZS + z) * 16 + x * 4 + (y % 2) * 2 + core


def moved(values, target):
    pairs = []
    for place in np.ndindex(XS, YS, ZS, CORES):
        x, y, z, core = target(*place)
        pairs.append((index_of(*place), index_of(x % XS, y % YS, z % ZS, core)))
    return lax.ppermute(values, BOTH, pairs)


def ahead(x, y, z, core):
    return x, y, z + 1 - 2 * core, core


def behind(x, y, z, core):
    return x, y, z - 1 + 2 * core, core


def across(x, y, z, core):
    return x, y + 2, z, core


def other_core(x, y, z, core):
    return x, y, z, 1 - core


GROUPS = (
    tuple((0, u) for u in "ABPQ") + ((1, "A"), (-1, "A"), (1, "B"), (-1, "B")),
    ((1, "P"), (-1, "P"), (1, "Q"), (-1, "Q"), (2, "A"), (-2, "A"), (2, "B"), (-2, "B")),
    ((2, "P"), (-2, "P"), (2, "Q"), (-2, "Q"), (3, "A"), (-3, "A"), (3, "B"), (-3, "B")),
    ((3, "P"), (-3, "P"), (3, "Q"), (-3, "Q")) + tuple((4, u) for u in "ABPQ"),
)


def product_kernel(slots, core_ref, cov_ref, *refs):
    chunks, (keep_ref, send_ref, total) = refs[: len(slots)], refs[len(slots) :]
    step = pl.program_id(0)
    core = core_ref[0]
    at = {slot: n for n, slot in enumerate(slots)}
    rows = []
    for n, (k, unit) in enumerate(slots):
        if k in (0, 4):
            rows.append(chunks[n][...])
        else:
            rows.append(jnp.where(core == 0, chunks[n][...], chunks[at[-k, unit]][...]))
    part = lax.dot_general(
        cov_ref[...], jnp.concatenate(rows, 0), (((1,), (1,)), ((), ())),
        preferred_element_type=jnp.float32,
    )

    @pl.when(step == 0)
    def _():
        total[...] = part

    @pl.when(step > 0)
    def _():
        total[...] += part

    @pl.when(step == pl.num_programs(0) - 1)
    def _():
        for n in range(8):
            here = pl.ds(n * 32, 32)
            keep_ref[here, :] = total[pl.ds((2 * n + core) * 32, 32), :]
            send_ref[here, :] = total[pl.ds((2 * n + 1 - core) * 32, 32), :]


def product(core, covariance, slots, chunks):
    height, depth = covariance.shape
    width = UNIT * len(slots)
    half = jax.ShapeDtypeStruct((height // 2, width), jnp.float32)
    whole = pl.BlockSpec((height // 2, width), lambda i: (0, 0))
    return pl.pallas_call(
        functools.partial(product_kernel, slots),
        grid=(depth // STEP_K,),
        in_specs=[pl.BlockSpec(memory_space=pltpu.SMEM), pl.BlockSpec((height, STEP_K), lambda i: (0, i))]
        + [pl.BlockSpec((UNIT, STEP_K), lambda i: (0, i))] * len(slots),
        out_specs=[whole, whole],
        out_shape=[half, half],
        scratch_shapes=[pltpu.VMEM((height, width), jnp.float32)],
        compiler_params=pltpu.CompilerParams(vmem_limit_bytes=16 * 1024 * 1024),
        cost_estimate=pl.CostEstimate(
            flops=2 * height * width * depth,
            bytes_accessed=2 * depth * (height + width),
            transcendentals=0,
        ),
    )(core, covariance, *chunks)


def on_device(covariance, operator_rows, row_index):
    row, col = lax.axis_index("row"), lax.axis_index("col")
    core = col % 2
    got = {(0, "A"): operator_rows[:UNIT], (0, "B"): operator_rows[UNIT:]}
    got[0, "P"] = moved(got[0, "A"], across)
    got[0, "Q"] = moved(got[0, "B"], across)
    for k in (1, 2, 3, 4):
        for unit in "BAP":
            got[k, unit] = moved(got[k - 1, unit], ahead)
            if k < 4:
                got[-k, unit] = moved(got[1 - k, unit], behind)
            if unit == "B":
                got[k, "Q"] = moved(got[k, "B"], across)
                if k < 4:
                    got[-k, "Q"] = moved(got[-k, "B"], across)

    core_of = jnp.full((1,), core, jnp.int32)
    keeps, sends = zip(*(product(core_of, covariance, g, [got[s] for s in g]) for g in GROUPS))
    came = moved(jnp.concatenate(sends, 1), other_core)
    sums = (jnp.concatenate(keeps, 1) + came).reshape(8, 32, -1)
    groups = [[2 * n + c for n in range(8)] for c in range(2)]
    summed = lax.all_to_all(sums, "col", 0, 0, axis_index_groups=groups).sum(0)

    slots = [s for g in GROUPS for s in g]
    shift = np.repeat([-k for k, _ in slots], UNIT)
    far = np.repeat([u in "PQ" for _, u in slots], UNIT).astype(np.int32)
    first = np.repeat([UNIT * (u in "BQ") for _, u in slots], UNIT) + np.tile(np.arange(UNIT), len(slots))
    y_hi, z = row // ZS, row % ZS
    stored = (((y_hi + far) % 2) * ZS + (z + shift) % ZS) * (2 * UNIT) + first
    places = (stored[:, None] == row_index[None, :]).astype(jnp.bfloat16)
    ordered = jnp.dot(summed.astype(jnp.bfloat16), places, preferred_element_type=jnp.float32)
    return ordered.astype(jnp.bfloat16)


def solution(mesh):
    in_specs = (P("row", "col"), P("row", "col"), P())
    out_specs = P(BOTH, None)
    return jax.shard_map(on_device, mesh=mesh, in_specs=in_specs, out_specs=out_specs, check_vma=False)
```

time: 316 us -> 115 us (0.36)
  waiting for transfers between devices: 266 us -> 23.6 us
  starting transfers between devices: 0.04 us -> 57.4 us
  Pallas kernels: 0 us -> 22.8 us
  other arithmetic: 14.7 us -> 0.98 us
  between operations: 13.4 us -> 0.26 us
  matrix products: 9.5 us -> 0.97 us
    psum x1 -> x0, waiting for transfers between devices: 209 us -> none  [on_device(): selected = lax.psum(masked.astype(jnp.bfloat16), 'row').astype(jnp.float32)]
    reduce_scatter x1 -> x0, waiting for transfers between devices: 57.2 us -> none  [on_device(): lax.psum_scatter(partial_sums, 'col', scatter_dimension=0, tiled=True)]
    ppermute x0 -> x31, starting transfers between devices: none -> 53.3 us  [moved(): return lax.ppermute(values, BOTH, pairs)]
    pallas_call x0 -> x4, Pallas kernels: none -> 22.8 us  [product(): pl.pallas_call(functools.partial(product_kernel, slots), grid=(depth // S...]
    ppermute x0 -> x31, waiting for transfers between devices: none -> 14.4 us  [moved(): return lax.ppermute(values, BOTH, pairs)]
    convert_element_type x2 -> x0, other arithmetic: 14 us -> none  [the longest x1 12.5 us: on_device(): selected = lax.psum(masked.astype(jnp.bfloat16), 'row').astype(jnp.float32)]
    all_to_all x0 -> x1, waiting for transfers between devices: none -> 9.16 us  [on_device(): summed = lax.all_to_all(sums, 'col', 0, 0, axis_index_groups=groups).sum(0)]
    dot_general x1, matrix products: 9.5 us -> 0.97 us  [on_device(): jnp.dot(summed.astype(jnp.bfloat16), places, preferred_element_type=jnp.f...]
  transfers between devices with their start and end apart: 2 -> 32, of which waited for: 2 -> 9; matrix products, arithmetic and copies ran while one was open for 0% -> 0% of each run, Pallas kernels for 0% -> 15%
where the time goes in v1:
time: 115 us; the launch traced here: 113 us
  starting transfers between devices  57.4 us (50%)
  waiting for transfers between devices  23.6 us (21%)
  Pallas kernels  22.8 us (20%)
  local copies, waits for them, and re-layouts  7.3 us (6%)
    ppermute x31, starting transfers between devices, moved(): return lax.ppermute(values, BOTH, pairs)  53.3 us
    pallas_call x4, Pallas kernels, product(): pl.pallas_call(functools.partial(product_kernel, slots), grid=(depth // S...  22.8 us
    ppermute x31, waiting for transfers between devices, moved(): return lax.ppermute(values, BOTH, pairs)  14.4 us
    all_to_all x1, waiting for transfers between devices, on_device(): summed = lax.all_to_all(sums, 'col', 0, 0, axis_index_groups=groups).sum(0)  9.16 us
    unnamed x34, local copies, waits for them, and re-layouts  6.23 us
    all_to_all x1, starting transfers between devices, on_device(): summed = lax.all_to_all(sums, 'col', 0, 0, axis_index_groups=groups).sum(0)  4.04 us
  transfers between devices with their start and end apart: 32, of which 9 were waited for; matrix products, arithmetic and copies ran while one was open for 0% of the time, Pallas kernels for 15%

profile of v1, /device:TPU:1, one launch (start us, length us, event | category | flops | bytes accessed | tf_op | source)
XLA Modules:
  0.0 113.2 jit_solution(6541438829164349897)
XLA Ops:
  0.0 1.1 fusion.10
  1.1 6.5 %collective-permute-start.4 = (bf16[16,8192]{1,0:T(8,128)(2,1)S(1)}, bf16[16,8192]{1,0:T(8,128)(2,1)S(1)}, u32[]{:S(2)}, u32[]{:S(2)}) collective-permute-start(bf16[16,8192]{1,0:T(8,128)(2,1)S(1)} %get-tuple-element.21.refs_1_), channel_id=1, source_target_pairs={{0,16},{1,113},{16,32},{17,1},{32,48},{33,17},{48,64},{49,33},{64,... | collective-permute-start | bytes 786440 | tf_op jit(solution)/shard_map/ppermute | solution.py:26
  7.6 2.9 %collective-permute-start = (bf16[16,8192]{1,0:T(8,128)(2,1)S(1)}, bf16[16,8192]{1,0:T(8,128)(2,1)S(1)}, u32[]{:S(2)}, u32[]{:S(2)}) collective-permute-start(bf16[16,8192]{1,0:T(8,128)(2,1)S(1)} %get-tuple-element.22.refs_0_), channel_id=1, source_target_pairs={{0,128},{1,129},{16,144},{17,145},{32,160},{33,161},{48,176},{49,1... | collective-permute-start | bytes 786440 | tf_op jit(solution)/shard_map/ppermute | solution.py:26
  10.5 2.7 %collective-permute-start.2 = (bf16[16,8192]{1,0:T(8,128)(2,1)S(1)}, bf16[16,8192]{1,0:T(8,128)(2,1)S(1)}, u32[]{:S(2)}, u32[]{:S(2)}) collective-permute-start(bf16[16,8192]{1,0:T(8,128)(2,1)S(1)} %get-tuple-element.22.refs_0_), channel_id=1, source_target_pairs={{0,16},{1,113},{16,32},{17,1},{32,48},{33,17},{48,64},{49,33},{64,... | collective-permute-start | bytes 786440 | tf_op jit(solution)/shard_map/ppermute | solution.py:26
  13.1 2.2 %collective-permute-start.1 = (bf16[16,8192]{1,0:T(8,128)(2,1)S(1)}, bf16[16,8192]{1,0:T(8,128)(2,1)S(1)}, u32[]{:S(2)}, u32[]{:S(2)}) collective-permute-start(bf16[16,8192]{1,0:T(8,128)(2,1)S(1)} %get-tuple-element.21.refs_1_), channel_id=1, source_target_pairs={{0,128},{1,129},{16,144},{17,145},{32,160},{33,161},{48,176},{49,1... | collective-permute-start | bytes 786440 | tf_op jit(solution)/shard_map/ppermute | solution.py:26
  15.3 3.4 %collective-permute-start.12 = (bf16[16,8192]{1,0:T(8,128)(2,1)S(1)}, bf16[16,8192]{1,0:T(8,128)(2,1)S(1)}, u32[]{:S(2)}, u32[]{:S(2)}) collective-permute-start(bf16[16,8192]{1,0:T(8,128)(2,1)S(1)} %collective-permute-done.4.refs_6_), channel_id=1, source_target_pairs={{0,16},{1,113},{16,32},{17,1},{32,48},{33,17},{48,64},{49,33},{64,... | collective-permute-start | bytes 786440 | tf_op jit(solution)/shard_map/ppermute | solution.py:26
  18.8 2.7 %collective-permute-start.6 = (bf16[16,8192]{1,0:T(8,128)(2,1)S(1)}, bf16[16,8192]{1,0:T(8,128)(2,1)S(1)}, u32[]{:S(2)}, u32[]{:S(2)}) collective-permute-start(bf16[16,8192]{1,0:T(8,128)(2,1)S(1)} %collective-permute-done.refs_2_), channel_id=1, source_target_pairs={{0,16},{1,113},{16,32},{17,1},{32,48},{33,17},{48,64},{49,33},{64,... | collective-permute-start | bytes 786440 | tf_op jit(solution)/shard_map/ppermute | solution.py:26
  21.8 2.7 %collective-permute-start.10 = (bf16[16,8192]{1,0:T(8,128)(2,1)S(1)}, bf16[16,8192]{1,0:T(8,128)(2,1)S(1)}, u32[]{:S(2)}, u32[]{:S(2)}) collective-permute-start(bf16[16,8192]{1,0:T(8,128)(2,1)S(1)} %collective-permute-done.2.refs_4_), channel_id=1, source_target_pairs={{0,16},{1,113},{16,32},{17,1},{32,48},{33,17},{48,64},{49,33},{64,... | collective-permute-start | bytes 786440 | tf_op jit(solution)/shard_map/ppermute | solution.py:26
  24.5 3.8 %collective-permute-done.13.refs_7_ = bf16[16,8192]{1,0:T(8,128)(2,1)S(1)} collective-permute-done((bf16[16,8192]{1,0:T(8,128)(2,1)S(1)}, bf16[16,8192]{1,0:T(8,128)(2,1)S(1)}, u32[]{:S(2)}, u32[]{:S(2)}) %collective-permute-start.13) | collective-permute-done | bytes 262176 | tf_op jit(solution)/shard_map/ppermute | solution.py:26
  28.3 1.8 %collective-permute-start.8 = (bf16[16,8192]{1,0:T(8,128)(2,1)S(1)}, bf16[16,8192]{1,0:T(8,128)(2,1)S(1)}, u32[]{:S(2)}, u32[]{:S(2)}) collective-permute-start(bf16[16,8192]{1,0:T(8,128)(2,1)S(1)} %collective-permute-done.4.refs_6_), channel_id=1, source_target_pairs={{0,128},{1,129},{16,144},{17,145},{32,160},{33,161},{48,176},{49,1... | collective-permute-start | bytes 786440 | tf_op jit(solution)/shard_map/ppermute | solution.py:26
  30.1 2.1 %collective-permute-start.9 = (bf16[16,8192]{1,0:T(8,128)(2,1)S(1)}, bf16[16,8192]{1,0:T(8,128)(2,1)S(1)}, u32[]{:S(2)}, u32[]{:S(2)}) collective-permute-start(bf16[16,8192]{1,0:T(8,128)(2,1)S(1)} %collective-permute-done.5.refs_7_), channel_id=1, source_target_pairs={{0,128},{1,129},{16,144},{17,145},{32,160},{33,161},{48,176},{49,1... | collective-permute-start | bytes 786440 | tf_op jit(solution)/shard_map/ppermute | solution.py:26
  32.2 1.7 %collective-permute-done.7.refs_1_ = bf16[16,8192]{1,0:T(8,128)(2,1)S(1)} collective-permute-done((bf16[16,8192]{1,0:T(8,128)(2,1)S(1)}, bf16[16,8192]{1,0:T(8,128)(2,1)S(1)}, u32[]{:S(2)}, u32[]{:S(2)}) %collective-permute-start.7) | collective-permute-done | bytes 262176 | tf_op jit(solution)/shard_map/ppermute | solution.py:26
  35.3 3.5 %collective-permute-done.11.refs_5_ = bf16[16,8192]{1,0:T(8,128)(2,1)} collective-permute-done((bf16[16,8192]{1,0:T(8,128)(2,1)S(1)}, bf16[16,8192]{1,0:T(8,128)(2,1)}, u32[]{:S(2)}, u32[]{:S(2)}) %collective-permute-start.11) | collective-permute-done | bytes 262176 | tf_op jit(solution)/shard_map/ppermute | solution.py:26
  39.5 1.5 %collective-permute-start.15 = (bf16[16,8192]{1,0:T(8,128)(2,1)S(1)}, bf16[16,8192]{1,0:T(8,128)(2,1)S(1)}, u32[]{:S(2)}, u32[]{:S(2)}) collective-permute-start(bf16[16,8192]{1,0:T(8,128)(2,1)S(1)} %collective-permute-done.7.refs_1_), channel_id=1, source_target_pairs={{0,112},{1,17},{16,0},{17,33},{32,16},{33,49},{48,32},{49,65},{64,... | collective-permute-start | bytes 786440 | tf_op jit(solution)/shard_map/ppermute | solution.py:26
  42.1 2.6 %collective-permute-start.16 = (bf16[16,8192]{1,0:T(8,128)(2,1)S(1)}, bf16[16,8192]{1,0:T(8,128)(2,1)S(1)}, u32[]{:S(2)}, u32[]{:S(2)}) collective-permute-start(bf16[16,8192]{1,0:T(8,128)(2,1)S(1)} %collective-permute-done.12.refs_6_), channel_id=1, source_target_pairs={{0,128},{1,129},{16,144},{17,145},{32,160},{33,161},{48,176},{49,1... | collective-permute-start | bytes 786440 | tf_op jit(solution)/shard_map/ppermute | solution.py:26
  45.1 1.2 %collective-permute-start.18 = (bf16[16,8192]{1,0:T(8,128)(2,1)S(1)}, bf16[16,8192]{1,0:T(8,128)(2,1)}, u32[]{:S(2)}, u32[]{:S(2)}) collective-permute-start(bf16[16,8192]{1,0:T(8,128)(2,1)S(1)} %collective-permute-done.10.refs_4_), channel_id=1, source_target_pairs={{0,16},{1,113},{16,32},{17,1},{32,48},{33,17},{48,64},{49,33},{64,... | collective-permute-start | bytes 786440 | tf_op jit(solution)/shard_map/ppermute | solution.py:26
  47.1 2.4 %collective-permute-done.15.refs_1_ = bf16[16,8192]{1,0:T(8,128)(2,1)S(1)} collective-permute-done((bf16[16,8192]{1,0:T(8,128)(2,1)S(1)}, bf16[16,8192]{1,0:T(8,128)(2,1)S(1)}, u32[]{:S(2)}, u32[]{:S(2)}) %collective-permute-start.15) | collective-permute-done | bytes 262176 | tf_op jit(solution)/shard_map/ppermute | solution.py:26
  49.4 1.9 %collective-permute-start.27 = (bf16[16,8192]{1,0:T(8,128)(2,1)}, bf16[16,8192]{1,0:T(8,128)(2,1)}, u32[]{:S(2)}, u32[]{:S(2)}) collective-permute-start(bf16[16,8192]{1,0:T(8,128)(2,1)} %collective-permute-done.20.refs_6_), channel_id=1, source_target_pairs={{0,16},{1,113},{16,32},{17,1},{32,48},{33,17},{48,64},{49,33},{64,... | collective-permute-start | bytes 786440 | tf_op jit(solution)/shard_map/ppermute | solution.py:26
  52.0 2.5 %collective-permute-start.24 = (bf16[16,8192]{1,0:T(8,128)(2,1)}, bf16[16,8192]{1,0:T(8,128)(2,1)}, u32[]{:S(2)}, u32[]{:S(2)}) collective-permute-start(bf16[16,8192]{1,0:T(8,128)(2,1)} %collective-permute-done.20.refs_6_), channel_id=1, source_target_pairs={{0,128},{1,129},{16,144},{17,145},{32,160},{33,161},{48,176},{49,1... | collective-permute-start | bytes 786440 | tf_op jit(solution)/shard_map/ppermute | solution.py:26
  55.3 1.6 %collective-permute-start.22 = (bf16[16,8192]{1,0:T(8,128)(2,1)}, bf16[16,8192]{1,0:T(8,128)(2,1)}, u32[]{:S(2)}, u32[]{:S(2)}) collective-permute-start(bf16[16,8192]{1,0:T(8,128)(2,1)} %collective-permute-done.14.refs_0_), channel_id=1, source_target_pairs={{0,16},{1,113},{16,32},{17,1},{32,48},{33,17},{48,64},{49,33},{64,... | collective-permute-start | bytes 786440 | tf_op jit(solution)/shard_map/ppermute | solution.py:26
  56.8 3.0 %collective-permute-start.25 = (bf16[16,8192]{1,0:T(8,128)(2,1)}, bf16[16,8192]{1,0:T(8,128)(2,1)S(1)}, u32[]{:S(2)}, u32[]{:S(2)}) collective-permute-start(bf16[16,8192]{1,0:T(8,128)(2,1)} %copy-done.5), channel_id=1, source_target_pairs={{0,128},{1,129},{16,144},{17,145},{32,160},{33,161},{48,176},{49,1... | collective-permute-start | bytes 786440 | tf_op jit(solution)/shard_map/ppermute | solution.py:26
  59.8 2.7 %collective-permute-start.26 = (bf16[16,8192]{1,0:T(8,128)(2,1)}, bf16[16,8192]{1,0:T(8,128)(2,1)S(1)}, u32[]{:S(2)}, u32[]{:S(2)}) collective-permute-start(bf16[16,8192]{1,0:T(8,128)(2,1)} %collective-permute-done.18.refs_4_), channel_id=1, source_target_pairs={{0,16},{1,113},{16,32},{17,1},{32,48},{33,17},{48,64},{49,33},{64,... | collective-permute-start | bytes 786440 | tf_op jit(solution)/shard_map/ppermute | solution.py:26
  62.9 1.4 %collective-permute-start.28 = (bf16[16,8192]{1,0:T(8,128)(2,1)}, bf16[16,8192]{1,0:T(8,128)(2,1)S(1)}, u32[]{:S(2)}, u32[]{:S(2)}) collective-permute-start(bf16[16,8192]{1,0:T(8,128)(2,1)} %collective-permute-done.22.refs_0_), channel_id=1, source_target_pairs={{0,16},{1,113},{16,32},{17,1},{32,48},{33,17},{48,64},{49,33},{64,... | collective-permute-start | bytes 786440 | tf_op jit(solution)/shard_map/ppermute | solution.py:26
  64.3 3.4 %copy-done = bf16[512,8192]{1,0:T(8,128)(2,1)S(1)} copy-done((bf16[512,8192]{1,0:T(8,128)(2,1)S(1)}, bf16[512,8192]{1,0:T(8,128)(2,1)}, u32[]{:S(2)}) %copy-start) | copy-done | bytes 8388632
  67.7 4.6 %shard_map.64 = (f32[256,128]{1,0:T(8,128)S(1)}, f32[256,128]{1,0:T(8,128)S(1)}) custom-call(s32[1]{0:T(128)} %bitcast.core_ref, bf16[512,8192]{1,0:T(8,128)(2,1)S(1)} %copy-done, bf16[16,8192]{1,0:T(8,128)(2,1)S(1)} %get-tuple-element.22.refs_0_, bf16[16,8192]{1,0:T(8,128)(2,1)S(1)} %get-tuple-element.21.refs_1_, ...), custom_call_target="tpu_custom_call" | custom-call | flops 1073741824 | bytes 10485760 | tf_op jit(solution)/shard_map/pallas_call | solution.py:90
  72.4 6.0 %shard_map.65 = (f32[256,128]{1,0:T(8,128)S(1)}, f32[256,128]{1,0:T(8,128)S(1)}) custom-call(s32[1]{0:T(128)} %bitcast.core_ref, bf16[512,8192]{1,0:T(8,128)(2,1)S(1)} %copy-done, bf16[16,8192]{1,0:T(8,128)(2,1)S(1)} %collective-permute-done.6.refs_0_, bf16[16,8192]{1,0:T(8,128)(2,1)S(1)} %collective-permute-done.7.refs_1_, bf16[16,8192]{1,0:T(8,128)(2,1)S(1)} %copy-done.2, ...), custom_call_target="tpu_custom_call" | custom-call | flops 1073741824 | bytes 10485760 | tf_op jit(solution)/shard_map/pallas_call | solution.py:90
  78.4 6.1 %shard_map.66 = (f32[256,128]{1,0:T(8,128)S(1)}, f32[256,128]{1,0:T(8,128)S(1)}) custom-call(s32[1]{0:T(128)} %bitcast.core_ref, bf16[512,8192]{1,0:T(8,128)(2,1)S(1)} %copy-done, bf16[16,8192]{1,0:T(8,128)(2,1)} %collective-permute-done.14.refs_0_, bf16[16,8192]{1,0:T(8,128)(2,1)S(1)} %copy-done.8, bf16[16,8192]{1,0:T(8,128)(2,1)S(1)} %copy-done.10, ...), custom_call_target="tpu_custom_call" | custom-call | flops 1073741824 | bytes 10485760 | tf_op jit(solution)/shard_map/pallas_call | solution.py:90
  84.6 6.0 %shard_map.67 = (f32[256,128]{1,0:T(8,128)S(1)}, f32[256,128]{1,0:T(8,128)S(1)}) custom-call(s32[1]{0:T(128)} %bitcast.core_ref, bf16[512,8192]{1,0:T(8,128)(2,1)S(1)} %copy-done, bf16[16,8192]{1,0:T(8,128)(2,1)} %collective-permute-done.22.refs_0_, bf16[16,8192]{1,0:T(8,128)(2,1)S(1)} %collective-permute-done.23.refs_1_, ...), custom_call_target="tpu_custom_call" | custom-call | flops 1073741824 | bytes 10485760 | tf_op jit(solution)/shard_map/pallas_call | solution.py:90
  90.7 5.9 %collective-permute-start.30 = (f32[256,512]{1,0:T(8,128)S(1)}, f32[256,512]{1,0:T(8,128)S(1)}, u32[]{:S(2)}, u32[]{:S(2)}) collective-permute-start(f32[256,512]{1,0:T(8,128)S(1)} %pad_maximum_fusion), channel_id=1, source_target_pairs={{0,1},{1,0},{16,17},{17,16},{32,33},{33,32},{48,49},{49,48},{64,65... | collective-permute-start | bytes 1572872 | tf_op jit(solution)/shard_map/ppermute | solution.py:26
  96.6 1.5 %collective-permute-done.30 = f32[256,512]{1,0:T(8,128)S(1)} collective-permute-done((f32[256,512]{1,0:T(8,128)S(1)}, f32[256,512]{1,0:T(8,128)S(1)}, u32[]{:S(2)}, u32[]{:S(2)}) %collective-permute-start.30) | collective-permute-done | bytes 524320 | tf_op jit(solution)/shard_map/ppermute | solution.py:26
  99.0 4.0 %all-to-all-start = ((f32[8,32,512]{2,1,0:T(8,128)}), f32[8,32,512]{2,1,0:T(8,128)S(1)}, u32[]{:S(2)}, u32[]{:S(2)}) async-start(f32[8,32,512]{2,1,0:T(8,128)} %bitcast.1), calls=%async_computation | async-start | bytes 1048576 | tf_op jit(solution)/shard_map/all_to_all | solution.py:128
  103.1 9.2 %all-to-all-done = f32[8,32,512]{2,1,0:T(8,128)S(1)} async-done(((f32[8,32,512]{2,1,0:T(8,128)}), f32[8,32,512]{2,1,0:T(8,128)S(1)}, u32[]{:S(2)}, u32[]{:S(2)}) %all-to-all-start) | async-done | bytes 524320 | tf_op jit(solution)/shard_map/all_to_all | solution.py:128
  (76 shorter events, 8.7 us)
Async XLA Ops:
  1.1 12.1 %collective-permute-start.4 = (bf16[16,8192]{1,0:T(8,128)(2,1)S(1)}, bf16[16,8192]{1,0:T(8,128)(2,1)S(1)}, u32[]{:S(2)}, u32[]{:S(2)}) collective-permute-start(bf16[16,8192]{1,0:T(8,128)(2,1)S(1)} %get-tuple-element.21.refs_1_), channel_id=1, source_target_pairs={{0,16},{1,113},{16,32},{17,1},{32,48},{33,17},{48,64},{49,33},{64,... | collective-permute-start | bytes 786440 | tf_op jit(solution)/shard_map/ppermute | solution.py:26
  7.5 7.8 %collective-permute-start.5 = (bf16[16,8192]{1,0:T(8,128)(2,1)S(1)}, bf16[16,8192]{1,0:T(8,128)(2,1)S(1)}, u32[]{:S(2)}, u32[]{:S(2)}) collective-permute-start(bf16[16,8192]{1,0:T(8,128)(2,1)S(1)} %get-tuple-element.21.refs_1_), channel_id=1, source_target_pairs={{0,112},{1,17},{16,0},{17,33},{32,16},{33,49},{48,32},{49,65},{64,... | collective-permute-start | bytes 786440 | tf_op jit(solution)/shard_map/ppermute | solution.py:26
  7.6 11.2 %collective-permute-start = (bf16[16,8192]{1,0:T(8,128)(2,1)S(1)}, bf16[16,8192]{1,0:T(8,128)(2,1)S(1)}, u32[]{:S(2)}, u32[]{:S(2)}) collective-permute-start(bf16[16,8192]{1,0:T(8,128)(2,1)S(1)} %get-tuple-element.22.refs_0_), channel_id=1, source_target_pairs={{0,128},{1,129},{16,144},{17,145},{32,160},{33,161},{48,176},{49,1... | collective-permute-start | bytes 786440 | tf_op jit(solution)/shard_map/ppermute | solution.py:26
  10.5 8.3 %collective-permute-start.2 = (bf16[16,8192]{1,0:T(8,128)(2,1)S(1)}, bf16[16,8192]{1,0:T(8,128)(2,1)S(1)}, u32[]{:S(2)}, u32[]{:S(2)}) collective-permute-start(bf16[16,8192]{1,0:T(8,128)(2,1)S(1)} %get-tuple-element.22.refs_0_), channel_id=1, source_target_pairs={{0,16},{1,113},{16,32},{17,1},{32,48},{33,17},{48,64},{49,33},{64,... | collective-permute-start | bytes 786440 | tf_op jit(solution)/shard_map/ppermute | solution.py:26
  13.1 8.6 %collective-permute-start.3 = (bf16[16,8192]{1,0:T(8,128)(2,1)S(1)}, bf16[16,8192]{1,0:T(8,128)(2,1)S(1)}, u32[]{:S(2)}, u32[]{:S(2)}) collective-permute-start(bf16[16,8192]{1,0:T(8,128)(2,1)S(1)} %get-tuple-element.22.refs_0_), channel_id=1, source_target_pairs={{0,112},{1,17},{16,0},{17,33},{32,16},{33,49},{48,32},{49,65},{64,... | collective-permute-start | bytes 786440 | tf_op jit(solution)/shard_map/ppermute | solution.py:26
  13.1 8.6 %collective-permute-start.1 = (bf16[16,8192]{1,0:T(8,128)(2,1)S(1)}, bf16[16,8192]{1,0:T(8,128)(2,1)S(1)}, u32[]{:S(2)}, u32[]{:S(2)}) collective-permute-start(bf16[16,8192]{1,0:T(8,128)(2,1)S(1)} %get-tuple-element.21.refs_1_), channel_id=1, source_target_pairs={{0,128},{1,129},{16,144},{17,145},{32,160},{33,161},{48,176},{49,1... | collective-permute-start | bytes 786440 | tf_op jit(solution)/shard_map/ppermute | solution.py:26
  15.3 9.1 %collective-permute-start.12 = (bf16[16,8192]{1,0:T(8,128)(2,1)S(1)}, bf16[16,8192]{1,0:T(8,128)(2,1)S(1)}, u32[]{:S(2)}, u32[]{:S(2)}) collective-permute-start(bf16[16,8192]{1,0:T(8,128)(2,1)S(1)} %collective-permute-done.4.refs_6_), channel_id=1, source_target_pairs={{0,16},{1,113},{16,32},{17,1},{32,48},{33,17},{48,64},{49,33},{64,... | collective-permute-start | bytes 786440 | tf_op jit(solution)/shard_map/ppermute | solution.py:26
  18.8 9.5 %collective-permute-start.13 = (bf16[16,8192]{1,0:T(8,128)(2,1)S(1)}, bf16[16,8192]{1,0:T(8,128)(2,1)S(1)}, u32[]{:S(2)}, u32[]{:S(2)}) collective-permute-start(bf16[16,8192]{1,0:T(8,128)(2,1)S(1)} %collective-permute-done.5.refs_7_), channel_id=1, source_target_pairs={{0,112},{1,17},{16,0},{17,33},{32,16},{33,49},{48,32},{49,65},{64,... | collective-permute-start | bytes 786440 | tf_op jit(solution)/shard_map/ppermute | solution.py:26
  18.8 11.3 %collective-permute-start.6 = (bf16[16,8192]{1,0:T(8,128)(2,1)S(1)}, bf16[16,8192]{1,0:T(8,128)(2,1)S(1)}, u32[]{:S(2)}, u32[]{:S(2)}) collective-permute-start(bf16[16,8192]{1,0:T(8,128)(2,1)S(1)} %collective-permute-done.refs_2_), channel_id=1, source_target_pairs={{0,16},{1,113},{16,32},{17,1},{32,48},{33,17},{48,64},{49,33},{64,... | collective-permute-start | bytes 786440 | tf_op jit(solution)/shard_map/ppermute | solution.py:26
  21.8 12.1 %collective-permute-start.7 = (bf16[16,8192]{1,0:T(8,128)(2,1)S(1)}, bf16[16,8192]{1,0:T(8,128)(2,1)S(1)}, u32[]{:S(2)}, u32[]{:S(2)}) collective-permute-start(bf16[16,8192]{1,0:T(8,128)(2,1)S(1)} %collective-permute-done.refs_2_), channel_id=1, source_target_pairs={{0,112},{1,17},{16,0},{17,33},{32,16},{33,49},{48,32},{49,65},{64,... | collective-permute-start | bytes 786440 | tf_op jit(solution)/shard_map/ppermute | solution.py:26
  21.8 12.9 %collective-permute-start.10 = (bf16[16,8192]{1,0:T(8,128)(2,1)S(1)}, bf16[16,8192]{1,0:T(8,128)(2,1)S(1)}, u32[]{:S(2)}, u32[]{:S(2)}) collective-permute-start(bf16[16,8192]{1,0:T(8,128)(2,1)S(1)} %collective-permute-done.2.refs_4_), channel_id=1, source_target_pairs={{0,16},{1,113},{16,32},{17,1},{32,48},{33,17},{48,64},{49,33},{64,... | collective-permute-start | bytes 786440 | tf_op jit(solution)/shard_map/ppermute | solution.py:26
  24.5 14.3 %collective-permute-start.11 = (bf16[16,8192]{1,0:T(8,128)(2,1)S(1)}, bf16[16,8192]{1,0:T(8,128)(2,1)}, u32[]{:S(2)}, u32[]{:S(2)}) collective-permute-start(bf16[16,8192]{1,0:T(8,128)(2,1)S(1)} %collective-permute-done.3.refs_5_), channel_id=1, source_target_pairs={{0,112},{1,17},{16,0},{17,33},{32,16},{33,49},{48,32},{49,65},{64,... | collective-permute-start | bytes 786440 | tf_op jit(solution)/shard_map/ppermute | solution.py:26
  28.3 10.6 %collective-permute-start.8 = (bf16[16,8192]{1,0:T(8,128)(2,1)S(1)}, bf16[16,8192]{1,0:T(8,128)(2,1)S(1)}, u32[]{:S(2)}, u32[]{:S(2)}) collective-permute-start(bf16[16,8192]{1,0:T(8,128)(2,1)S(1)} %collective-permute-done.4.refs_6_), channel_id=1, source_target_pairs={{0,128},{1,129},{16,144},{17,145},{32,160},{33,161},{48,176},{49,1... | collective-permute-start | bytes 786440 | tf_op jit(solution)/shard_map/ppermute | solution.py:26
  30.1 11.3 %collective-permute-start.9 = (bf16[16,8192]{1,0:T(8,128)(2,1)S(1)}, bf16[16,8192]{1,0:T(8,128)(2,1)S(1)}, u32[]{:S(2)}, u32[]{:S(2)}) collective-permute-start(bf16[16,8192]{1,0:T(8,128)(2,1)S(1)} %collective-permute-done.5.refs_7_), channel_id=1, source_target_pairs={{0,128},{1,129},{16,144},{17,145},{32,160},{33,161},{48,176},{49,1... | collective-permute-start | bytes 786440 | tf_op jit(solution)/shard_map/ppermute | solution.py:26
  33.9 10.8 %collective-permute-start.20 = (bf16[16,8192]{1,0:T(8,128)(2,1)S(1)}, bf16[16,8192]{1,0:T(8,128)(2,1)}, u32[]{:S(2)}, u32[]{:S(2)}) collective-permute-start(bf16[16,8192]{1,0:T(8,128)(2,1)S(1)} %collective-permute-done.12.refs_6_), channel_id=1, source_target_pairs={{0,16},{1,113},{16,32},{17,1},{32,48},{33,17},{48,64},{49,33},{64,... | collective-permute-start | bytes 786440 | tf_op jit(solution)/shard_map/ppermute | solution.py:26
  34.7 10.4 %collective-permute-start.21 = (bf16[16,8192]{1,0:T(8,128)(2,1)S(1)}, bf16[16,8192]{1,0:T(8,128)(2,1)S(1)}, u32[]{:S(2)}, u32[]{:S(2)}) collective-permute-start(bf16[16,8192]{1,0:T(8,128)(2,1)S(1)} %collective-permute-done.13.refs_7_), channel_id=1, source_target_pairs={{0,112},{1,17},{16,0},{17,33},{32,16},{33,49},{48,32},{49,65},{64,... | collective-permute-start | bytes 786440 | tf_op jit(solution)/shard_map/ppermute | solution.py:26
  38.8 8.3 %collective-permute-start.14 = (bf16[16,8192]{1,0:T(8,128)(2,1)S(1)}, bf16[16,8192]{1,0:T(8,128)(2,1)}, u32[]{:S(2)}, u32[]{:S(2)}) collective-permute-start(bf16[16,8192]{1,0:T(8,128)(2,1)S(1)} %collective-permute-done.6.refs_0_), channel_id=1, source_target_pairs={{0,16},{1,113},{16,32},{17,1},{32,48},{33,17},{48,64},{49,33},{64,... | collective-permute-start | bytes 786440 | tf_op jit(solution)/shard_map/ppermute | solution.py:26
  39.5 9.9 %collective-permute-start.15 = (bf16[16,8192]{1,0:T(8,128)(2,1)S(1)}, bf16[16,8192]{1,0:T(8,128)(2,1)S(1)}, u32[]{:S(2)}, u32[]{:S(2)}) collective-permute-start(bf16[16,8192]{1,0:T(8,128)(2,1)S(1)} %collective-permute-done.7.refs_1_), channel_id=1, source_target_pairs={{0,112},{1,17},{16,0},{17,33},{32,16},{33,49},{48,32},{49,65},{64,... | collective-permute-start | bytes 786440 | tf_op jit(solution)/shard_map/ppermute | solution.py:26
  42.1 9.2 %collective-permute-start.16 = (bf16[16,8192]{1,0:T(8,128)(2,1)S(1)}, bf16[16,8192]{1,0:T(8,128)(2,1)S(1)}, u32[]{:S(2)}, u32[]{:S(2)}) collective-permute-start(bf16[16,8192]{1,0:T(8,128)(2,1)S(1)} %collective-permute-done.12.refs_6_), channel_id=1, source_target_pairs={{0,128},{1,129},{16,144},{17,145},{32,160},{33,161},{48,176},{49,1... | collective-permute-start | bytes 786440 | tf_op jit(solution)/shard_map/ppermute | solution.py:26
  44.7 9.9 %collective-permute-start.17 = (bf16[16,8192]{1,0:T(8,128)(2,1)S(1)}, bf16[16,8192]{1,0:T(8,128)(2,1)S(1)}, u32[]{:S(2)}, u32[]{:S(2)}) collective-permute-start(bf16[16,8192]{1,0:T(8,128)(2,1)S(1)} %collective-permute-done.13.refs_7_), channel_id=1, source_target_pairs={{0,128},{1,129},{16,144},{17,145},{32,160},{33,161},{48,176},{49,1... | collective-permute-start | bytes 786440 | tf_op jit(solution)/shard_map/ppermute | solution.py:26
  45.1 11.8 %collective-permute-start.18 = (bf16[16,8192]{1,0:T(8,128)(2,1)S(1)}, bf16[16,8192]{1,0:T(8,128)(2,1)}, u32[]{:S(2)}, u32[]{:S(2)}) collective-permute-start(bf16[16,8192]{1,0:T(8,128)(2,1)S(1)} %collective-permute-done.10.refs_4_), channel_id=1, source_target_pairs={{0,16},{1,113},{16,32},{17,1},{32,48},{33,17},{48,64},{49,33},{64,... | collective-permute-start | bytes 786440 | tf_op jit(solution)/shard_map/ppermute | solution.py:26
  47.1 12.7 %collective-permute-start.19 = (bf16[16,8192]{1,0:T(8,128)(2,1)}, bf16[16,8192]{1,0:T(8,128)(2,1)}, u32[]{:S(2)}, u32[]{:S(2)}) collective-permute-start(bf16[16,8192]{1,0:T(8,128)(2,1)} %collective-permute-done.11.refs_5_), channel_id=1, source_target_pairs={{0,112},{1,17},{16,0},{17,33},{32,16},{33,49},{48,32},{49,65},{64,... | collective-permute-start | bytes 786440 | tf_op jit(solution)/shard_map/ppermute | solution.py:26
  49.4 10.4 %collective-permute-start.27 = (bf16[16,8192]{1,0:T(8,128)(2,1)}, bf16[16,8192]{1,0:T(8,128)(2,1)}, u32[]{:S(2)}, u32[]{:S(2)}) collective-permute-start(bf16[16,8192]{1,0:T(8,128)(2,1)} %collective-permute-done.20.refs_6_), channel_id=1, source_target_pairs={{0,16},{1,113},{16,32},{17,1},{32,48},{33,17},{48,64},{49,33},{64,... | collective-permute-start | bytes 786440 | tf_op jit(solution)/shard_map/ppermute | solution.py:26
  52.0 10.4 %collective-permute-start.24 = (bf16[16,8192]{1,0:T(8,128)(2,1)}, bf16[16,8192]{1,0:T(8,128)(2,1)}, u32[]{:S(2)}, u32[]{:S(2)}) collective-permute-start(bf16[16,8192]{1,0:T(8,128)(2,1)} %collective-permute-done.20.refs_6_), channel_id=1, source_target_pairs={{0,128},{1,129},{16,144},{17,145},{32,160},{33,161},{48,176},{49,1... | collective-permute-start | bytes 786440 | tf_op jit(solution)/shard_map/ppermute | solution.py:26
  55.3 7.6 %collective-permute-start.22 = (bf16[16,8192]{1,0:T(8,128)(2,1)}, bf16[16,8192]{1,0:T(8,128)(2,1)}, u32[]{:S(2)}, u32[]{:S(2)}) collective-permute-start(bf16[16,8192]{1,0:T(8,128)(2,1)} %collective-permute-done.14.refs_0_), channel_id=1, source_target_pairs={{0,16},{1,113},{16,32},{17,1},{32,48},{33,17},{48,64},{49,33},{64,... | collective-permute-start | bytes 786440 | tf_op jit(solution)/shard_map/ppermute | solution.py:26
  56.8 27.8 %collective-permute-start.25 = (bf16[16,8192]{1,0:T(8,128)(2,1)}, bf16[16,8192]{1,0:T(8,128)(2,1)S(1)}, u32[]{:S(2)}, u32[]{:S(2)}) collective-permute-start(bf16[16,8192]{1,0:T(8,128)(2,1)} %copy-done.5), channel_id=1, source_target_pairs={{0,128},{1,129},{16,144},{17,145},{32,160},{33,161},{48,176},{49,1... | collective-permute-start | bytes 786440 | tf_op jit(solution)/shard_map/ppermute | solution.py:26
  59.8 24.8 %collective-permute-start.23 = (bf16[16,8192]{1,0:T(8,128)(2,1)}, bf16[16,8192]{1,0:T(8,128)(2,1)S(1)}, u32[]{:S(2)}, u32[]{:S(2)}) collective-permute-start(bf16[16,8192]{1,0:T(8,128)(2,1)} %copy-done.7), channel_id=1, source_target_pairs={{0,112},{1,17},{16,0},{17,33},{32,16},{33,49},{48,32},{49,65},{64,... | collective-permute-start | bytes 786440 | tf_op jit(solution)/shard_map/ppermute | solution.py:26
  59.8 24.8 %collective-permute-start.26 = (bf16[16,8192]{1,0:T(8,128)(2,1)}, bf16[16,8192]{1,0:T(8,128)(2,1)S(1)}, u32[]{:S(2)}, u32[]{:S(2)}) collective-permute-start(bf16[16,8192]{1,0:T(8,128)(2,1)} %collective-permute-done.18.refs_4_), channel_id=1, source_target_pairs={{0,16},{1,113},{16,32},{17,1},{32,48},{33,17},{48,64},{49,33},{64,... | collective-permute-start | bytes 786440 | tf_op jit(solution)/shard_map/ppermute | solution.py:26
  62.5 22.1 %collective-permute-start.29 = (bf16[16,8192]{1,0:T(8,128)(2,1)}, bf16[16,8192]{1,0:T(8,128)(2,1)S(1)}, u32[]{:S(2)}, u32[]{:S(2)}) collective-permute-start(bf16[16,8192]{1,0:T(8,128)(2,1)} %collective-permute-done.27.refs_5_), channel_id=1, source_target_pairs={{0,128},{1,129},{16,144},{17,145},{32,160},{33,161},{48,176},{49,1... | collective-permute-start | bytes 786440 | tf_op jit(solution)/shard_map/ppermute | solution.py:26
  62.9 21.8 %collective-permute-start.28 = (bf16[16,8192]{1,0:T(8,128)(2,1)}, bf16[16,8192]{1,0:T(8,128)(2,1)S(1)}, u32[]{:S(2)}, u32[]{:S(2)}) collective-permute-start(bf16[16,8192]{1,0:T(8,128)(2,1)} %collective-permute-done.22.refs_0_), channel_id=1, source_target_pairs={{0,16},{1,113},{16,32},{17,1},{32,48},{33,17},{48,64},{49,33},{64,... | collective-permute-start | bytes 786440 | tf_op jit(solution)/shard_map/ppermute | solution.py:26
  90.7 7.4 %collective-permute-start.30 = (f32[256,512]{1,0:T(8,128)S(1)}, f32[256,512]{1,0:T(8,128)S(1)}, u32[]{:S(2)}, u32[]{:S(2)}) collective-permute-start(f32[256,512]{1,0:T(8,128)S(1)} %pad_maximum_fusion), channel_id=1, source_target_pairs={{0,1},{1,0},{16,17},{17,16},{32,33},{33,32},{48,49},{49,48},{64,65... | collective-permute-start | bytes 1572872 | tf_op jit(solution)/shard_map/ppermute | solution.py:26
  99.0 13.2 %all-to-all-start = ((f32[8,32,512]{2,1,0:T(8,128)}), f32[8,32,512]{2,1,0:T(8,128)S(1)}, u32[]{:S(2)}, u32[]{:S(2)}) async-start(f32[8,32,512]{2,1,0:T(8,128)} %bitcast.1), calls=%async_computation | async-start | bytes 1048576 | tf_op jit(solution)/shard_map/all_to_all | solution.py:128
  (17 other events, 158.4 us)

commit v2 on v1

v2 whole, which is shorter than its diff:
```python
import functools

import jax
import jax.numpy as jnp
import numpy as np
from jax import lax
from jax.experimental import pallas as pl
from jax.experimental.pallas import tpu as pltpu
from jax.sharding import PartitionSpec as P

BOTH = ("row", "col")
XS, YS, ZS, CORES = 4, 4, 8, 2
UNIT = 16
STEP_K = 1024


def index_of(x, y, z, core):
    return ((y // 2) * ZS + z) * 16 + x * 4 + (y % 2) * 2 + core


def moved(values, target):
    pairs = []
    for place in np.ndindex(XS, YS, ZS, CORES):
        x, y, z, core = target(*place)
        pairs.append((index_of(*place), index_of(x % XS, y % YS, z % ZS, core)))
    return lax.ppermute(values, BOTH, pairs)


def ahead(x, y, z, core):
    return x, y, z + 1 - 2 * core, core


def behind(x, y, z, core):
    return x, y, z - 1 + 2 * core, core


def across(x, y, z, core):
    return x, y + 2, z, core


def other_core(x, y, z, core):
    return x, y, z, 1 - core


def along(sign):
    return ahead if sign > 0 else behind


def both(k, units):
    return tuple((s, u) for u in units for s in (k, -k))


GROUPS = (
    tuple((0, u) for u in "ABPQ") + both(1, "ABPQ"),
    both(2, "ABPQ"),
    both(3, "ABPQ") + tuple((4, u) for u in "ABPQ"),
)
CROSSINGS = ((0,), (1, -1), (2, -2), (3, -3), (4,))


def place_of(k, unit):
    if unit == "Q":
        group = next(g for g in CROSSINGS if k in g)
        return ("Q", group), UNIT * group.index(k)
    if unit in "AB" and abs(k) < 2:
        return ("S", k), UNIT * (unit == "B")
    if unit in "AP" and abs(k) > 1:
        return ("AP", k), UNIT * (unit == "P")
    return (unit, k), 0


def product_kernel(slots, arrays, held, before, last, core_ref, cov_ref, *refs):
    blocks = dict(zip(arrays, refs))
    total = refs[-1]
    core = core_ref[0]
    for at in range(0, cov_ref.shape[1], STEP_K):
        here = pl.ds(at, STEP_K)
        rows = []
        for k, unit in slots:
            name, first = place_of(k, unit)
            block = blocks[name][pl.ds(first, UNIT), here]
            if k not in (0, 4):
                name, first = place_of(-k, unit)
                block = jnp.where(core == 0, block, blocks[name][pl.ds(first, UNIT), here])
            rows.append(block)
        part = lax.dot_general(
            cov_ref[:, here], jnp.concatenate(rows, 0), (((1,), (1,)), ((), ())),
            preferred_element_type=jnp.float32,
        )
        total[...] = part if at == 0 else total[...] + part
    if last:
        earlier_ref, keep_ref, send_ref = refs[len(arrays) : len(arrays) + 3]
        for n in range(8):
            here = pl.ds(n * 32, 32)
            for out_ref, at in ((keep_ref, (2 * n + core) * 32), (send_ref, (2 * n + 1 - core) * 32)):
                out_ref[here, :before] = earlier_ref[pl.ds(at, 32), :]
                out_ref[here, before:] = total[pl.ds(at, 32), :]
    else:
        out_ref = refs[-2 - held]
        if before:
            out_ref[:, :before] = refs[len(arrays) + held][...]
        out_ref[:, before:] = total[...]


def in_vmem(values):
    return pltpu.with_memory_space_constraint(values, pltpu.VMEM)


def product(core, covariance, group, got, held, earlier=None):
    height, depth = covariance.shape
    slots, last = GROUPS[group], group == len(GROUPS) - 1
    before = 0 if earlier is None else earlier.shape[1]
    width = UNIT * len(slots)
    arrays = list(dict.fromkeys(place_of(*slot)[0] for slot in slots))
    vmem, as_is = pl.BlockSpec(memory_space=pltpu.VMEM), pl.BlockSpec(memory_space=pl.ANY)
    outs = 1 + last
    return pl.pallas_call(
        functools.partial(product_kernel, slots, arrays, len(held), before, last),
        in_specs=[pl.BlockSpec(memory_space=pltpu.SMEM), vmem]
        + [vmem] * len(arrays) + [as_is] * len(held) + [vmem] * (before > 0),
        out_specs=[vmem] * outs + [as_is] * len(held),
        out_shape=[jax.ShapeDtypeStruct((height // outs, before + width), jnp.float32)] * outs
        + [jax.ShapeDtypeStruct(h.shape, h.dtype) for h in held],
        input_output_aliases={2 + len(arrays) + n: outs + n for n in range(len(held))},
        scratch_shapes=[pltpu.VMEM((height, width), jnp.float32)],
        compiler_params=pltpu.CompilerParams(vmem_limit_bytes=6 * 1024 * 1024),
        cost_estimate=pl.CostEstimate(
            flops=2 * height * width * depth,
            bytes_accessed=2 * depth * (height + width),
            transcendentals=0,
        ),
    )(
        core, covariance, *(in_vmem(got[a]) for a in arrays), *held,
        *([in_vmem(earlier)] if before else []),
    )


def on_device(covariance, operator_rows, row_index):
    row, col = lax.axis_index("row"), lax.axis_index("col")
    core_of = jnp.full((1,), col % 2, jnp.int32)
    resident = in_vmem(covariance)
    got = {("S", 0): operator_rows}

    def send(unit, k):
        for sign in (1, -1) if k < 3 else (1,):
            got[unit, sign * (k + 1)] = moved(got[unit, sign * k], along(sign))

    def split(k):
        for step in sorted({k, -k}):
            got["A", step], got["B", step] = got["S", step][:UNIT], got["S", step][UNIT:]

    def rows_across(n):
        return jnp.concatenate([got["B", k] for k in CROSSINGS[n]], 0)

    def send_across(n, rows):
        got["Q", CROSSINGS[n]] = moved(rows, across)

    split(0)
    send("S", 0)
    got["P", 0] = moved(got["A", 0], across)
    send_across(0, rows_across(0))
    send("P", 0)
    split(1)
    send("B", 1)
    send_across(1, rows_across(1))
    for s in (1, -1):
        got["AP", s] = jnp.concatenate([got["A", s], got["P", s]], 0)
    send("AP", 1)
    send("B", 2)
    send_across(2, rows_across(2))
    send("AP", 2)
    send("B", 3)
    some, rows = product(core_of, resident, 0, got, [rows_across(3)])
    send_across(3, rows)
    most, rows = product(core_of, resident, 1, got, [rows_across(4)], some)
    send_across(4, rows)
    send("AP", 3)
    keep, sent = product(core_of, resident, 2, got, [], most)

    came = moved(sent, other_core)
    sums = (keep + came).reshape(8, 32, keep.shape[1])
    groups = [[2 * n + c for n in range(8)] for c in range(2)]
    apart = lax.all_to_all(sums, "col", 0, 0, axis_index_groups=groups)
    summed = apart.sum(0).astype(jnp.bfloat16)

    slots = [s for g in GROUPS for s in g]
    shift = np.repeat([-k for k, _ in slots], UNIT)
    far = np.repeat([u in "PQ" for _, u in slots], UNIT).astype(np.int32)
    first = np.repeat([UNIT * (u in "BQ") for _, u in slots], UNIT) + np.tile(np.arange(UNIT), len(slots))
    y_hi, z = row // ZS, row % ZS
    stored = (((y_hi + far) % 2) * ZS + (z + shift) % ZS) * (2 * UNIT) + first
    places = (stored[:, None] == row_index[None, :]).astype(jnp.bfloat16)
    ordered = jnp.dot(summed, places, preferred_element_type=jnp.float32)
    return ordered.astype(jnp.bfloat16)


def solution(mesh):
    in_specs = (P("row", "col"), P("row", "col"), P())
    out_specs = P(BOTH, None)
    return jax.shard_map(on_device, mesh=mesh, in_specs=in_specs, out_specs=out_specs, check_vma=False)
```

time: 115 us -> 95.7 us (0.83); the launches traced: 113 us -> 95.4 us
  starting transfers between devices: 57.4 us -> 38.9 us
  waiting for transfers between devices: 23.6 us -> 41.8 us
  Pallas kernels: 22.8 us -> 7.81 us
  local copies, waits for them, and re-layouts: 7.3 us -> 4.57 us
    ppermute x31 -> x21, starting transfers between devices: 53.3 us -> 34.7 us  [moved(): return lax.ppermute(values, BOTH, pairs)]
    ppermute x31 -> x21, waiting for transfers between devices: 14.4 us -> 32.7 us  [moved(): return lax.ppermute(values, BOTH, pairs)]
    pallas_call x4 -> x3, Pallas kernels: 22.8 us -> 7.81 us  [product(): pl.pallas_call(functools.partial(product_kernel, slots, arrays, len(held)...]
    unnamed x34 -> x15, local copies, waits for them, and re-layouts: 6.23 us -> 3.43 us
  transfers between devices with their start and end apart: 32 -> 22, of which waited for: 9 -> 10; matrix products, arithmetic and copies ran while one was open for 0% -> 1% of each run, Pallas kernels for 15% -> 5%
where the time goes in v2:
time: 95.7 us; the launch traced here: 95.4 us
  waiting for transfers between devices  41.8 us (44%)
  starting transfers between devices  38.9 us (41%)
  Pallas kernels  7.81 us (8%)
  local copies, waits for them, and re-layouts  4.57 us (5%)
  other arithmetic  1.11 us (1%)
  matrix products  0.97 us (1%)
    ppermute x21, starting transfers between devices, moved(): return lax.ppermute(values, BOTH, pairs)  34.7 us
    ppermute x21, waiting for transfers between devices, moved(): return lax.ppermute(values, BOTH, pairs)  32.7 us
    all_to_all x1, waiting for transfers between devices, on_device(): apart = lax.all_to_all(sums, 'col', 0, 0, axis_index_groups=groups)  9.16 us
    pallas_call x3, Pallas kernels, product(): pl.pallas_call(functools.partial(product_kernel, slots, arrays, len(held)...  7.81 us
    all_to_all x1, starting transfers between devices, on_device(): apart = lax.all_to_all(sums, 'col', 0, 0, axis_index_groups=groups)  4.13 us
    unnamed x15, local copies, waits for them, and re-layouts  3.43 us
  transfers between devices with their start and end apart: 22, of which 10 were waited for; matrix products, arithmetic and copies ran while one was open for 1% of the time, Pallas kernels for 5%

profile of v2, /device:TPU:1, one launch (start us, length us, event | category | flops | bytes accessed | tf_op | source)
XLA Modules:
  0.0 95.4 jit_solution(925279343061499914)
XLA Ops:
  0.0 6.4 %collective-permute-start = (bf16[32,8192]{1,0:T(8,128)(2,1)}, bf16[32,8192]{1,0:T(8,128)(2,1)S(1)}, u32[]{:S(2)}, u32[]{:S(2)}) collective-permute-start(bf16[32,8192]{1,0:T(8,128)(2,1)} %refs_0_.1), channel_id=1, source_target_pairs={{0,16},{1,113},{16,32},{17,1},{32,48},{33,17},{48,64},{49,33},{64,... | collective-permute-start | bytes 1572872 | tf_op jit(solution)/shard_map/ppermute | solution.py:26
  6.4 1.1 %fusion.10 = (bf16[16,8192]{1,0:T(8,128)(2,1)S(1)}, bf16[16,8192]{1,0:T(8,128)(2,1)S(1)}) fusion(bf16[32,8192]{1,0:T(8,128)(2,1)} %refs_0_.1), kind=kLoop, calls=%fused_computation.26 | loop fusion | bytes 1048576 | tf_op jit(solution)/shard_map/slice | solution.py:150
  7.5 3.0 %collective-permute-start.1 = (bf16[16,8192]{1,0:T(8,128)(2,1)S(1)}, bf16[16,8192]{1,0:T(8,128)(2,1)S(1)}, u32[]{:S(2)}, u32[]{:S(2)}) collective-permute-start(bf16[16,8192]{1,0:T(8,128)(2,1)S(1)} %get-tuple-element.18), channel_id=1, source_target_pairs={{0,128},{1,129},{16,144},{17,145},{32,160},{33,161},{48,176},{49,1... | collective-permute-start | bytes 786440 | tf_op jit(solution)/shard_map/ppermute | solution.py:26
  10.5 0.2 collective-permute-start.13
  10.7 4.6 %collective-permute-done.1.refs_1_ = bf16[16,8192]{1,0:T(8,128)(2,1)S(1)} collective-permute-done((bf16[16,8192]{1,0:T(8,128)(2,1)S(1)}, bf16[16,8192]{1,0:T(8,128)(2,1)S(1)}, u32[]{:S(2)}, u32[]{:S(2)}) %collective-permute-start.1) | collective-permute-done | bytes 262176 | tf_op jit(solution)/shard_map/ppermute | solution.py:26
  15.3 2.4 %collective-permute-start.2 = (bf16[16,8192]{1,0:T(8,128)(2,1)S(1)}, bf16[16,8192]{1,0:T(8,128)(2,1)S(1)}, u32[]{:S(2)}, u32[]{:S(2)}) collective-permute-start(bf16[16,8192]{1,0:T(8,128)(2,1)S(1)} %collective-permute-done.1.refs_1_), channel_id=1, source_target_pairs={{0,16},{1,113},{16,32},{17,1},{32,48},{33,17},{48,64},{49,33},{64,... | collective-permute-start | bytes 786440 | tf_op jit(solution)/shard_map/ppermute | solution.py:26
  17.8 2.7 %collective-permute-start.9 = (bf16[16,8192]{1,0:T(8,128)(2,1)S(1)}, bf16[16,8192]{1,0:T(8,128)(2,1)S(1)}, u32[]{:S(2)}, u32[]{:S(2)}) collective-permute-start(bf16[16,8192]{1,0:T(8,128)(2,1)S(1)} %get-tuple-element.21), channel_id=1, source_target_pairs={{0,16},{1,113},{16,32},{17,1},{32,48},{33,17},{48,64},{49,33},{64,... | collective-permute-start | bytes 786440 | tf_op jit(solution)/shard_map/ppermute | solution.py:26
  20.7 1.7 %collective-permute-done.2.refs_5_ = bf16[16,8192]{1,0:T(8,128)(2,1)S(1)} collective-permute-done((bf16[16,8192]{1,0:T(8,128)(2,1)S(1)}, bf16[16,8192]{1,0:T(8,128)(2,1)S(1)}, u32[]{:S(2)}, u32[]{:S(2)}) %collective-permute-start.2) | collective-permute-done | bytes 262176 | tf_op jit(solution)/shard_map/ppermute | solution.py:26
  22.4 3.5 %collective-permute-start.14 = (bf16[32,8192]{1,0:T(8,128)(2,1)S(1)}, bf16[32,8192]{1,0:T(8,128)(2,1)S(1)}, u32[]{:S(2)}, u32[]{:S(2)}) collective-permute-start(bf16[32,8192]{1,0:T(8,128)(2,1)S(1)} %pad_maximum_fusion.2), channel_id=1, source_target_pairs={{0,128},{1,129},{16,144},{17,145},{32,160},{33,161},{48,176},{49,1... | collective-permute-start | bytes 1572872 | tf_op jit(solution)/shard_map/ppermute | solution.py:26
  25.9 1.4 %collective-permute-done.6.refs_6_ = bf16[16,8192]{1,0:T(8,128)(2,1)S(1)} collective-permute-done((bf16[16,8192]{1,0:T(8,128)(2,1)S(1)}, bf16[16,8192]{1,0:T(8,128)(2,1)S(1)}, u32[]{:S(2)}, u32[]{:S(2)}) %collective-permute-start.6) | collective-permute-done | bytes 262176 | tf_op jit(solution)/shard_map/ppermute | solution.py:26
  27.3 1.6 %collective-permute-start.3 = (bf16[32,8192]{1,0:T(8,128)(2,1)S(1)}, bf16[32,8192]{1,0:T(8,128)(2,1)S(1)}, u32[]{:S(2)}, u32[]{:S(2)}) collective-permute-start(bf16[32,8192]{1,0:T(8,128)(2,1)S(1)} %pad_maximum_fusion), channel_id=1, source_target_pairs={{0,16},{1,113},{16,32},{17,1},{32,48},{33,17},{48,64},{49,33},{64,... | collective-permute-start | bytes 1572872 | tf_op jit(solution)/shard_map/ppermute | solution.py:26
  28.9 2.5 %collective-permute-start.10 = (bf16[16,8192]{1,0:T(8,128)(2,1)S(1)}, bf16[16,8192]{1,0:T(8,128)(2,1)S(1)}, u32[]{:S(2)}, u32[]{:S(2)}) collective-permute-start(bf16[16,8192]{1,0:T(8,128)(2,1)S(1)} %collective-permute-done.9.refs_2_), channel_id=1, source_target_pairs={{0,16},{1,113},{16,32},{17,1},{32,48},{33,17},{48,64},{49,33},{64,... | collective-permute-start | bytes 786440 | tf_op jit(solution)/shard_map/ppermute | solution.py:26
  31.4 0.1 collective-permute-done.11.refs_3_
  31.6 9.6 %collective-permute-done.10.refs_2_ = bf16[16,8192]{1,0:T(8,128)(2,1)S(1)} collective-permute-done((bf16[16,8192]{1,0:T(8,128)(2,1)S(1)}, bf16[16,8192]{1,0:T(8,128)(2,1)S(1)}, u32[]{:S(2)}, u32[]{:S(2)}) %collective-permute-start.10) | collective-permute-done | bytes 262176 | tf_op jit(solution)/shard_map/ppermute | solution.py:26
  41.2 3.6 %collective-permute-start.18 = (bf16[32,8192]{1,0:T(8,128)(2,1)S(1)}, bf16[32,8192]{1,0:T(8,128)(2,1)S(1)}, u32[]{:S(2)}, u32[]{:S(2)}) collective-permute-start(bf16[32,8192]{1,0:T(8,128)(2,1)S(1)} %pad_maximum_fusion.4), channel_id=1, source_target_pairs={{0,128},{1,129},{16,144},{17,145},{32,160},{33,161},{48,176},{49,1... | collective-permute-start | bytes 1572872 | tf_op jit(solution)/shard_map/ppermute | solution.py:26
  44.8 2.1 %collective-permute-start.4 = (bf16[32,8192]{1,0:T(8,128)(2,1)S(1)}, bf16[32,8192]{1,0:T(8,128)(2,1)S(1)}, u32[]{:S(2)}, u32[]{:S(2)}) collective-permute-start(bf16[32,8192]{1,0:T(8,128)(2,1)S(1)} %collective-permute-done.3.refs_0_), channel_id=1, source_target_pairs={{0,16},{1,113},{16,32},{17,1},{32,48},{33,17},{48,64},{49,33},{64,... | collective-permute-start | bytes 1572872 | tf_op jit(solution)/shard_map/ppermute | solution.py:26
  46.9 1.2 %collective-permute-start.17 = (bf16[16,8192]{1,0:T(8,128)(2,1)S(1)}, bf16[16,8192]{1,0:T(8,128)(2,1)S(1)}, u32[]{:S(2)}, u32[]{:S(2)}) collective-permute-start(bf16[16,8192]{1,0:T(8,128)(2,1)S(1)} %collective-permute-done.10.refs_2_), channel_id=1, source_target_pairs={{0,16},{1,113},{16,32},{17,1},{32,48},{33,17},{48,64},{49,33},{64,... | collective-permute-start | bytes 786440 | tf_op jit(solution)/shard_map/ppermute | solution.py:26
  48.1 3.4 %copy-done = bf16[512,8192]{1,0:T(8,128)(2,1)S(1)} copy-done((bf16[512,8192]{1,0:T(8,128)(2,1)S(1)}, bf16[512,8192]{1,0:T(8,128)(2,1)}, u32[]{:S(2)}) %copy-start) | copy-done | bytes 8388632
  51.5 2.6 %shard_map.64 = (f32[512,192]{1,0:T(8,128)S(1)}, bf16[32,8192]{1,0:T(8,128)(2,1)S(1)}) custom-call(s32[1]{0:T(128)} %bitcast.core_ref, bf16[512,8192]{1,0:T(8,128)(2,1)S(1)} %copy-done, bf16[32,8192]{1,0:T(8,128)(2,1)S(1)} %copy-done.2, bf16[16,8192]{1,0:T(8,128)(2,1)S(1)} %collective-permute-done.1.refs_1_, ...), custom_call_target="tpu_custom_call", output_to_operand_aliasing={{1}: (10, {})} | custom-call | flops 1610612736 | bytes 11534336 | tf_op jit(solution)/shard_map/pallas_call | solution.py:117
  54.2 0.7 collective-permute-start.15
  54.8 3.8 %collective-permute-done.4.refs_0_ = bf16[32,8192]{1,0:T(8,128)(2,1)S(1)} collective-permute-done((bf16[32,8192]{1,0:T(8,128)(2,1)S(1)}, bf16[32,8192]{1,0:T(8,128)(2,1)S(1)}, u32[]{:S(2)}, u32[]{:S(2)}) %collective-permute-start.4) | collective-permute-done | bytes 524320 | tf_op jit(solution)/shard_map/ppermute | solution.py:26
  58.6 3.4 %collective-permute-start.16 = (bf16[32,8192]{1,0:T(8,128)(2,1)S(1)}, bf16[32,8192]{1,0:T(8,128)(2,1)S(1)}, u32[]{:S(2)}, u32[]{:S(2)}) collective-permute-start(bf16[32,8192]{1,0:T(8,128)(2,1)S(1)} %collective-permute-done.4.refs_0_), channel_id=1, source_target_pairs={{0,16},{1,113},{16,32},{17,1},{32,48},{33,17},{48,64},{49,33},{64,... | collective-permute-start | bytes 1572872 | tf_op jit(solution)/shard_map/ppermute | solution.py:26
  62.0 2.4 %shard_map.65 = (f32[512,320]{1,0:T(8,128)S(1)}, bf16[16,8192]{1,0:T(8,128)(2,1)S(1)}) custom-call(s32[1]{0:T(128)} %bitcast.core_ref, bf16[512,8192]{1,0:T(8,128)(2,1)S(1)} %copy-done.1, bf16[32,8192]{1,0:T(8,128)(2,1)S(1)} %collective-permute-done.3.refs_0_, bf16[32,8192]{1,0:T(8,128)(2,1)S(1)} %collective-permute-done.7.refs_1_, ...), custom_call_target="tpu_custom_call", output_to_operand_aliasing={{1}: (7, {})} | custom-call | flops 1073741824 | bytes 10485760 | tf_op jit(solution)/shard_map/pallas_call | solution.py:117
  64.5 4.0 %collective-permute-done.15.refs_4_ = bf16[32,8192]{1,0:T(8,128)(2,1)S(1)} collective-permute-done((bf16[32,8192]{1,0:T(8,128)(2,1)S(1)}, bf16[32,8192]{1,0:T(8,128)(2,1)S(1)}, u32[]{:S(2)}, u32[]{:S(2)}) %collective-permute-start.15) | collective-permute-done | bytes 524320 | tf_op jit(solution)/shard_map/ppermute | solution.py:26
  68.6 5.8 %collective-permute-done.19.refs_7_ = bf16[16,8192]{1,0:T(8,128)(2,1)S(1)} collective-permute-done((bf16[16,8192]{1,0:T(8,128)(2,1)S(1)}, bf16[16,8192]{1,0:T(8,128)(2,1)S(1)}, u32[]{:S(2)}, u32[]{:S(2)}) %collective-permute-start.19) | collective-permute-done | bytes 262176 | tf_op jit(solution)/shard_map/ppermute | solution.py:26
  74.4 2.8 %shard_map.66 = (f32[256,512]{1,0:T(8,128)S(1)}, f32[256,512]{1,0:T(8,128)S(1)}) custom-call(s32[1]{0:T(128)} %bitcast.core_ref, bf16[512,8192]{1,0:T(8,128)(2,1)S(1)} %copy-done.1, bf16[32,8192]{1,0:T(8,128)(2,1)S(1)} %collective-permute-done.4.refs_0_, bf16[32,8192]{1,0:T(8,128)(2,1)S(1)} %collective-permute-done.8.refs_1_, ...), custom_call_target="tpu_custom_call" | custom-call | flops 1610612736 | bytes 11534336 | tf_op jit(solution)/shard_map/pallas_call | solution.py:117
  77.2 1.4 %collective-permute-start.20 = (f32[256,512]{1,0:T(8,128)S(1)}, f32[256,512]{1,0:T(8,128)S(1)}, u32[]{:S(2)}, u32[]{:S(2)}) collective-permute-start(f32[256,512]{1,0:T(8,128)S(1)} %get-tuple-element.16), channel_id=1, source_target_pairs={{0,1},{1,0},{16,17},{17,16},{32,33},{33,32},{48,49},{49,48},{64,65... | collective-permute-start | bytes 1572872 | tf_op jit(solution)/shard_map/ppermute | solution.py:26
  78.6 1.5 %collective-permute-done.20 = f32[256,512]{1,0:T(8,128)S(1)} collective-permute-done((f32[256,512]{1,0:T(8,128)S(1)}, f32[256,512]{1,0:T(8,128)S(1)}, u32[]{:S(2)}, u32[]{:S(2)}) %collective-permute-start.20) | collective-permute-done | bytes 524320 | tf_op jit(solution)/shard_map/ppermute | solution.py:26
  80.1 0.9 add.40
  81.0 4.1 %all-to-all-start = ((f32[8,32,512]{2,1,0:T(8,128)}), f32[8,32,512]{2,1,0:T(8,128)S(1)}, u32[]{:S(2)}, u32[]{:S(2)}) async-start(f32[8,32,512]{2,1,0:T(8,128)} %bitcast.1), calls=%async_computation | async-start | bytes 1048576 | tf_op jit(solution)/shard_map/all_to_all | solution.py:183
  85.2 9.2 %all-to-all-done = f32[8,32,512]{2,1,0:T(8,128)S(1)} async-done(((f32[8,32,512]{2,1,0:T(8,128)}), f32[8,32,512]{2,1,0:T(8,128)S(1)}, u32[]{:S(2)}, u32[]{:S(2)}) %all-to-all-start) | async-done | bytes 524320 | tf_op jit(solution)/shard_map/all_to_all | solution.py:183
  94.4 1.0 %convolution_convert_fusion = bf16[32,512]{1,0:T(8,128)(2,1)} fusion(s32[512]{0:T(512)S(1)} %copy-done.6, s32[512]{0:T(512)S(1)} %fusion.7, bf16[32,512]{1,0:T(8,128)(2,1)S(1)} %reduce_sum.9), kind=kOutput, calls=%fused_computation | convolution fusion | flops 17055744 | bytes 69632 | tf_op jit(solution)/shard_map/dot_general | solution.py:193
  (42 shorter events, 0.6 us)
Async XLA Ops:
  0.0 48.1 %copy-start.2 = (bf16[32,8192]{1,0:T(8,128)(2,1)S(1)}, bf16[32,8192]{1,0:T(8,128)(2,1)}, u32[]{:S(2)}) copy-start(bf16[32,8192]{1,0:T(8,128)(2,1)} %refs_0_.1) | copy-start | bytes 1572868
  0.0 17.7 %collective-permute-start = (bf16[32,8192]{1,0:T(8,128)(2,1)}, bf16[32,8192]{1,0:T(8,128)(2,1)S(1)}, u32[]{:S(2)}, u32[]{:S(2)}) collective-permute-start(bf16[32,8192]{1,0:T(8,128)(2,1)} %refs_0_.1), channel_id=1, source_target_pairs={{0,16},{1,113},{16,32},{17,1},{32,48},{33,17},{48,64},{49,33},{64,... | collective-permute-start | bytes 1572872 | tf_op jit(solution)/shard_map/ppermute | solution.py:26
  7.5 7.8 %collective-permute-start.1 = (bf16[16,8192]{1,0:T(8,128)(2,1)S(1)}, bf16[16,8192]{1,0:T(8,128)(2,1)S(1)}, u32[]{:S(2)}, u32[]{:S(2)}) collective-permute-start(bf16[16,8192]{1,0:T(8,128)(2,1)S(1)} %get-tuple-element.18), channel_id=1, source_target_pairs={{0,128},{1,129},{16,144},{17,145},{32,160},{33,161},{48,176},{49,1... | collective-permute-start | bytes 786440 | tf_op jit(solution)/shard_map/ppermute | solution.py:26
  10.5 10.0 %collective-permute-start.5 = (bf16[32,8192]{1,0:T(8,128)(2,1)}, bf16[32,8192]{1,0:T(8,128)(2,1)S(1)}, u32[]{:S(2)}, u32[]{:S(2)}) collective-permute-start(bf16[32,8192]{1,0:T(8,128)(2,1)} %refs_0_.1), channel_id=1, source_target_pairs={{0,112},{1,17},{16,0},{17,33},{32,16},{33,49},{48,32},{49,65},{64,... | collective-permute-start | bytes 1572872 | tf_op jit(solution)/shard_map/ppermute | solution.py:26
  10.5 36.4 %collective-permute-start.13 = (bf16[16,8192]{1,0:T(8,128)(2,1)S(1)}, bf16[16,8192]{1,0:T(8,128)(2,1)S(1)}, u32[]{:S(2)}, u32[]{:S(2)}) collective-permute-start(bf16[16,8192]{1,0:T(8,128)(2,1)S(1)} %get-tuple-element.17), channel_id=1, source_target_pairs={{0,128},{1,129},{16,144},{17,145},{32,160},{33,161},{48,176},{49,1... | collective-permute-start | bytes 786440 | tf_op jit(solution)/shard_map/ppermute | solution.py:26
  15.3 7.1 %collective-permute-start.2 = (bf16[16,8192]{1,0:T(8,128)(2,1)S(1)}, bf16[16,8192]{1,0:T(8,128)(2,1)S(1)}, u32[]{:S(2)}, u32[]{:S(2)}) collective-permute-start(bf16[16,8192]{1,0:T(8,128)(2,1)S(1)} %collective-permute-done.1.refs_1_), channel_id=1, source_target_pairs={{0,16},{1,113},{16,32},{17,1},{32,48},{33,17},{48,64},{49,33},{64,... | collective-permute-start | bytes 786440 | tf_op jit(solution)/shard_map/ppermute | solution.py:26
  17.7 9.6 %collective-permute-start.6 = (bf16[16,8192]{1,0:T(8,128)(2,1)S(1)}, bf16[16,8192]{1,0:T(8,128)(2,1)S(1)}, u32[]{:S(2)}, u32[]{:S(2)}) collective-permute-start(bf16[16,8192]{1,0:T(8,128)(2,1)S(1)} %collective-permute-done.1.refs_1_), channel_id=1, source_target_pairs={{0,112},{1,17},{16,0},{17,33},{32,16},{33,49},{48,32},{49,65},{64,... | collective-permute-start | bytes 786440 | tf_op jit(solution)/shard_map/ppermute | solution.py:26
  17.8 11.1 %collective-permute-start.9 = (bf16[16,8192]{1,0:T(8,128)(2,1)S(1)}, bf16[16,8192]{1,0:T(8,128)(2,1)S(1)}, u32[]{:S(2)}, u32[]{:S(2)}) collective-permute-start(bf16[16,8192]{1,0:T(8,128)(2,1)S(1)} %get-tuple-element.21), channel_id=1, source_target_pairs={{0,16},{1,113},{16,32},{17,1},{32,48},{33,17},{48,64},{49,33},{64,... | collective-permute-start | bytes 786440 | tf_op jit(solution)/shard_map/ppermute | solution.py:26
  20.6 11.0 %collective-permute-start.11 = (bf16[16,8192]{1,0:T(8,128)(2,1)S(1)}, bf16[16,8192]{1,0:T(8,128)(2,1)S(1)}, u32[]{:S(2)}, u32[]{:S(2)}) collective-permute-start(bf16[16,8192]{1,0:T(8,128)(2,1)S(1)} %get-tuple-element.19), channel_id=1, source_target_pairs={{0,112},{1,17},{16,0},{17,33},{32,16},{33,49},{48,32},{49,65},{64,... | collective-permute-start | bytes 786440 | tf_op jit(solution)/shard_map/ppermute | solution.py:26
  22.4 25.7 %collective-permute-start.14 = (bf16[32,8192]{1,0:T(8,128)(2,1)S(1)}, bf16[32,8192]{1,0:T(8,128)(2,1)S(1)}, u32[]{:S(2)}, u32[]{:S(2)}) collective-permute-start(bf16[32,8192]{1,0:T(8,128)(2,1)S(1)} %pad_maximum_fusion.2), channel_id=1, source_target_pairs={{0,128},{1,129},{16,144},{17,145},{32,160},{33,161},{48,176},{49,1... | collective-permute-start | bytes 1572872 | tf_op jit(solution)/shard_map/ppermute | solution.py:26
  27.3 17.5 %collective-permute-start.3 = (bf16[32,8192]{1,0:T(8,128)(2,1)S(1)}, bf16[32,8192]{1,0:T(8,128)(2,1)S(1)}, u32[]{:S(2)}, u32[]{:S(2)}) collective-permute-start(bf16[32,8192]{1,0:T(8,128)(2,1)S(1)} %pad_maximum_fusion), channel_id=1, source_target_pairs={{0,16},{1,113},{16,32},{17,1},{32,48},{33,17},{48,64},{49,33},{64,... | collective-permute-start | bytes 1572872 | tf_op jit(solution)/shard_map/ppermute | solution.py:26
  28.9 12.3 %collective-permute-start.10 = (bf16[16,8192]{1,0:T(8,128)(2,1)S(1)}, bf16[16,8192]{1,0:T(8,128)(2,1)S(1)}, u32[]{:S(2)}, u32[]{:S(2)}) collective-permute-start(bf16[16,8192]{1,0:T(8,128)(2,1)S(1)} %collective-permute-done.9.refs_2_), channel_id=1, source_target_pairs={{0,16},{1,113},{16,32},{17,1},{32,48},{33,17},{48,64},{49,33},{64,... | collective-permute-start | bytes 786440 | tf_op jit(solution)/shard_map/ppermute | solution.py:26
  31.6 9.7 %collective-permute-start.12 = (bf16[16,8192]{1,0:T(8,128)(2,1)S(1)}, bf16[16,8192]{1,0:T(8,128)(2,1)S(1)}, u32[]{:S(2)}, u32[]{:S(2)}) collective-permute-start(bf16[16,8192]{1,0:T(8,128)(2,1)S(1)} %collective-permute-done.11.refs_3_), channel_id=1, source_target_pairs={{0,112},{1,17},{16,0},{17,33},{32,16},{33,49},{48,32},{49,65},{64,... | collective-permute-start | bytes 786440 | tf_op jit(solution)/shard_map/ppermute | solution.py:26
  41.2 13.6 %collective-permute-start.7 = (bf16[32,8192]{1,0:T(8,128)(2,1)S(1)}, bf16[32,8192]{1,0:T(8,128)(2,1)S(1)}, u32[]{:S(2)}, u32[]{:S(2)}) collective-permute-start(bf16[32,8192]{1,0:T(8,128)(2,1)S(1)} %pad_maximum_fusion.1), channel_id=1, source_target_pairs={{0,112},{1,17},{16,0},{17,33},{32,16},{33,49},{48,32},{49,65},{64,... | collective-permute-start | bytes 1572872 | tf_op jit(solution)/shard_map/ppermute | solution.py:26
  41.2 20.7 %collective-permute-start.18 = (bf16[32,8192]{1,0:T(8,128)(2,1)S(1)}, bf16[32,8192]{1,0:T(8,128)(2,1)S(1)}, u32[]{:S(2)}, u32[]{:S(2)}) collective-permute-start(bf16[32,8192]{1,0:T(8,128)(2,1)S(1)} %pad_maximum_fusion.4), channel_id=1, source_target_pairs={{0,128},{1,129},{16,144},{17,145},{32,160},{33,161},{48,176},{49,1... | collective-permute-start | bytes 1572872 | tf_op jit(solution)/shard_map/ppermute | solution.py:26
  44.8 13.8 %collective-permute-start.4 = (bf16[32,8192]{1,0:T(8,128)(2,1)S(1)}, bf16[32,8192]{1,0:T(8,128)(2,1)S(1)}, u32[]{:S(2)}, u32[]{:S(2)}) collective-permute-start(bf16[32,8192]{1,0:T(8,128)(2,1)S(1)} %collective-permute-done.3.refs_0_), channel_id=1, source_target_pairs={{0,16},{1,113},{16,32},{17,1},{32,48},{33,17},{48,64},{49,33},{64,... | collective-permute-start | bytes 1572872 | tf_op jit(solution)/shard_map/ppermute | solution.py:26
  46.9 15.0 %collective-permute-start.17 = (bf16[16,8192]{1,0:T(8,128)(2,1)S(1)}, bf16[16,8192]{1,0:T(8,128)(2,1)S(1)}, u32[]{:S(2)}, u32[]{:S(2)}) collective-permute-start(bf16[16,8192]{1,0:T(8,128)(2,1)S(1)} %collective-permute-done.10.refs_2_), channel_id=1, source_target_pairs={{0,16},{1,113},{16,32},{17,1},{32,48},{33,17},{48,64},{49,33},{64,... | collective-permute-start | bytes 786440 | tf_op jit(solution)/shard_map/ppermute | solution.py:26
  48.1 3.4 %copy-start = (bf16[512,8192]{1,0:T(8,128)(2,1)S(1)}, bf16[512,8192]{1,0:T(8,128)(2,1)}, u32[]{:S(2)}) copy-start(bf16[512,8192]{1,0:T(8,128)(2,1)} %cov_ref.5) | copy-start | bytes 25165828
  51.5 10.5 %copy-start.1 = (bf16[512,8192]{1,0:T(8,128)(2,1)S(1)}, bf16[512,8192]{1,0:T(8,128)(2,1)}, u32[]{:S(2)}) copy-start(bf16[512,8192]{1,0:T(8,128)(2,1)} %cov_ref.5) | copy-start | bytes 25165828
  54.2 14.4 %collective-permute-start.15 = (bf16[32,8192]{1,0:T(8,128)(2,1)S(1)}, bf16[32,8192]{1,0:T(8,128)(2,1)S(1)}, u32[]{:S(2)}, u32[]{:S(2)}) collective-permute-start(bf16[32,8192]{1,0:T(8,128)(2,1)S(1)} %get-tuple-element.11), channel_id=1, source_target_pairs={{0,128},{1,129},{16,144},{17,145},{32,160},{33,161},{48,176},{49,1... | collective-permute-start | bytes 1572872 | tf_op jit(solution)/shard_map/ppermute | solution.py:26
  54.8 13.8 %collective-permute-start.8 = (bf16[32,8192]{1,0:T(8,128)(2,1)S(1)}, bf16[32,8192]{1,0:T(8,128)(2,1)S(1)}, u32[]{:S(2)}, u32[]{:S(2)}) collective-permute-start(bf16[32,8192]{1,0:T(8,128)(2,1)S(1)} %collective-permute-done.7.refs_1_), channel_id=1, source_target_pairs={{0,112},{1,17},{16,0},{17,33},{32,16},{33,49},{48,32},{49,65},{64,... | collective-permute-start | bytes 1572872 | tf_op jit(solution)/shard_map/ppermute | solution.py:26
  58.6 15.8 %collective-permute-start.16 = (bf16[32,8192]{1,0:T(8,128)(2,1)S(1)}, bf16[32,8192]{1,0:T(8,128)(2,1)S(1)}, u32[]{:S(2)}, u32[]{:S(2)}) collective-permute-start(bf16[32,8192]{1,0:T(8,128)(2,1)S(1)} %collective-permute-done.4.refs_0_), channel_id=1, source_target_pairs={{0,16},{1,113},{16,32},{17,1},{32,48},{33,17},{48,64},{49,33},{64,... | collective-permute-start | bytes 1572872 | tf_op jit(solution)/shard_map/ppermute | solution.py:26
  64.4 20.7 %copy-start.3 = (s32[512]{0:T(512)S(1)}, s32[512]{0:T(512)}, u32[]{:S(2)}) copy-start(s32[512]{0:T(512)} %constant.66.clone) | copy-start | bytes 6148
  64.4 20.7 %copy-start.4 = (s32[512]{0:T(512)S(1)}, s32[512]{0:T(512)}, u32[]{:S(2)}) copy-start(s32[512]{0:T(512)} %constant.67.clone) | copy-start | bytes 6148
  64.4 20.7 %copy-start.5 = (s32[512]{0:T(512)S(1)}, s32[512]{0:T(512)}, u32[]{:S(2)}) copy-start(s32[512]{0:T(512)} %constant.68.clone) | copy-start | bytes 6148
  64.4 29.9 %copy-start.6 = (s32[512]{0:T(512)S(1)}, s32[512]{0:T(512)}, u32[]{:S(2)}) copy-start(s32[512]{0:T(512)} %param.8) | copy-start | bytes 6148
  64.4 10.0 %collective-permute-start.19 = (bf16[16,8192]{1,0:T(8,128)(2,1)S(1)}, bf16[16,8192]{1,0:T(8,128)(2,1)S(1)}, u32[]{:S(2)}, u32[]{:S(2)}) collective-permute-start(bf16[16,8192]{1,0:T(8,128)(2,1)S(1)} %get-tuple-element.13), channel_id=1, source_target_pairs={{0,128},{1,129},{16,144},{17,145},{32,160},{33,161},{48,176},{49,1... | collective-permute-start | bytes 786440 | tf_op jit(solution)/shard_map/ppermute | solution.py:26
  77.2 2.9 %collective-permute-start.20 = (f32[256,512]{1,0:T(8,128)S(1)}, f32[256,512]{1,0:T(8,128)S(1)}, u32[]{:S(2)}, u32[]{:S(2)}) collective-permute-start(f32[256,512]{1,0:T(8,128)S(1)} %get-tuple-element.16), channel_id=1, source_target_pairs={{0,1},{1,0},{16,17},{17,16},{32,33},{33,32},{48,49},{49,48},{64,65... | collective-permute-start | bytes 1572872 | tf_op jit(solution)/shard_map/ppermute | solution.py:26
  81.0 13.3 %all-to-all-start = ((f32[8,32,512]{2,1,0:T(8,128)}), f32[8,32,512]{2,1,0:T(8,128)S(1)}, u32[]{:S(2)}, u32[]{:S(2)}) async-start(f32[8,32,512]{2,1,0:T(8,128)} %bitcast.1), calls=%async_computation | async-start | bytes 1048576 | tf_op jit(solution)/shard_map/all_to_all | solution.py:183

commit v3 on v2

--- a/solution.py
+++ b/solution.py
@@ -62,10 +62,6 @@
     if unit == "Q":
         group = next(g for g in CROSSINGS if k in g)
         return ("Q", group), UNIT * group.index(k)
-    if unit in "AB" and abs(k) < 2:
-        return ("S", k), UNIT * (unit == "B")
-    if unit in "AP" and abs(k) > 1:
-        return ("AP", k), UNIT * (unit == "P")
     return (unit, k), 0
 
 
@@ -123,7 +119,7 @@
         + [jax.ShapeDtypeStruct(h.shape, h.dtype) for h in held],
         input_output_aliases={2 + len(arrays) + n: outs + n for n in range(len(held))},
         scratch_shapes=[pltpu.VMEM((height, width), jnp.float32)],
-        compiler_params=pltpu.CompilerParams(vmem_limit_bytes=6 * 1024 * 1024),
+        compiler_params=pltpu.CompilerParams(vmem_limit_bytes=24 * 1024 * 1024),
         cost_estimate=pl.CostEstimate(
             flops=2 * height * width * depth,
             bytes_accessed=2 * depth * (height + width),
@@ -135,6 +131,17 @@
     )
 
 
+def after(resident, values):
+    return pl.pallas_call(
+        lambda resident_ref, values_ref, out_ref: None,
+        in_specs=[pl.BlockSpec(memory_space=pltpu.VMEM), pl.BlockSpec(memory_space=pl.ANY)],
+        out_specs=pl.BlockSpec(memory_space=pl.ANY),
+        out_shape=jax.ShapeDtypeStruct(values.shape, values.dtype),
+        input_output_aliases={1: 0},
+        compiler_params=pltpu.CompilerParams(vmem_limit_bytes=24 * 1024 * 1024),
+    )(resident, values)
+
+
 def on_device(covariance, operator_rows, row_index):
     row, col = lax.axis_index("row"), lax.axis_index("col")
     core_of = jnp.full((1,), col % 2, jnp.int32)
@@ -156,25 +163,26 @@
         got["Q", CROSSINGS[n]] = moved(rows, across)
 
     split(0)
-    send("S", 0)
     got["P", 0] = moved(got["A", 0], across)
-    send_across(0, rows_across(0))
+    send("B", 0)
+    send("A", 0)
+    send_across(0, after(resident, rows_across(0)))
+    send("B", 1)
     send("P", 0)
-    split(1)
-    send("B", 1)
     send_across(1, rows_across(1))
-    for s in (1, -1):
-        got["AP", s] = jnp.concatenate([got["A", s], got["P", s]], 0)
-    send("AP", 1)
+    send("A", 1)
     send("B", 2)
+    send("P", 1)
     send_across(2, rows_across(2))
-    send("AP", 2)
+    some, got["A", 2], got["A", -2] = product(core_of, resident, 0, got, [got["A", 2], got["A", -2]])
+    send("A", 2)
     send("B", 3)
-    some, rows = product(core_of, resident, 0, got, [rows_across(3)])
-    send_across(3, rows)
-    most, rows = product(core_of, resident, 1, got, [rows_across(4)], some)
-    send_across(4, rows)
-    send("AP", 3)
+    send("P", 2)
+    send_across(3, rows_across(3))
+    send_across(4, rows_across(4))
+    most, got["A", 3] = product(core_of, resident, 1, got, [got["A", 3]], some)
+    send("A", 3)
+    send("P", 3)
     keep, sent = product(core_of, resident, 2, got, [], most)
 
     came = moved(sent, other_core)

time: 95.7 us -> 95.2 us (level)
  starting transfers between devices: 38.9 us -> 45.3 us
  waiting for transfers between devices: 41.8 us -> 35.4 us
    ppermute x21 -> x28, waiting for transfers between devices: 32.7 us -> 26.2 us  [moved(): return lax.ppermute(values, BOTH, pairs)]
    ppermute x21 -> x28, starting transfers between devices: 34.7 us -> 41 us  [moved(): return lax.ppermute(values, BOTH, pairs)]
    unnamed x15 -> x11, local copies, waits for them, and re-layouts: 3.43 us -> 3.42 us
  transfers between devices with their start and end apart: 22 -> 29, of which waited for: 10 -> 13; matrix products, arithmetic and copies ran while one was open for 1% -> 0% of each run, Pallas kernels for 5% -> 5%
where the time goes in v3:
time: 95.2 us; the launch traced here: 95 us
  starting transfers between devices  45.3 us (48%)
  waiting for transfers between devices  35.4 us (37%)
  Pallas kernels  7.72 us (8%)
  local copies, waits for them, and re-layouts  4.48 us (5%)
  other arithmetic  1.03 us (1%)
  matrix products  0.97 us (1%)
    ppermute x28, starting transfers between devices, moved(): return lax.ppermute(values, BOTH, pairs)  41 us
    ppermute x28, waiting for transfers between devices, moved(): return lax.ppermute(values, BOTH, pairs)  26.2 us
    all_to_all x1, waiting for transfers between devices, on_device(): apart = lax.all_to_all(sums, 'col', 0, 0, axis_index_groups=groups)  9.16 us
    pallas_call x3, Pallas kernels, product(): pl.pallas_call(functools.partial(product_kernel, slots, arrays, len(held)...  7.72 us
    all_to_all x1, starting transfers between devices, on_device(): apart = lax.all_to_all(sums, 'col', 0, 0, axis_index_groups=groups)  4.27 us
    unnamed x11, local copies, waits for them, and re-layouts  3.42 us
  transfers between devices with their start and end apart: 29, of which 13 were waited for; matrix products, arithmetic and copies ran while one was open for 0% of the time, Pallas kernels for 5%

profile of v3, /device:TPU:1, one launch (start us, length us, event | category | flops | bytes accessed | tf_op | source)
XLA Modules:
  0.0 95.0 jit_solution(2662501703416105850)
XLA Ops:
  1.1 6.5 %collective-permute-start.4 = (bf16[16,8192]{1,0:T(8,128)(2,1)S(1)}, bf16[16,8192]{1,0:T(8,128)(2,1)S(1)}, u32[]{:S(2)}, u32[]{:S(2)}) collective-permute-start(bf16[16,8192]{1,0:T(8,128)(2,1)S(1)} %get-tuple-element.19.refs_1_), channel_id=1, source_target_pairs={{0,16},{1,113},{16,32},{17,1},{32,48},{33,17},{48,64},{49,33},{64,... | collective-permute-start | bytes 786440 | tf_op jit(solution)/shard_map/ppermute | solution.py:26
  7.5 2.9 %collective-permute-start = (bf16[16,8192]{1,0:T(8,128)(2,1)S(1)}, bf16[16,8192]{1,0:T(8,128)(2,1)S(1)}, u32[]{:S(2)}, u32[]{:S(2)}) collective-permute-start(bf16[16,8192]{1,0:T(8,128)(2,1)S(1)} %get-tuple-element.20.refs_0_), channel_id=1, source_target_pairs={{0,128},{1,129},{16,144},{17,145},{32,160},{33,161},{48,176},{49,1... | collective-permute-start | bytes 786440 | tf_op jit(solution)/shard_map/ppermute | solution.py:26
  10.5 2.7 %collective-permute-start.2 = (bf16[16,8192]{1,0:T(8,128)(2,1)S(1)}, bf16[16,8192]{1,0:T(8,128)(2,1)S(1)}, u32[]{:S(2)}, u32[]{:S(2)}) collective-permute-start(bf16[16,8192]{1,0:T(8,128)(2,1)S(1)} %get-tuple-element.20.refs_0_), channel_id=1, source_target_pairs={{0,16},{1,113},{16,32},{17,1},{32,48},{33,17},{48,64},{49,33},{64,... | collective-permute-start | bytes 786440 | tf_op jit(solution)/shard_map/ppermute | solution.py:26
  13.2 3.4 %copy-done = bf16[512,8192]{1,0:T(8,128)(2,1)S(1)} copy-done((bf16[512,8192]{1,0:T(8,128)(2,1)S(1)}, bf16[512,8192]{1,0:T(8,128)(2,1)}, u32[]{:S(2)}) %copy-start) | copy-done | bytes 8388632
  16.7 1.7 %collective-permute-start.6 = (bf16[16,8192]{1,0:T(8,128)(2,1)S(1)}, bf16[16,8192]{1,0:T(8,128)(2,1)S(1)}, u32[]{:S(2)}, u32[]{:S(2)}) collective-permute-start(bf16[16,8192]{1,0:T(8,128)(2,1)S(1)} %collective-permute-done.refs_2_), channel_id=1, source_target_pairs={{0,16},{1,113},{16,32},{17,1},{32,48},{33,17},{48,64},{49,33},{64,... | collective-permute-start | bytes 786440 | tf_op jit(solution)/shard_map/ppermute | solution.py:26
  18.4 3.5 %collective-permute-done.3.refs_5_ = bf16[16,8192]{1,0:T(8,128)(2,1)S(1)} collective-permute-done((bf16[16,8192]{1,0:T(8,128)(2,1)S(1)}, bf16[16,8192]{1,0:T(8,128)(2,1)S(1)}, u32[]{:S(2)}, u32[]{:S(2)}) %collective-permute-start.3) | collective-permute-done | bytes 262176 | tf_op jit(solution)/shard_map/ppermute | solution.py:26
  22.0 1.3 %collective-permute-start.12 = (bf16[16,8192]{1,0:T(8,128)(2,1)S(1)}, bf16[16,8192]{1,0:T(8,128)(2,1)S(1)}, u32[]{:S(2)}, u32[]{:S(2)}) collective-permute-start(bf16[16,8192]{1,0:T(8,128)(2,1)S(1)} %collective-permute-done.5.refs_7_), channel_id=1, source_target_pairs={{0,112},{1,17},{16,0},{17,33},{32,16},{33,49},{48,32},{49,65},{64,... | collective-permute-start | bytes 786440 | tf_op jit(solution)/shard_map/ppermute | solution.py:26
  23.3 2.0 %collective-permute-done.1.refs_3_ = bf16[16,8192]{1,0:T(8,128)(2,1)S(1)} collective-permute-done((bf16[16,8192]{1,0:T(8,128)(2,1)S(1)}, bf16[16,8192]{1,0:T(8,128)(2,1)S(1)}, u32[]{:S(2)}, u32[]{:S(2)}) %collective-permute-start.1) | collective-permute-done | bytes 262176 | tf_op jit(solution)/shard_map/ppermute | solution.py:26
  25.4 2.6 %collective-permute-done.7.refs_9_ = bf16[16,8192]{1,0:T(8,128)(2,1)S(1)} collective-permute-done((bf16[16,8192]{1,0:T(8,128)(2,1)S(1)}, bf16[16,8192]{1,0:T(8,128)(2,1)S(1)}, u32[]{:S(2)}, u32[]{:S(2)}) %collective-permute-start.7) | collective-permute-done | bytes 262176 | tf_op jit(solution)/shard_map/ppermute | solution.py:26
  28.4 2.2 %collective-permute-done.11.refs_2_ = bf16[16,8192]{1,0:T(8,128)(2,1)S(1)} collective-permute-done((bf16[16,8192]{1,0:T(8,128)(2,1)S(1)}, bf16[16,8192]{1,0:T(8,128)(2,1)S(1)}, u32[]{:S(2)}, u32[]{:S(2)}) %collective-permute-start.11) | collective-permute-done | bytes 262176 | tf_op jit(solution)/shard_map/ppermute | solution.py:26
  30.6 3.4 %collective-permute-start.18 = (bf16[16,8192]{1,0:T(8,128)(2,1)S(1)}, bf16[16,8192]{1,0:T(8,128)(2,1)S(1)}, u32[]{:S(2)}, u32[]{:S(2)}) collective-permute-start(bf16[16,8192]{1,0:T(8,128)(2,1)S(1)} %collective-permute-done.11.refs_2_), channel_id=1, source_target_pairs={{0,16},{1,113},{16,32},{17,1},{32,48},{33,17},{48,64},{49,33},{64,... | collective-permute-start | bytes 786440 | tf_op jit(solution)/shard_map/ppermute | solution.py:26
  34.0 5.2 %collective-permute-done.10.refs_12_ = bf16[16,8192]{1,0:T(8,128)(2,1)S(1)} collective-permute-done((bf16[16,8192]{1,0:T(8,128)(2,1)S(1)}, bf16[16,8192]{1,0:T(8,128)(2,1)S(1)}, u32[]{:S(2)}, u32[]{:S(2)}) %collective-permute-start.10) | collective-permute-done | bytes 262176 | tf_op jit(solution)/shard_map/ppermute | solution.py:26
  39.2 1.3 %collective-permute-start.15 = (bf16[32,8192]{1,0:T(8,128)(2,1)S(1)}, bf16[32,8192]{1,0:T(8,128)(2,1)S(1)}, u32[]{:S(2)}, u32[]{:S(2)}) collective-permute-start(bf16[32,8192]{1,0:T(8,128)(2,1)S(1)} %pad_maximum_fusion.1), channel_id=1, source_target_pairs={{0,128},{1,129},{16,144},{17,145},{32,160},{33,161},{48,176},{49,1... | collective-permute-start | bytes 1572872 | tf_op jit(solution)/shard_map/ppermute | solution.py:26
  40.6 1.3 %collective-permute-start.14 = (bf16[16,8192]{1,0:T(8,128)(2,1)S(1)}, bf16[16,8192]{1,0:T(8,128)(2,1)S(1)}, u32[]{:S(2)}, u32[]{:S(2)}) collective-permute-start(bf16[16,8192]{1,0:T(8,128)(2,1)S(1)} %collective-permute-done.7.refs_9_), channel_id=1, source_target_pairs={{0,112},{1,17},{16,0},{17,33},{32,16},{33,49},{48,32},{49,65},{64,... | collective-permute-start | bytes 786440 | tf_op jit(solution)/shard_map/ppermute | solution.py:26
  42.0 2.6 %shard_map.65 = (f32[512,192]{1,0:T(8,128)S(1)}, bf16[16,8192]{1,0:T(8,128)(2,1)S(1)}, bf16[16,8192]{1,0:T(8,128)(2,1)S(1)}) custom-call(s32[1]{0:T(128)} %bitcast.core_ref, bf16[512,8192]{1,0:T(8,128)(2,1)S(1)} %copy-done, bf16[16,8192]{1,0:T(8,128)(2,1)S(1)} %get-tuple-element.20.refs_0_, ...), custom_call_target="tpu_custom_call", output_to_operand_aliasing={{1}: (13, {}), {2}: (14, {})} | custom-call | flops 1610612736 | bytes 11534336 | tf_op jit(solution)/shard_map/pallas_call | solution.py:113
  44.6 1.4 %collective-permute-start.16 = (bf16[16,8192]{1,0:T(8,128)(2,1)S(1)}, bf16[16,8192]{1,0:T(8,128)(2,1)S(1)}, u32[]{:S(2)}, u32[]{:S(2)}) collective-permute-start(bf16[16,8192]{1,0:T(8,128)(2,1)S(1)} %get-tuple-element.12.refs_0_), channel_id=1, source_target_pairs={{0,16},{1,113},{16,32},{17,1},{32,48},{33,17},{48,64},{49,33},{64,... | collective-permute-start | bytes 786440 | tf_op jit(solution)/shard_map/ppermute | solution.py:26
  46.2 1.7 %collective-permute-start.22 = (bf16[32,8192]{1,0:T(8,128)(2,1)S(1)}, bf16[32,8192]{1,0:T(8,128)(2,1)S(1)}, u32[]{:S(2)}, u32[]{:S(2)}) collective-permute-start(bf16[32,8192]{1,0:T(8,128)(2,1)S(1)} %pad_maximum_fusion.2), channel_id=1, source_target_pairs={{0,128},{1,129},{16,144},{17,145},{32,160},{33,161},{48,176},{49,1... | collective-permute-start | bytes 1572872 | tf_op jit(solution)/shard_map/ppermute | solution.py:26
  47.9 1.7 %collective-permute-done.14.refs_5_ = bf16[16,8192]{1,0:T(8,128)(2,1)S(1)} collective-permute-done((bf16[16,8192]{1,0:T(8,128)(2,1)S(1)}, bf16[16,8192]{1,0:T(8,128)(2,1)S(1)}, u32[]{:S(2)}, u32[]{:S(2)}) %collective-permute-start.14) | collective-permute-done | bytes 262176 | tf_op jit(solution)/shard_map/ppermute | solution.py:26
  49.6 1.1 %collective-permute-start.24 = (bf16[16,8192]{1,0:T(8,128)(2,1)S(1)}, bf16[16,8192]{1,0:T(8,128)(2,1)S(1)}, u32[]{:S(2)}, u32[]{:S(2)}) collective-permute-start(bf16[16,8192]{1,0:T(8,128)(2,1)S(1)} %collective-permute-done.18.refs_2_), channel_id=1, source_target_pairs={{0,16},{1,113},{16,32},{17,1},{32,48},{33,17},{48,64},{49,33},{64,... | collective-permute-start | bytes 786440 | tf_op jit(solution)/shard_map/ppermute | solution.py:26
  50.7 1.9 %collective-permute-done.16.refs_7_ = bf16[16,8192]{1,0:T(8,128)(2,1)S(1)} collective-permute-done((bf16[16,8192]{1,0:T(8,128)(2,1)S(1)}, bf16[16,8192]{1,0:T(8,128)(2,1)S(1)}, u32[]{:S(2)}, u32[]{:S(2)}) %collective-permute-start.16) | collective-permute-done | bytes 262176 | tf_op jit(solution)/shard_map/ppermute | solution.py:26
  52.6 2.3 %collective-permute-start.20 = (bf16[16,8192]{1,0:T(8,128)(2,1)S(1)}, bf16[16,8192]{1,0:T(8,128)(2,1)S(1)}, u32[]{:S(2)}, u32[]{:S(2)}) collective-permute-start(bf16[16,8192]{1,0:T(8,128)(2,1)S(1)} %collective-permute-done.13.refs_4_), channel_id=1, source_target_pairs={{0,16},{1,113},{16,32},{17,1},{32,48},{33,17},{48,64},{49,33},{64,... | collective-permute-start | bytes 786440 | tf_op jit(solution)/shard_map/ppermute | solution.py:26
  54.9 2.4 %shard_map.66 = (f32[512,320]{1,0:T(8,128)S(1)}, bf16[16,8192]{1,0:T(8,128)(2,1)S(1)}) custom-call(s32[1]{0:T(128)} %bitcast.core_ref, bf16[512,8192]{1,0:T(8,128)(2,1)S(1)} %copy-done, bf16[16,8192]{1,0:T(8,128)(2,1)S(1)} %get-tuple-element.12.refs_0_, bf16[16,8192]{1,0:T(8,128)(2,1)S(1)} %get-tuple-element.13.refs_1_, ...), custom_call_target="tpu_custom_call", output_to_operand_aliasing={{1}: (9, {})} | custom-call | flops 1073741824 | bytes 10485760 | tf_op jit(solution)/shard_map/pallas_call | solution.py:113
  57.4 2.7 %collective-permute-start.23 = (bf16[16,8192]{1,0:T(8,128)(2,1)S(1)}, bf16[16,8192]{1,0:T(8,128)(2,1)S(1)}, u32[]{:S(2)}, u32[]{:S(2)}) collective-permute-start(bf16[16,8192]{1,0:T(8,128)(2,1)S(1)} %get-tuple-element.15.refs_0_), channel_id=1, source_target_pairs={{0,16},{1,113},{16,32},{17,1},{32,48},{33,17},{48,64},{49,33},{64,... | collective-permute-start | bytes 786440 | tf_op jit(solution)/shard_map/ppermute | solution.py:26
  60.1 1.4 %collective-permute-start.26 = (bf16[16,8192]{1,0:T(8,128)(2,1)S(1)}, bf16[16,8192]{1,0:T(8,128)(2,1)S(1)}, u32[]{:S(2)}, u32[]{:S(2)}) collective-permute-start(bf16[16,8192]{1,0:T(8,128)(2,1)S(1)} %collective-permute-done.24.refs_8_), channel_id=1, source_target_pairs={{0,128},{1,129},{16,144},{17,145},{32,160},{33,161},{48,176},{49,1... | collective-permute-start | bytes 786440 | tf_op jit(solution)/shard_map/ppermute | solution.py:26
  61.6 2.1 %collective-permute-start.25 = (bf16[16,8192]{1,0:T(8,128)(2,1)S(1)}, bf16[16,8192]{1,0:T(8,128)(2,1)S(1)}, u32[]{:S(2)}, u32[]{:S(2)}) collective-permute-start(bf16[16,8192]{1,0:T(8,128)(2,1)S(1)} %collective-permute-done.20.refs_4_), channel_id=1, source_target_pairs={{0,16},{1,113},{16,32},{17,1},{32,48},{33,17},{48,64},{49,33},{64,... | collective-permute-start | bytes 786440 | tf_op jit(solution)/shard_map/ppermute | solution.py:26
  64.2 2.2 %collective-permute-done.23.refs_7_ = bf16[16,8192]{1,0:T(8,128)(2,1)S(1)} collective-permute-done((bf16[16,8192]{1,0:T(8,128)(2,1)S(1)}, bf16[16,8192]{1,0:T(8,128)(2,1)S(1)}, u32[]{:S(2)}, u32[]{:S(2)}) %collective-permute-start.23) | collective-permute-done | bytes 262176 | tf_op jit(solution)/shard_map/ppermute | solution.py:26
  66.4 2.0 %collective-permute-done.26.refs_10_ = bf16[16,8192]{1,0:T(8,128)(2,1)S(1)} collective-permute-done((bf16[16,8192]{1,0:T(8,128)(2,1)S(1)}, bf16[16,8192]{1,0:T(8,128)(2,1)S(1)}, u32[]{:S(2)}, u32[]{:S(2)}) %collective-permute-start.26) | collective-permute-done | bytes 262176 | tf_op jit(solution)/shard_map/ppermute | solution.py:26
  69.2 2.8 %shard_map.67 = (f32[256,512]{1,0:T(8,128)S(1)}, f32[256,512]{1,0:T(8,128)S(1)}) custom-call(s32[1]{0:T(128)} %bitcast.core_ref, bf16[512,8192]{1,0:T(8,128)(2,1)S(1)} %copy-done, bf16[16,8192]{1,0:T(8,128)(2,1)S(1)} %get-tuple-element.15.refs_0_, bf16[16,8192]{1,0:T(8,128)(2,1)S(1)} %collective-permute-done.17.refs_1_, ...), custom_call_target="tpu_custom_call" | custom-call | flops 1610612736 | bytes 11534336 | tf_op jit(solution)/shard_map/pallas_call | solution.py:113
  72.0 6.1 %collective-permute-start.27 = (f32[256,512]{1,0:T(8,128)S(1)}, f32[256,512]{1,0:T(8,128)S(1)}, u32[]{:S(2)}, u32[]{:S(2)}) collective-permute-start(f32[256,512]{1,0:T(8,128)S(1)} %get-tuple-element.18), channel_id=1, source_target_pairs={{0,1},{1,0},{16,17},{17,16},{32,33},{33,32},{48,49},{49,48},{64,65... | collective-permute-start | bytes 1572872 | tf_op jit(solution)/shard_map/ppermute | solution.py:26
  78.1 1.5 %collective-permute-done.27 = f32[256,512]{1,0:T(8,128)S(1)} collective-permute-done((f32[256,512]{1,0:T(8,128)S(1)}, f32[256,512]{1,0:T(8,128)S(1)}, u32[]{:S(2)}, u32[]{:S(2)}) %collective-permute-start.27) | collective-permute-done | bytes 524320 | tf_op jit(solution)/shard_map/ppermute | solution.py:26
  80.5 4.3 %all-to-all-start = ((f32[8,32,512]{2,1,0:T(8,128)}), f32[8,32,512]{2,1,0:T(8,128)S(1)}, u32[]{:S(2)}, u32[]{:S(2)}) async-start(f32[8,32,512]{2,1,0:T(8,128)} %bitcast.1), calls=%async_computation | async-start | bytes 1048576 | tf_op jit(solution)/shard_map/all_to_all | solution.py:191
  84.8 9.2 %all-to-all-done = f32[8,32,512]{2,1,0:T(8,128)S(1)} async-done(((f32[8,32,512]{2,1,0:T(8,128)}), f32[8,32,512]{2,1,0:T(8,128)S(1)}, u32[]{:S(2)}, u32[]{:S(2)}) %all-to-all-start) | async-done | bytes 524320 | tf_op jit(solution)/shard_map/all_to_all | solution.py:191
  (49 shorter events, 5.5 us)
Async XLA Ops:
  1.1 15.5 %collective-permute-start.4 = (bf16[16,8192]{1,0:T(8,128)(2,1)S(1)}, bf16[16,8192]{1,0:T(8,128)(2,1)S(1)}, u32[]{:S(2)}, u32[]{:S(2)}) collective-permute-start(bf16[16,8192]{1,0:T(8,128)(2,1)S(1)} %get-tuple-element.19.refs_1_), channel_id=1, source_target_pairs={{0,16},{1,113},{16,32},{17,1},{32,48},{33,17},{48,64},{49,33},{64,... | collective-permute-start | bytes 786440 | tf_op jit(solution)/shard_map/ppermute | solution.py:26
  7.5 9.1 %collective-permute-start = (bf16[16,8192]{1,0:T(8,128)(2,1)S(1)}, bf16[16,8192]{1,0:T(8,128)(2,1)S(1)}, u32[]{:S(2)}, u32[]{:S(2)}) collective-permute-start(bf16[16,8192]{1,0:T(8,128)(2,1)S(1)} %get-tuple-element.20.refs_0_), channel_id=1, source_target_pairs={{0,128},{1,129},{16,144},{17,145},{32,160},{33,161},{48,176},{49,1... | collective-permute-start | bytes 786440 | tf_op jit(solution)/shard_map/ppermute | solution.py:26
  10.5 7.9 %collective-permute-start.5 = (bf16[16,8192]{1,0:T(8,128)(2,1)S(1)}, bf16[16,8192]{1,0:T(8,128)(2,1)S(1)}, u32[]{:S(2)}, u32[]{:S(2)}) collective-permute-start(bf16[16,8192]{1,0:T(8,128)(2,1)S(1)} %get-tuple-element.19.refs_1_), channel_id=1, source_target_pairs={{0,112},{1,17},{16,0},{17,33},{32,16},{33,49},{48,32},{49,65},{64,... | collective-permute-start | bytes 786440 | tf_op jit(solution)/shard_map/ppermute | solution.py:26
  10.5 11.4 %collective-permute-start.3 = (bf16[16,8192]{1,0:T(8,128)(2,1)S(1)}, bf16[16,8192]{1,0:T(8,128)(2,1)S(1)}, u32[]{:S(2)}, u32[]{:S(2)}) collective-permute-start(bf16[16,8192]{1,0:T(8,128)(2,1)S(1)} %get-tuple-element.20.refs_0_), channel_id=1, source_target_pairs={{0,112},{1,17},{16,0},{17,33},{32,16},{33,49},{48,32},{49,65},{64,... | collective-permute-start | bytes 786440 | tf_op jit(solution)/shard_map/ppermute | solution.py:26
  10.5 11.5 %collective-permute-start.2 = (bf16[16,8192]{1,0:T(8,128)(2,1)S(1)}, bf16[16,8192]{1,0:T(8,128)(2,1)S(1)}, u32[]{:S(2)}, u32[]{:S(2)}) collective-permute-start(bf16[16,8192]{1,0:T(8,128)(2,1)S(1)} %get-tuple-element.20.refs_0_), channel_id=1, source_target_pairs={{0,16},{1,113},{16,32},{17,1},{32,48},{33,17},{48,64},{49,33},{64,... | collective-permute-start | bytes 786440 | tf_op jit(solution)/shard_map/ppermute | solution.py:26
  16.6 8.7 %collective-permute-start.1 = (bf16[16,8192]{1,0:T(8,128)(2,1)S(1)}, bf16[16,8192]{1,0:T(8,128)(2,1)S(1)}, u32[]{:S(2)}, u32[]{:S(2)}) collective-permute-start(bf16[16,8192]{1,0:T(8,128)(2,1)S(1)} %shard_map.64), channel_id=1, source_target_pairs={{0,128},{1,129},{16,144},{17,145},{32,160},{33,161},{48,176},{49,1... | collective-permute-start | bytes 786440 | tf_op jit(solution)/shard_map/ppermute | solution.py:26
  16.7 8.7 %collective-permute-start.6 = (bf16[16,8192]{1,0:T(8,128)(2,1)S(1)}, bf16[16,8192]{1,0:T(8,128)(2,1)S(1)}, u32[]{:S(2)}, u32[]{:S(2)}) collective-permute-start(bf16[16,8192]{1,0:T(8,128)(2,1)S(1)} %collective-permute-done.refs_2_), channel_id=1, source_target_pairs={{0,16},{1,113},{16,32},{17,1},{32,48},{33,17},{48,64},{49,33},{64,... | collective-permute-start | bytes 786440 | tf_op jit(solution)/shard_map/ppermute | solution.py:26
  18.4 9.6 %collective-permute-start.7 = (bf16[16,8192]{1,0:T(8,128)(2,1)S(1)}, bf16[16,8192]{1,0:T(8,128)(2,1)S(1)}, u32[]{:S(2)}, u32[]{:S(2)}) collective-permute-start(bf16[16,8192]{1,0:T(8,128)(2,1)S(1)} %collective-permute-done.refs_2_), channel_id=1, source_target_pairs={{0,112},{1,17},{16,0},{17,33},{32,16},{33,49},{48,32},{49,65},{64,... | collective-permute-start | bytes 786440 | tf_op jit(solution)/shard_map/ppermute | solution.py:26
  21.8 8.7 %collective-permute-start.11 = (bf16[16,8192]{1,0:T(8,128)(2,1)S(1)}, bf16[16,8192]{1,0:T(8,128)(2,1)S(1)}, u32[]{:S(2)}, u32[]{:S(2)}) collective-permute-start(bf16[16,8192]{1,0:T(8,128)(2,1)S(1)} %collective-permute-done.4.refs_6_), channel_id=1, source_target_pairs={{0,16},{1,113},{16,32},{17,1},{32,48},{33,17},{48,64},{49,33},{64,... | collective-permute-start | bytes 786440 | tf_op jit(solution)/shard_map/ppermute | solution.py:26
  22.0 12.0 %collective-permute-start.12 = (bf16[16,8192]{1,0:T(8,128)(2,1)S(1)}, bf16[16,8192]{1,0:T(8,128)(2,1)S(1)}, u32[]{:S(2)}, u32[]{:S(2)}) collective-permute-start(bf16[16,8192]{1,0:T(8,128)(2,1)S(1)} %collective-permute-done.5.refs_7_), channel_id=1, source_target_pairs={{0,112},{1,17},{16,0},{17,33},{32,16},{33,49},{48,32},{49,65},{64,... | collective-permute-start | bytes 786440 | tf_op jit(solution)/shard_map/ppermute | solution.py:26
  25.3 15.3 %collective-permute-start.8 = (bf16[32,8192]{1,0:T(8,128)(2,1)S(1)}, bf16[32,8192]{1,0:T(8,128)(2,1)S(1)}, u32[]{:S(2)}, u32[]{:S(2)}) collective-permute-start(bf16[32,8192]{1,0:T(8,128)(2,1)S(1)} %pad_maximum_fusion), channel_id=1, source_target_pairs={{0,128},{1,129},{16,144},{17,145},{32,160},{33,161},{48,176},{49,1... | collective-permute-start | bytes 1572872 | tf_op jit(solution)/shard_map/ppermute | solution.py:26
  25.4 13.8 %collective-permute-start.10 = (bf16[16,8192]{1,0:T(8,128)(2,1)S(1)}, bf16[16,8192]{1,0:T(8,128)(2,1)S(1)}, u32[]{:S(2)}, u32[]{:S(2)}) collective-permute-start(bf16[16,8192]{1,0:T(8,128)(2,1)S(1)} %collective-permute-done.3.refs_5_), channel_id=1, source_target_pairs={{0,112},{1,17},{16,0},{17,33},{32,16},{33,49},{48,32},{49,65},{64,... | collective-permute-start | bytes 786440 | tf_op jit(solution)/shard_map/ppermute | solution.py:26
  28.0 12.6 %collective-permute-start.9 = (bf16[16,8192]{1,0:T(8,128)(2,1)S(1)}, bf16[16,8192]{1,0:T(8,128)(2,1)S(1)}, u32[]{:S(2)}, u32[]{:S(2)}) collective-permute-start(bf16[16,8192]{1,0:T(8,128)(2,1)S(1)} %collective-permute-done.2.refs_4_), channel_id=1, source_target_pairs={{0,16},{1,113},{16,32},{17,1},{32,48},{33,17},{48,64},{49,33},{64,... | collective-permute-start | bytes 786440 | tf_op jit(solution)/shard_map/ppermute | solution.py:26
  30.6 14.0 %collective-permute-start.18 = (bf16[16,8192]{1,0:T(8,128)(2,1)S(1)}, bf16[16,8192]{1,0:T(8,128)(2,1)S(1)}, u32[]{:S(2)}, u32[]{:S(2)}) collective-permute-start(bf16[16,8192]{1,0:T(8,128)(2,1)S(1)} %collective-permute-done.11.refs_2_), channel_id=1, source_target_pairs={{0,16},{1,113},{16,32},{17,1},{32,48},{33,17},{48,64},{49,33},{64,... | collective-permute-start | bytes 786440 | tf_op jit(solution)/shard_map/ppermute | solution.py:26
  34.0 12.0 %collective-permute-start.19 = (bf16[16,8192]{1,0:T(8,128)(2,1)S(1)}, bf16[16,8192]{1,0:T(8,128)(2,1)S(1)}, u32[]{:S(2)}, u32[]{:S(2)}) collective-permute-start(bf16[16,8192]{1,0:T(8,128)(2,1)S(1)} %collective-permute-done.12.refs_3_), channel_id=1, source_target_pairs={{0,112},{1,17},{16,0},{17,33},{32,16},{33,49},{48,32},{49,65},{64,... | collective-permute-start | bytes 786440 | tf_op jit(solution)/shard_map/ppermute | solution.py:26
  39.2 15.7 %collective-permute-start.15 = (bf16[32,8192]{1,0:T(8,128)(2,1)S(1)}, bf16[32,8192]{1,0:T(8,128)(2,1)S(1)}, u32[]{:S(2)}, u32[]{:S(2)}) collective-permute-start(bf16[32,8192]{1,0:T(8,128)(2,1)S(1)} %pad_maximum_fusion.1), channel_id=1, source_target_pairs={{0,128},{1,129},{16,144},{17,145},{32,160},{33,161},{48,176},{49,1... | collective-permute-start | bytes 1572872 | tf_op jit(solution)/shard_map/ppermute | solution.py:26
  40.5 5.7 %collective-permute-start.13 = (bf16[16,8192]{1,0:T(8,128)(2,1)S(1)}, bf16[16,8192]{1,0:T(8,128)(2,1)S(1)}, u32[]{:S(2)}, u32[]{:S(2)}) collective-permute-start(bf16[16,8192]{1,0:T(8,128)(2,1)S(1)} %collective-permute-done.6.refs_8_), channel_id=1, source_target_pairs={{0,16},{1,113},{16,32},{17,1},{32,48},{33,17},{48,64},{49,33},{64,... | collective-permute-start | bytes 786440 | tf_op jit(solution)/shard_map/ppermute | solution.py:26
  40.6 9.0 %collective-permute-start.14 = (bf16[16,8192]{1,0:T(8,128)(2,1)S(1)}, bf16[16,8192]{1,0:T(8,128)(2,1)S(1)}, u32[]{:S(2)}, u32[]{:S(2)}) collective-permute-start(bf16[16,8192]{1,0:T(8,128)(2,1)S(1)} %collective-permute-done.7.refs_9_), channel_id=1, source_target_pairs={{0,112},{1,17},{16,0},{17,33},{32,16},{33,49},{48,32},{49,65},{64,... | collective-permute-start | bytes 786440 | tf_op jit(solution)/shard_map/ppermute | solution.py:26
  44.6 8.1 %collective-permute-start.16 = (bf16[16,8192]{1,0:T(8,128)(2,1)S(1)}, bf16[16,8192]{1,0:T(8,128)(2,1)S(1)}, u32[]{:S(2)}, u32[]{:S(2)}) collective-permute-start(bf16[16,8192]{1,0:T(8,128)(2,1)S(1)} %get-tuple-element.12.refs_0_), channel_id=1, source_target_pairs={{0,16},{1,113},{16,32},{17,1},{32,48},{33,17},{48,64},{49,33},{64,... | collective-permute-start | bytes 786440 | tf_op jit(solution)/shard_map/ppermute | solution.py:26
  46.0 11.4 %collective-permute-start.17 = (bf16[16,8192]{1,0:T(8,128)(2,1)S(1)}, bf16[16,8192]{1,0:T(8,128)(2,1)S(1)}, u32[]{:S(2)}, u32[]{:S(2)}) collective-permute-start(bf16[16,8192]{1,0:T(8,128)(2,1)S(1)} %get-tuple-element.13.refs_1_), channel_id=1, source_target_pairs={{0,112},{1,17},{16,0},{17,33},{32,16},{33,49},{48,32},{49,65},{64,... | collective-permute-start | bytes 786440 | tf_op jit(solution)/shard_map/ppermute | solution.py:26
  46.2 20.2 %collective-permute-start.22 = (bf16[32,8192]{1,0:T(8,128)(2,1)S(1)}, bf16[32,8192]{1,0:T(8,128)(2,1)S(1)}, u32[]{:S(2)}, u32[]{:S(2)}) collective-permute-start(bf16[32,8192]{1,0:T(8,128)(2,1)S(1)} %pad_maximum_fusion.2), channel_id=1, source_target_pairs={{0,128},{1,129},{16,144},{17,145},{32,160},{33,161},{48,176},{49,1... | collective-permute-start | bytes 1572872 | tf_op jit(solution)/shard_map/ppermute | solution.py:26
  49.6 10.5 %collective-permute-start.24 = (bf16[16,8192]{1,0:T(8,128)(2,1)S(1)}, bf16[16,8192]{1,0:T(8,128)(2,1)S(1)}, u32[]{:S(2)}, u32[]{:S(2)}) collective-permute-start(bf16[16,8192]{1,0:T(8,128)(2,1)S(1)} %collective-permute-done.18.refs_2_), channel_id=1, source_target_pairs={{0,16},{1,113},{16,32},{17,1},{32,48},{33,17},{48,64},{49,33},{64,... | collective-permute-start | bytes 786440 | tf_op jit(solution)/shard_map/ppermute | solution.py:26
  52.6 8.9 %collective-permute-start.20 = (bf16[16,8192]{1,0:T(8,128)(2,1)S(1)}, bf16[16,8192]{1,0:T(8,128)(2,1)S(1)}, u32[]{:S(2)}, u32[]{:S(2)}) collective-permute-start(bf16[16,8192]{1,0:T(8,128)(2,1)S(1)} %collective-permute-done.13.refs_4_), channel_id=1, source_target_pairs={{0,16},{1,113},{16,32},{17,1},{32,48},{33,17},{48,64},{49,33},{64,... | collective-permute-start | bytes 786440 | tf_op jit(solution)/shard_map/ppermute | solution.py:26
  54.9 9.3 %collective-permute-start.21 = (bf16[16,8192]{1,0:T(8,128)(2,1)S(1)}, bf16[16,8192]{1,0:T(8,128)(2,1)S(1)}, u32[]{:S(2)}, u32[]{:S(2)}) collective-permute-start(bf16[16,8192]{1,0:T(8,128)(2,1)S(1)} %collective-permute-done.14.refs_5_), channel_id=1, source_target_pairs={{0,112},{1,17},{16,0},{17,33},{32,16},{33,49},{48,32},{49,65},{64,... | collective-permute-start | bytes 786440 | tf_op jit(solution)/shard_map/ppermute | solution.py:26
  57.3 27.5 %copy-start.1 = (s32[512]{0:T(512)S(1)}, s32[512]{0:T(512)}, u32[]{:S(2)}) copy-start(s32[512]{0:T(512)} %constant.66.clone) | copy-start | bytes 6148
  57.3 27.5 %copy-start.2 = (s32[512]{0:T(512)S(1)}, s32[512]{0:T(512)}, u32[]{:S(2)}) copy-start(s32[512]{0:T(512)} %constant.67.clone) | copy-start | bytes 6148
  57.4 36.7 %copy-start.4 = (s32[512]{0:T(512)S(1)}, s32[512]{0:T(512)}, u32[]{:S(2)}) copy-start(s32[512]{0:T(512)} %param.8) | copy-start | bytes 6148
  57.4 9.0 %collective-permute-start.23 = (bf16[16,8192]{1,0:T(8,128)(2,1)S(1)}, bf16[16,8192]{1,0:T(8,128)(2,1)S(1)}, u32[]{:S(2)}, u32[]{:S(2)}) collective-permute-start(bf16[16,8192]{1,0:T(8,128)(2,1)S(1)} %get-tuple-element.15.refs_0_), channel_id=1, source_target_pairs={{0,16},{1,113},{16,32},{17,1},{32,48},{33,17},{48,64},{49,33},{64,... | collective-permute-start | bytes 786440 | tf_op jit(solution)/shard_map/ppermute | solution.py:26
  60.1 8.3 %collective-permute-start.26 = (bf16[16,8192]{1,0:T(8,128)(2,1)S(1)}, bf16[16,8192]{1,0:T(8,128)(2,1)S(1)}, u32[]{:S(2)}, u32[]{:S(2)}) collective-permute-start(bf16[16,8192]{1,0:T(8,128)(2,1)S(1)} %collective-permute-done.24.refs_8_), channel_id=1, source_target_pairs={{0,128},{1,129},{16,144},{17,145},{32,160},{33,161},{48,176},{49,1... | collective-permute-start | bytes 786440 | tf_op jit(solution)/shard_map/ppermute | solution.py:26
  61.6 7.6 %collective-permute-start.25 = (bf16[16,8192]{1,0:T(8,128)(2,1)S(1)}, bf16[16,8192]{1,0:T(8,128)(2,1)S(1)}, u32[]{:S(2)}, u32[]{:S(2)}) collective-permute-start(bf16[16,8192]{1,0:T(8,128)(2,1)S(1)} %collective-permute-done.20.refs_4_), channel_id=1, source_target_pairs={{0,16},{1,113},{16,32},{17,1},{32,48},{33,17},{48,64},{49,33},{64,... | collective-permute-start | bytes 786440 | tf_op jit(solution)/shard_map/ppermute | solution.py:26
  72.0 7.7 %collective-permute-start.27 = (f32[256,512]{1,0:T(8,128)S(1)}, f32[256,512]{1,0:T(8,128)S(1)}, u32[]{:S(2)}, u32[]{:S(2)}) collective-permute-start(f32[256,512]{1,0:T(8,128)S(1)} %get-tuple-element.18), channel_id=1, source_target_pairs={{0,1},{1,0},{16,17},{17,16},{32,33},{33,32},{48,49},{49,48},{64,65... | collective-permute-start | bytes 1572872 | tf_op jit(solution)/shard_map/ppermute | solution.py:26
  80.5 13.5 %all-to-all-start = ((f32[8,32,512]{2,1,0:T(8,128)}), f32[8,32,512]{2,1,0:T(8,128)S(1)}, u32[]{:S(2)}, u32[]{:S(2)}) async-start(f32[8,32,512]{2,1,0:T(8,128)} %bitcast.1), calls=%async_computation | async-start | bytes 1048576 | tf_op jit(solution)/shard_map/all_to_all | solution.py:191
  (2 other events, 30.8 us)

commit v4 on v3

--- a/solution.py
+++ b/solution.py
@@ -51,9 +51,8 @@
 
 
 GROUPS = (
-    tuple((0, u) for u in "ABPQ") + both(1, "ABPQ"),
-    both(2, "ABPQ"),
-    both(3, "ABPQ") + tuple((4, u) for u in "ABPQ"),
+    tuple((0, u) for u in "ABPQ") + both(1, "ABPQ") + both(2, "AB"),
+    both(2, "PQ") + both(3, "ABPQ") + tuple((4, u) for u in "ABPQ"),
 )
 CROSSINGS = ((0,), (1, -1), (2, -2), (3, -3), (4,))
 
@@ -174,16 +173,15 @@
     send("B", 2)
     send("P", 1)
     send_across(2, rows_across(2))
-    some, got["A", 2], got["A", -2] = product(core_of, resident, 0, got, [got["A", 2], got["A", -2]])
     send("A", 2)
+    some, got["P", 2], got["P", -2] = product(core_of, resident, 0, got, [got["P", 2], got["P", -2]])
     send("B", 3)
     send("P", 2)
     send_across(3, rows_across(3))
     send_across(4, rows_across(4))
-    most, got["A", 3] = product(core_of, resident, 1, got, [got["A", 3]], some)
     send("A", 3)
     send("P", 3)
-    keep, sent = product(core_of, resident, 2, got, [], most)
+    keep, sent = product(core_of, resident, 1, got, [], some)
 
     came = moved(sent, other_core)
     sums = (keep + came).reshape(8, 32, keep.shape[1])

time: 95.2 us -> 103 us (1.082)
  waiting for transfers between devices: 35.4 us -> 44.2 us
  local copies, waits for them, and re-layouts: 4.48 us -> 7.85 us
  Pallas kernels: 7.72 us -> 4.8 us
  starting transfers between devices: 45.3 us -> 43.6 us
    ppermute x28, waiting for transfers between devices: 26.2 us -> 35 us  [moved(): return lax.ppermute(values, BOTH, pairs)]
    unnamed x11 -> x13, local copies, waits for them, and re-layouts: 3.42 us -> 6.79 us
    pallas_call x3 -> x2, Pallas kernels: 7.72 us -> 4.8 us  [product(): pl.pallas_call(functools.partial(product_kernel, slots, arrays, len(held)...]
    ppermute x28, starting transfers between devices: 41 us -> 39 us  [moved(): return lax.ppermute(values, BOTH, pairs)]
  transfers between devices with their start and end apart: 29 -> 29, of which waited for: 13 -> 12; matrix products, arithmetic and copies ran while one was open for 0% -> 0% of each run, Pallas kernels for 5% -> 2%
where the time goes in v4:
time: 103 us
  waiting for transfers between devices  44.2 us (43%)
  starting transfers between devices  43.6 us (42%)
  local copies, waits for them, and re-layouts  7.85 us (8%)
  Pallas kernels  4.8 us (5%)
  other arithmetic  1.06 us (1%)
    ppermute x28, starting transfers between devices, moved(): return lax.ppermute(values, BOTH, pairs)  39 us
    ppermute x28, waiting for transfers between devices, moved(): return lax.ppermute(values, BOTH, pairs)  35 us
    all_to_all x1, waiting for transfers between devices, on_device(): apart = lax.all_to_all(sums, 'col', 0, 0, axis_index_groups=groups)  9.16 us
    unnamed x13, local copies, waits for them, and re-layouts  6.79 us
    pallas_call x2, Pallas kernels, product(): pl.pallas_call(functools.partial(product_kernel, slots, arrays, len(held)...  4.8 us
    all_to_all x1, starting transfers between devices, on_device(): apart = lax.all_to_all(sums, 'col', 0, 0, axis_index_groups=groups)  4.61 us
  transfers between devices with their start and end apart: 29, of which 12 were waited for; matrix products, arithmetic and copies ran while one was open for 0% of the time, Pallas kernels for 2%

profile of v4, /device:TPU:1, one launch (start us, length us, event | category | flops | bytes accessed | tf_op | source)
XLA Modules:
  0.0 102.6 jit_solution(13341753570594780067)
XLA Ops:
  0.0 1.1 %fusion.10 = (bf16[16,8192]{1,0:T(8,128)(2,1)S(1)}, bf16[16,8192]{1,0:T(8,128)(2,1)S(1)}) fusion(bf16[32,8192]{1,0:T(8,128)(2,1)} %param.7), kind=kLoop, calls=%fused_computation.24 | loop fusion | bytes 1048576 | tf_op jit(solution)/shard_map/slice | solution.py:156
  1.1 6.5 %collective-permute-start.4 = (bf16[16,8192]{1,0:T(8,128)(2,1)S(1)}, bf16[16,8192]{1,0:T(8,128)(2,1)S(1)}, u32[]{:S(2)}, u32[]{:S(2)}) collective-permute-start(bf16[16,8192]{1,0:T(8,128)(2,1)S(1)} %get-tuple-element.15.refs_1_), channel_id=1, source_target_pairs={{0,16},{1,113},{16,32},{17,1},{32,48},{33,17},{48,64},{49,33},{64,... | collective-permute-start | bytes 786440 | tf_op jit(solution)/shard_map/ppermute | solution.py:26
  7.6 2.9 %collective-permute-start = (bf16[16,8192]{1,0:T(8,128)(2,1)S(1)}, bf16[16,8192]{1,0:T(8,128)(2,1)S(1)}, u32[]{:S(2)}, u32[]{:S(2)}) collective-permute-start(bf16[16,8192]{1,0:T(8,128)(2,1)S(1)} %get-tuple-element.16.refs_0_), channel_id=1, source_target_pairs={{0,128},{1,129},{16,144},{17,145},{32,160},{33,161},{48,176},{49,1... | collective-permute-start | bytes 786440 | tf_op jit(solution)/shard_map/ppermute | solution.py:26
  10.5 2.7 %collective-permute-start.2 = (bf16[16,8192]{1,0:T(8,128)(2,1)S(1)}, bf16[16,8192]{1,0:T(8,128)(2,1)S(1)}, u32[]{:S(2)}, u32[]{:S(2)}) collective-permute-start(bf16[16,8192]{1,0:T(8,128)(2,1)S(1)} %get-tuple-element.16.refs_0_), channel_id=1, source_target_pairs={{0,16},{1,113},{16,32},{17,1},{32,48},{33,17},{48,64},{49,33},{64,... | collective-permute-start | bytes 786440 | tf_op jit(solution)/shard_map/ppermute | solution.py:26
  13.2 3.4 %copy-done = bf16[512,8192]{1,0:T(8,128)(2,1)S(1)} copy-done((bf16[512,8192]{1,0:T(8,128)(2,1)S(1)}, bf16[512,8192]{1,0:T(8,128)(2,1)}, u32[]{:S(2)}) %copy-start) | copy-done | bytes 8388632
  16.6 2.1 %collective-permute-start.11 = (bf16[16,8192]{1,0:T(8,128)(2,1)S(1)}, bf16[16,8192]{1,0:T(8,128)(2,1)S(1)}, u32[]{:S(2)}, u32[]{:S(2)}) collective-permute-start(bf16[16,8192]{1,0:T(8,128)(2,1)S(1)} %collective-permute-done.4.refs_6_), channel_id=1, source_target_pairs={{0,16},{1,113},{16,32},{17,1},{32,48},{33,17},{48,64},{49,33},{64,... | collective-permute-start | bytes 786440 | tf_op jit(solution)/shard_map/ppermute | solution.py:26
  18.8 0.9 collective-permute-start.6
  20.3 4.9 %collective-permute-done.1.refs_3_ = bf16[16,8192]{1,0:T(8,128)(2,1)S(1)} collective-permute-done((bf16[16,8192]{1,0:T(8,128)(2,1)S(1)}, bf16[16,8192]{1,0:T(8,128)(2,1)S(1)}, u32[]{:S(2)}, u32[]{:S(2)}) %collective-permute-start.1) | collective-permute-done | bytes 262176 | tf_op jit(solution)/shard_map/ppermute | solution.py:26
  25.2 2.7 %collective-permute-start.9 = (bf16[16,8192]{1,0:T(8,128)(2,1)S(1)}, bf16[16,8192]{1,0:T(8,128)(2,1)S(1)}, u32[]{:S(2)}, u32[]{:S(2)}) collective-permute-start(bf16[16,8192]{1,0:T(8,128)(2,1)S(1)} %collective-permute-done.2.refs_4_), channel_id=1, source_target_pairs={{0,16},{1,113},{16,32},{17,1},{32,48},{33,17},{48,64},{49,33},{64,... | collective-permute-start | bytes 786440 | tf_op jit(solution)/shard_map/ppermute | solution.py:26
  28.0 5.4 %collective-permute-done.12.refs_14_ = bf16[16,8192]{1,0:T(8,128)(2,1)S(1)} collective-permute-done((bf16[16,8192]{1,0:T(8,128)(2,1)S(1)}, bf16[16,8192]{1,0:T(8,128)(2,1)S(1)}, u32[]{:S(2)}, u32[]{:S(2)}) %collective-permute-start.12) | collective-permute-done | bytes 262176 | tf_op jit(solution)/shard_map/ppermute | solution.py:26
  33.4 5.1 %collective-permute-start.8 = (bf16[32,8192]{1,0:T(8,128)(2,1)S(1)}, bf16[32,8192]{1,0:T(8,128)(2,1)S(1)}, u32[]{:S(2)}, u32[]{:S(2)}) collective-permute-start(bf16[32,8192]{1,0:T(8,128)(2,1)S(1)} %pad_maximum_fusion), channel_id=1, source_target_pairs={{0,128},{1,129},{16,144},{17,145},{32,160},{33,161},{48,176},{49,1... | collective-permute-start | bytes 1572872 | tf_op jit(solution)/shard_map/ppermute | solution.py:26
  38.8 1.2 %collective-permute-start.14 = (bf16[16,8192]{1,0:T(8,128)(2,1)S(1)}, bf16[16,8192]{1,0:T(8,128)(2,1)S(1)}, u32[]{:S(2)}, u32[]{:S(2)}) collective-permute-start(bf16[16,8192]{1,0:T(8,128)(2,1)S(1)} %collective-permute-done.7.refs_9_), channel_id=1, source_target_pairs={{0,112},{1,17},{16,0},{17,33},{32,16},{33,49},{48,32},{49,65},{64,... | collective-permute-start | bytes 786440 | tf_op jit(solution)/shard_map/ppermute | solution.py:26
  40.0 1.5 %collective-permute-start.18 = (bf16[16,8192]{1,0:T(8,128)(2,1)S(1)}, bf16[16,8192]{1,0:T(8,128)(2,1)S(1)}, u32[]{:S(2)}, u32[]{:S(2)}) collective-permute-start(bf16[16,8192]{1,0:T(8,128)(2,1)S(1)} %collective-permute-done.11.refs_13_), channel_id=1, source_target_pairs={{0,16},{1,113},{16,32},{17,1},{32,48},{33,17},{48,64},{49,33},{64,... | collective-permute-start | bytes 786440 | tf_op jit(solution)/shard_map/ppermute | solution.py:26
  41.5 7.7 %collective-permute-done.8.refs_10_ = bf16[32,8192]{1,0:T(8,128)(2,1)S(1)} collective-permute-done((bf16[32,8192]{1,0:T(8,128)(2,1)S(1)}, bf16[32,8192]{1,0:T(8,128)(2,1)S(1)}, u32[]{:S(2)}, u32[]{:S(2)}) %collective-permute-start.8) | collective-permute-done | bytes 524320 | tf_op jit(solution)/shard_map/ppermute | solution.py:26
  49.2 3.1 %collective-permute-start.15 = (bf16[32,8192]{1,0:T(8,128)(2,1)S(1)}, bf16[32,8192]{1,0:T(8,128)(2,1)S(1)}, u32[]{:S(2)}, u32[]{:S(2)}) collective-permute-start(bf16[32,8192]{1,0:T(8,128)(2,1)S(1)} %pad_maximum_fusion.1), channel_id=1, source_target_pairs={{0,128},{1,129},{16,144},{17,145},{32,160},{33,161},{48,176},{49,1... | collective-permute-start | bytes 1572872 | tf_op jit(solution)/shard_map/ppermute | solution.py:26
  52.4 1.4 %collective-permute-start.17 = (bf16[16,8192]{1,0:T(8,128)(2,1)S(1)}, bf16[16,8192]{1,0:T(8,128)(2,1)S(1)}, u32[]{:S(2)}, u32[]{:S(2)}) collective-permute-start(bf16[16,8192]{1,0:T(8,128)(2,1)S(1)} %collective-permute-done.10.refs_12_), channel_id=1, source_target_pairs={{0,112},{1,17},{16,0},{17,33},{32,16},{33,49},{48,32},{49,65},{64,... | collective-permute-start | bytes 786440 | tf_op jit(solution)/shard_map/ppermute | solution.py:26
  53.8 3.4 %copy-done.1 = bf16[512,8192]{1,0:T(8,128)(2,1)S(1)} copy-done((bf16[512,8192]{1,0:T(8,128)(2,1)S(1)}, bf16[512,8192]{1,0:T(8,128)(2,1)}, u32[]{:S(2)}) %copy-start.1) | copy-done | bytes 8388632
  57.1 2.4 %shard_map.65 = (f32[512,256]{1,0:T(8,128)S(1)}, bf16[16,8192]{1,0:T(8,128)(2,1)S(1)}, bf16[16,8192]{1,0:T(8,128)(2,1)S(1)}) custom-call(s32[1]{0:T(128)} %bitcast.core_ref, bf16[512,8192]{1,0:T(8,128)(2,1)S(1)} %copy-done.1, bf16[16,8192]{1,0:T(8,128)(2,1)S(1)} %get-tuple-element.16.refs_0_, ...), custom_call_target="tpu_custom_call", output_to_operand_aliasing={{1}: (17, {}), {2}: (18, {})} | custom-call | flops 2147483648 | bytes 12582912 | tf_op jit(solution)/shard_map/pallas_call | solution.py:112
  59.5 1.4 %collective-permute-start.20 = (bf16[16,8192]{1,0:T(8,128)(2,1)S(1)}, bf16[16,8192]{1,0:T(8,128)(2,1)S(1)}, u32[]{:S(2)}, u32[]{:S(2)}) collective-permute-start(bf16[16,8192]{1,0:T(8,128)(2,1)S(1)} %get-tuple-element.10.refs_0_), channel_id=1, source_target_pairs={{0,16},{1,113},{16,32},{17,1},{32,48},{33,17},{48,64},{49,33},{64,... | collective-permute-start | bytes 786440 | tf_op jit(solution)/shard_map/ppermute | solution.py:26
  61.9 2.2 %collective-permute-start.24 = (bf16[16,8192]{1,0:T(8,128)(2,1)S(1)}, bf16[16,8192]{1,0:T(8,128)(2,1)S(1)}, u32[]{:S(2)}, u32[]{:S(2)}) collective-permute-start(bf16[16,8192]{1,0:T(8,128)(2,1)S(1)} %collective-permute-done.18.refs_5_), channel_id=1, source_target_pairs={{0,16},{1,113},{16,32},{17,1},{32,48},{33,17},{48,64},{49,33},{64,... | collective-permute-start | bytes 786440 | tf_op jit(solution)/shard_map/ppermute | solution.py:26
  64.1 1.7 %collective-permute-done.20.refs_7_ = bf16[16,8192]{1,0:T(8,128)(2,1)S(1)} collective-permute-done((bf16[16,8192]{1,0:T(8,128)(2,1)S(1)}, bf16[16,8192]{1,0:T(8,128)(2,1)S(1)}, u32[]{:S(2)}, u32[]{:S(2)}) %collective-permute-start.20) | collective-permute-done | bytes 262176 | tf_op jit(solution)/shard_map/ppermute | solution.py:26
  65.8 1.6 %collective-permute-start.23 = (bf16[16,8192]{1,0:T(8,128)(2,1)S(1)}, bf16[16,8192]{1,0:T(8,128)(2,1)S(1)}, u32[]{:S(2)}, u32[]{:S(2)}) collective-permute-start(bf16[16,8192]{1,0:T(8,128)(2,1)S(1)} %collective-permute-done.16.refs_3_), channel_id=1, source_target_pairs={{0,16},{1,113},{16,32},{17,1},{32,48},{33,17},{48,64},{49,33},{64,... | collective-permute-start | bytes 786440 | tf_op jit(solution)/shard_map/ppermute | solution.py:26
  67.3 2.7 %collective-permute-done.21.refs_8_ = bf16[16,8192]{1,0:T(8,128)(2,1)S(1)} collective-permute-done((bf16[16,8192]{1,0:T(8,128)(2,1)S(1)}, bf16[16,8192]{1,0:T(8,128)(2,1)S(1)}, u32[]{:S(2)}, u32[]{:S(2)}) %collective-permute-start.21) | collective-permute-done | bytes 262176 | tf_op jit(solution)/shard_map/ppermute | solution.py:26
  70.8 2.8 %collective-permute-done.23.refs_10_ = bf16[16,8192]{1,0:T(8,128)(2,1)S(1)} collective-permute-done((bf16[16,8192]{1,0:T(8,128)(2,1)S(1)}, bf16[16,8192]{1,0:T(8,128)(2,1)S(1)}, u32[]{:S(2)}, u32[]{:S(2)}) %collective-permute-start.23) | collective-permute-done | bytes 262176 | tf_op jit(solution)/shard_map/ppermute | solution.py:26
  73.6 2.8 %collective-permute-done.25.refs_12_ = bf16[16,8192]{1,0:T(8,128)(2,1)S(1)} collective-permute-done((bf16[16,8192]{1,0:T(8,128)(2,1)S(1)}, bf16[16,8192]{1,0:T(8,128)(2,1)S(1)}, u32[]{:S(2)}, u32[]{:S(2)}) %collective-permute-start.25) | collective-permute-done | bytes 262176 | tf_op jit(solution)/shard_map/ppermute | solution.py:26
  76.4 4.3 %collective-permute-done.26.refs_13_ = bf16[16,8192]{1,0:T(8,128)(2,1)S(1)} collective-permute-done((bf16[16,8192]{1,0:T(8,128)(2,1)S(1)}, bf16[16,8192]{1,0:T(8,128)(2,1)S(1)}, u32[]{:S(2)}, u32[]{:S(2)}) %collective-permute-start.26) | collective-permute-done | bytes 262176 | tf_op jit(solution)/shard_map/ppermute | solution.py:26
  80.6 2.4 %shard_map.66 = (f32[256,512]{1,0:T(8,128)S(1)}, f32[256,512]{1,0:T(8,128)S(1)}) custom-call(s32[1]{0:T(128)} %bitcast.core_ref, bf16[512,8192]{1,0:T(8,128)(2,1)S(1)} %copy-done.1, bf16[16,8192]{1,0:T(8,128)(2,1)S(1)} %get-tuple-element.10.refs_0_, bf16[16,8192]{1,0:T(8,128)(2,1)S(1)} %get-tuple-element.11.refs_1_, ...), custom_call_target="tpu_custom_call" | custom-call | flops 2147483648 | bytes 12582912 | tf_op jit(solution)/shard_map/pallas_call | solution.py:112
  83.1 2.2 %collective-permute-start.27 = (f32[256,512]{1,0:T(8,128)S(1)}, f32[256,512]{1,0:T(8,128)S(1)}, u32[]{:S(2)}, u32[]{:S(2)}) collective-permute-start(f32[256,512]{1,0:T(8,128)S(1)} %get-tuple-element.14), channel_id=1, source_target_pairs={{0,1},{1,0},{16,17},{17,16},{32,33},{33,32},{48,49},{49,48},{64,65... | collective-permute-start | bytes 1572872 | tf_op jit(solution)/shard_map/ppermute | solution.py:26
  85.3 1.5 %collective-permute-done.27 = f32[256,512]{1,0:T(8,128)S(1)} collective-permute-done((f32[256,512]{1,0:T(8,128)S(1)}, f32[256,512]{1,0:T(8,128)S(1)}, u32[]{:S(2)}, u32[]{:S(2)}) %collective-permute-start.27) | collective-permute-done | bytes 524320 | tf_op jit(solution)/shard_map/ppermute | solution.py:26
  87.7 4.6 %all-to-all-start = ((f32[8,32,512]{2,1,0:T(8,128)}), f32[8,32,512]{2,1,0:T(8,128)S(1)}, u32[]{:S(2)}, u32[]{:S(2)}) async-start(f32[8,32,512]{2,1,0:T(8,128)} %bitcast.1), calls=%async_computation | async-start | bytes 1048576 | tf_op jit(solution)/shard_map/all_to_all | solution.py:189
  92.4 9.2 %all-to-all-done = f32[8,32,512]{2,1,0:T(8,128)S(1)} async-done(((f32[8,32,512]{2,1,0:T(8,128)}), f32[8,32,512]{2,1,0:T(8,128)S(1)}, u32[]{:S(2)}, u32[]{:S(2)}) %all-to-all-start) | async-done | bytes 524320 | tf_op jit(solution)/shard_map/all_to_all | solution.py:189
  101.6 1.0 convolution_convert_fusion
  (50 shorter events, 3.8 us)
Async XLA Ops:
  1.1 15.5 %collective-permute-start.4 = (bf16[16,8192]{1,0:T(8,128)(2,1)S(1)}, bf16[16,8192]{1,0:T(8,128)(2,1)S(1)}, u32[]{:S(2)}, u32[]{:S(2)}) collective-permute-start(bf16[16,8192]{1,0:T(8,128)(2,1)S(1)} %get-tuple-element.15.refs_1_), channel_id=1, source_target_pairs={{0,16},{1,113},{16,32},{17,1},{32,48},{33,17},{48,64},{49,33},{64,... | collective-permute-start | bytes 786440 | tf_op jit(solution)/shard_map/ppermute | solution.py:26
  7.5 9.1 %collective-permute-start.5 = (bf16[16,8192]{1,0:T(8,128)(2,1)S(1)}, bf16[16,8192]{1,0:T(8,128)(2,1)S(1)}, u32[]{:S(2)}, u32[]{:S(2)}) collective-permute-start(bf16[16,8192]{1,0:T(8,128)(2,1)S(1)} %get-tuple-element.15.refs_1_), channel_id=1, source_target_pairs={{0,112},{1,17},{16,0},{17,33},{32,16},{33,49},{48,32},{49,65},{64,... | collective-permute-start | bytes 786440 | tf_op jit(solution)/shard_map/ppermute | solution.py:26
  7.6 11.2 %collective-permute-start = (bf16[16,8192]{1,0:T(8,128)(2,1)S(1)}, bf16[16,8192]{1,0:T(8,128)(2,1)S(1)}, u32[]{:S(2)}, u32[]{:S(2)}) collective-permute-start(bf16[16,8192]{1,0:T(8,128)(2,1)S(1)} %get-tuple-element.16.refs_0_), channel_id=1, source_target_pairs={{0,128},{1,129},{16,144},{17,145},{32,160},{33,161},{48,176},{49,1... | collective-permute-start | bytes 786440 | tf_op jit(solution)/shard_map/ppermute | solution.py:26
  10.5 9.2 %collective-permute-start.3 = (bf16[16,8192]{1,0:T(8,128)(2,1)S(1)}, bf16[16,8192]{1,0:T(8,128)(2,1)S(1)}, u32[]{:S(2)}, u32[]{:S(2)}) collective-permute-start(bf16[16,8192]{1,0:T(8,128)(2,1)S(1)} %get-tuple-element.16.refs_0_), channel_id=1, source_target_pairs={{0,112},{1,17},{16,0},{17,33},{32,16},{33,49},{48,32},{49,65},{64,... | collective-permute-start | bytes 786440 | tf_op jit(solution)/shard_map/ppermute | solution.py:26
  10.5 9.8 %collective-permute-start.2 = (bf16[16,8192]{1,0:T(8,128)(2,1)S(1)}, bf16[16,8192]{1,0:T(8,128)(2,1)S(1)}, u32[]{:S(2)}, u32[]{:S(2)}) collective-permute-start(bf16[16,8192]{1,0:T(8,128)(2,1)S(1)} %get-tuple-element.16.refs_0_), channel_id=1, source_target_pairs={{0,16},{1,113},{16,32},{17,1},{32,48},{33,17},{48,64},{49,33},{64,... | collective-permute-start | bytes 786440 | tf_op jit(solution)/shard_map/ppermute | solution.py:26
  16.6 8.7 %collective-permute-start.1 = (bf16[16,8192]{1,0:T(8,128)(2,1)S(1)}, bf16[16,8192]{1,0:T(8,128)(2,1)S(1)}, u32[]{:S(2)}, u32[]{:S(2)}) collective-permute-start(bf16[16,8192]{1,0:T(8,128)(2,1)S(1)} %shard_map.64), channel_id=1, source_target_pairs={{0,128},{1,129},{16,144},{17,145},{32,160},{33,161},{48,176},{49,1... | collective-permute-start | bytes 786440 | tf_op jit(solution)/shard_map/ppermute | solution.py:26
  16.6 8.6 %collective-permute-start.11 = (bf16[16,8192]{1,0:T(8,128)(2,1)S(1)}, bf16[16,8192]{1,0:T(8,128)(2,1)S(1)}, u32[]{:S(2)}, u32[]{:S(2)}) collective-permute-start(bf16[16,8192]{1,0:T(8,128)(2,1)S(1)} %collective-permute-done.4.refs_6_), channel_id=1, source_target_pairs={{0,16},{1,113},{16,32},{17,1},{32,48},{33,17},{48,64},{49,33},{64,... | collective-permute-start | bytes 786440 | tf_op jit(solution)/shard_map/ppermute | solution.py:26
  18.8 19.7 %collective-permute-start.6 = (bf16[16,8192]{1,0:T(8,128)(2,1)S(1)}, bf16[16,8192]{1,0:T(8,128)(2,1)S(1)}, u32[]{:S(2)}, u32[]{:S(2)}) collective-permute-start(bf16[16,8192]{1,0:T(8,128)(2,1)S(1)} %collective-permute-done.refs_2_), channel_id=1, source_target_pairs={{0,16},{1,113},{16,32},{17,1},{32,48},{33,17},{48,64},{49,33},{64,... | collective-permute-start | bytes 786440 | tf_op jit(solution)/shard_map/ppermute | solution.py:26
  19.6 19.1 %collective-permute-start.7 = (bf16[16,8192]{1,0:T(8,128)(2,1)S(1)}, bf16[16,8192]{1,0:T(8,128)(2,1)S(1)}, u32[]{:S(2)}, u32[]{:S(2)}) collective-permute-start(bf16[16,8192]{1,0:T(8,128)(2,1)S(1)} %collective-permute-done.refs_2_), channel_id=1, source_target_pairs={{0,112},{1,17},{16,0},{17,33},{32,16},{33,49},{48,32},{49,65},{64,... | collective-permute-start | bytes 786440 | tf_op jit(solution)/shard_map/ppermute | solution.py:26
  20.2 13.2 %collective-permute-start.12 = (bf16[16,8192]{1,0:T(8,128)(2,1)S(1)}, bf16[16,8192]{1,0:T(8,128)(2,1)S(1)}, u32[]{:S(2)}, u32[]{:S(2)}) collective-permute-start(bf16[16,8192]{1,0:T(8,128)(2,1)S(1)} %collective-permute-done.5.refs_7_), channel_id=1, source_target_pairs={{0,112},{1,17},{16,0},{17,33},{32,16},{33,49},{48,32},{49,65},{64,... | collective-permute-start | bytes 786440 | tf_op jit(solution)/shard_map/ppermute | solution.py:26
  25.2 14.7 %collective-permute-start.10 = (bf16[16,8192]{1,0:T(8,128)(2,1)S(1)}, bf16[16,8192]{1,0:T(8,128)(2,1)S(1)}, u32[]{:S(2)}, u32[]{:S(2)}) collective-permute-start(bf16[16,8192]{1,0:T(8,128)(2,1)S(1)} %collective-permute-done.3.refs_5_), channel_id=1, source_target_pairs={{0,112},{1,17},{16,0},{17,33},{32,16},{33,49},{48,32},{49,65},{64,... | collective-permute-start | bytes 786440 | tf_op jit(solution)/shard_map/ppermute | solution.py:26
  25.2 16.2 %collective-permute-start.9 = (bf16[16,8192]{1,0:T(8,128)(2,1)S(1)}, bf16[16,8192]{1,0:T(8,128)(2,1)S(1)}, u32[]{:S(2)}, u32[]{:S(2)}) collective-permute-start(bf16[16,8192]{1,0:T(8,128)(2,1)S(1)} %collective-permute-done.2.refs_4_), channel_id=1, source_target_pairs={{0,16},{1,113},{16,32},{17,1},{32,48},{33,17},{48,64},{49,33},{64,... | collective-permute-start | bytes 786440 | tf_op jit(solution)/shard_map/ppermute | solution.py:26
  33.4 15.8 %collective-permute-start.8 = (bf16[32,8192]{1,0:T(8,128)(2,1)S(1)}, bf16[32,8192]{1,0:T(8,128)(2,1)S(1)}, u32[]{:S(2)}, u32[]{:S(2)}) collective-permute-start(bf16[32,8192]{1,0:T(8,128)(2,1)S(1)} %pad_maximum_fusion), channel_id=1, source_target_pairs={{0,128},{1,129},{16,144},{17,145},{32,160},{33,161},{48,176},{49,1... | collective-permute-start | bytes 1572872 | tf_op jit(solution)/shard_map/ppermute | solution.py:26
  38.5 13.8 %collective-permute-start.13 = (bf16[16,8192]{1,0:T(8,128)(2,1)S(1)}, bf16[16,8192]{1,0:T(8,128)(2,1)S(1)}, u32[]{:S(2)}, u32[]{:S(2)}) collective-permute-start(bf16[16,8192]{1,0:T(8,128)(2,1)S(1)} %collective-permute-done.6.refs_8_), channel_id=1, source_target_pairs={{0,16},{1,113},{16,32},{17,1},{32,48},{33,17},{48,64},{49,33},{64,... | collective-permute-start | bytes 786440 | tf_op jit(solution)/shard_map/ppermute | solution.py:26
  38.8 13.6 %collective-permute-start.14 = (bf16[16,8192]{1,0:T(8,128)(2,1)S(1)}, bf16[16,8192]{1,0:T(8,128)(2,1)S(1)}, u32[]{:S(2)}, u32[]{:S(2)}) collective-permute-start(bf16[16,8192]{1,0:T(8,128)(2,1)S(1)} %collective-permute-done.7.refs_9_), channel_id=1, source_target_pairs={{0,112},{1,17},{16,0},{17,33},{32,16},{33,49},{48,32},{49,65},{64,... | collective-permute-start | bytes 786440 | tf_op jit(solution)/shard_map/ppermute | solution.py:26
  40.0 19.6 %collective-permute-start.18 = (bf16[16,8192]{1,0:T(8,128)(2,1)S(1)}, bf16[16,8192]{1,0:T(8,128)(2,1)S(1)}, u32[]{:S(2)}, u32[]{:S(2)}) collective-permute-start(bf16[16,8192]{1,0:T(8,128)(2,1)S(1)} %collective-permute-done.11.refs_13_), channel_id=1, source_target_pairs={{0,16},{1,113},{16,32},{17,1},{32,48},{33,17},{48,64},{49,33},{64,... | collective-permute-start | bytes 786440 | tf_op jit(solution)/shard_map/ppermute | solution.py:26
  41.4 19.5 %collective-permute-start.19 = (bf16[16,8192]{1,0:T(8,128)(2,1)S(1)}, bf16[16,8192]{1,0:T(8,128)(2,1)S(1)}, u32[]{:S(2)}, u32[]{:S(2)}) collective-permute-start(bf16[16,8192]{1,0:T(8,128)(2,1)S(1)} %collective-permute-done.12.refs_14_), channel_id=1, source_target_pairs={{0,112},{1,17},{16,0},{17,33},{32,16},{33,49},{48,32},{49,65},{64,... | collective-permute-start | bytes 786440 | tf_op jit(solution)/shard_map/ppermute | solution.py:26
  49.2 21.6 %collective-permute-start.15 = (bf16[32,8192]{1,0:T(8,128)(2,1)S(1)}, bf16[32,8192]{1,0:T(8,128)(2,1)S(1)}, u32[]{:S(2)}, u32[]{:S(2)}) collective-permute-start(bf16[32,8192]{1,0:T(8,128)(2,1)S(1)} %pad_maximum_fusion.1), channel_id=1, source_target_pairs={{0,128},{1,129},{16,144},{17,145},{32,160},{33,161},{48,176},{49,1... | collective-permute-start | bytes 1572872 | tf_op jit(solution)/shard_map/ppermute | solution.py:26
  52.3 8.9 %collective-permute-start.16 = (bf16[16,8192]{1,0:T(8,128)(2,1)S(1)}, bf16[16,8192]{1,0:T(8,128)(2,1)S(1)}, u32[]{:S(2)}, u32[]{:S(2)}) collective-permute-start(bf16[16,8192]{1,0:T(8,128)(2,1)S(1)} %collective-permute-done.9.refs_11_), channel_id=1, source_target_pairs={{0,16},{1,113},{16,32},{17,1},{32,48},{33,17},{48,64},{49,33},{64,... | collective-permute-start | bytes 786440 | tf_op jit(solution)/shard_map/ppermute | solution.py:26
  52.4 9.5 %collective-permute-start.17 = (bf16[16,8192]{1,0:T(8,128)(2,1)S(1)}, bf16[16,8192]{1,0:T(8,128)(2,1)S(1)}, u32[]{:S(2)}, u32[]{:S(2)}) collective-permute-start(bf16[16,8192]{1,0:T(8,128)(2,1)S(1)} %collective-permute-done.10.refs_12_), channel_id=1, source_target_pairs={{0,112},{1,17},{16,0},{17,33},{32,16},{33,49},{48,32},{49,65},{64,... | collective-permute-start | bytes 786440 | tf_op jit(solution)/shard_map/ppermute | solution.py:26
  59.5 6.3 %collective-permute-start.20 = (bf16[16,8192]{1,0:T(8,128)(2,1)S(1)}, bf16[16,8192]{1,0:T(8,128)(2,1)S(1)}, u32[]{:S(2)}, u32[]{:S(2)}) collective-permute-start(bf16[16,8192]{1,0:T(8,128)(2,1)S(1)} %get-tuple-element.10.refs_0_), channel_id=1, source_target_pairs={{0,16},{1,113},{16,32},{17,1},{32,48},{33,17},{48,64},{49,33},{64,... | collective-permute-start | bytes 786440 | tf_op jit(solution)/shard_map/ppermute | solution.py:26
  60.9 31.4 %copy-start.3 = (s32[512]{0:T(512)S(1)}, s32[512]{0:T(512)}, u32[]{:S(2)}) copy-start(s32[512]{0:T(512)} %constant.67.clone) | copy-start | bytes 6148
  60.9 31.4 %copy-start.4 = (s32[512]{0:T(512)S(1)}, s32[512]{0:T(512)}, u32[]{:S(2)}) copy-start(s32[512]{0:T(512)} %constant.68.clone) | copy-start | bytes 6148
  60.9 9.2 %collective-permute-start.21 = (bf16[16,8192]{1,0:T(8,128)(2,1)S(1)}, bf16[16,8192]{1,0:T(8,128)(2,1)S(1)}, u32[]{:S(2)}, u32[]{:S(2)}) collective-permute-start(bf16[16,8192]{1,0:T(8,128)(2,1)S(1)} %get-tuple-element.11.refs_1_), channel_id=1, source_target_pairs={{0,112},{1,17},{16,0},{17,33},{32,16},{33,49},{48,32},{49,65},{64,... | collective-permute-start | bytes 786440 | tf_op jit(solution)/shard_map/ppermute | solution.py:26
  61.2 40.4 %copy-start.5 = (s32[512]{0:T(512)S(1)}, s32[512]{0:T(512)}, u32[]{:S(2)}) copy-start(s32[512]{0:T(512)} %param.8) | copy-start | bytes 6148
  61.2 15.1 %collective-permute-start.22 = (bf16[32,8192]{1,0:T(8,128)(2,1)S(1)}, bf16[32,8192]{1,0:T(8,128)(2,1)S(1)}, u32[]{:S(2)}, u32[]{:S(2)}) collective-permute-start(bf16[32,8192]{1,0:T(8,128)(2,1)S(1)} %pad_maximum_fusion.2), channel_id=1, source_target_pairs={{0,128},{1,129},{16,144},{17,145},{32,160},{33,161},{48,176},{49,1... | collective-permute-start | bytes 1572872 | tf_op jit(solution)/shard_map/ppermute | solution.py:26
  61.9 8.8 %collective-permute-start.24 = (bf16[16,8192]{1,0:T(8,128)(2,1)S(1)}, bf16[16,8192]{1,0:T(8,128)(2,1)S(1)}, u32[]{:S(2)}, u32[]{:S(2)}) collective-permute-start(bf16[16,8192]{1,0:T(8,128)(2,1)S(1)} %collective-permute-done.18.refs_5_), channel_id=1, source_target_pairs={{0,16},{1,113},{16,32},{17,1},{32,48},{33,17},{48,64},{49,33},{64,... | collective-permute-start | bytes 786440 | tf_op jit(solution)/shard_map/ppermute | solution.py:26
  65.8 7.8 %collective-permute-start.23 = (bf16[16,8192]{1,0:T(8,128)(2,1)S(1)}, bf16[16,8192]{1,0:T(8,128)(2,1)S(1)}, u32[]{:S(2)}, u32[]{:S(2)}) collective-permute-start(bf16[16,8192]{1,0:T(8,128)(2,1)S(1)} %collective-permute-done.16.refs_3_), channel_id=1, source_target_pairs={{0,16},{1,113},{16,32},{17,1},{32,48},{33,17},{48,64},{49,33},{64,... | collective-permute-start | bytes 786440 | tf_op jit(solution)/shard_map/ppermute | solution.py:26
  70.1 6.3 %collective-permute-start.25 = (bf16[16,8192]{1,0:T(8,128)(2,1)S(1)}, bf16[16,8192]{1,0:T(8,128)(2,1)S(1)}, u32[]{:S(2)}, u32[]{:S(2)}) collective-permute-start(bf16[16,8192]{1,0:T(8,128)(2,1)S(1)} %collective-permute-done.20.refs_7_), channel_id=1, source_target_pairs={{0,16},{1,113},{16,32},{17,1},{32,48},{33,17},{48,64},{49,33},{64,... | collective-permute-start | bytes 786440 | tf_op jit(solution)/shard_map/ppermute | solution.py:26
  70.8 9.9 %collective-permute-start.26 = (bf16[16,8192]{1,0:T(8,128)(2,1)S(1)}, bf16[16,8192]{1,0:T(8,128)(2,1)S(1)}, u32[]{:S(2)}, u32[]{:S(2)}) collective-permute-start(bf16[16,8192]{1,0:T(8,128)(2,1)S(1)} %collective-permute-done.24.refs_11_), channel_id=1, source_target_pairs={{0,128},{1,129},{16,144},{17,145},{32,160},{33,161},{48,176},{49,1... | collective-permute-start | bytes 786440 | tf_op jit(solution)/shard_map/ppermute | solution.py:26
  83.1 3.8 %collective-permute-start.27 = (f32[256,512]{1,0:T(8,128)S(1)}, f32[256,512]{1,0:T(8,128)S(1)}, u32[]{:S(2)}, u32[]{:S(2)}) collective-permute-start(f32[256,512]{1,0:T(8,128)S(1)} %get-tuple-element.14), channel_id=1, source_target_pairs={{0,1},{1,0},{16,17},{17,16},{32,33},{33,32},{48,49},{49,48},{64,65... | collective-permute-start | bytes 1572872 | tf_op jit(solution)/shard_map/ppermute | solution.py:26
  87.7 13.8 %all-to-all-start = ((f32[8,32,512]{2,1,0:T(8,128)}), f32[8,32,512]{2,1,0:T(8,128)S(1)}, u32[]{:S(2)}, u32[]{:S(2)}) async-start(f32[8,32,512]{2,1,0:T(8,128)} %bitcast.1), calls=%async_computation | async-start | bytes 1048576 | tf_op jit(solution)/shard_map/all_to_all | solution.py:189
  (3 other events, 38.2 us)

commit v5 on v3

--- a/solution.py
+++ b/solution.py
@@ -174,10 +174,10 @@
     send("B", 2)
     send("P", 1)
     send_across(2, rows_across(2))
-    some, got["A", 2], got["A", -2] = product(core_of, resident, 0, got, [got["A", 2], got["A", -2]])
-    send("A", 2)
+    some, got["B", 3], got["B", -3] = product(core_of, resident, 0, got, [got["B", 3], got["B", -3]])
     send("B", 3)
     send("P", 2)
+    send("A", 2)
     send_across(3, rows_across(3))
     send_across(4, rows_across(4))
     most, got["A", 3] = product(core_of, resident, 1, got, [got["A", 3]], some)

time: 95.2 us -> 97.5 us (1.024)
  starting transfers between devices: 45.3 us -> 48.9 us
  waiting for transfers between devices: 35.4 us -> 34.1 us
    ppermute x28, starting transfers between devices: 41 us -> 44.6 us  [moved(): return lax.ppermute(values, BOTH, pairs)]
    ppermute x28, waiting for transfers between devices: 26.2 us -> 24.9 us  [moved(): return lax.ppermute(values, BOTH, pairs)]
where the time goes in v5:
time: 97.5 us; the launch traced here: 97.3 us
  starting transfers between devices  48.9 us (50%)
  waiting for transfers between devices  34.1 us (35%)
  Pallas kernels  7.73 us (8%)
  local copies, waits for them, and re-layouts  4.48 us (5%)
  other arithmetic  1.03 us (1%)
    ppermute x28, starting transfers between devices, moved(): return lax.ppermute(values, BOTH, pairs)  44.6 us
    ppermute x28, waiting for transfers between devices, moved(): return lax.ppermute(values, BOTH, pairs)  24.9 us
    all_to_all x1, waiting for transfers between devices, on_device(): apart = lax.all_to_all(sums, 'col', 0, 0, axis_index_groups=groups)  9.16 us
    pallas_call x3, Pallas kernels, product(): pl.pallas_call(functools.partial(product_kernel, slots, arrays, len(held)...  7.73 us
    all_to_all x1, starting transfers between devices, on_device(): apart = lax.all_to_all(sums, 'col', 0, 0, axis_index_groups=groups)  4.23 us
    unnamed x11, local copies, waits for them, and re-layouts  3.42 us
  transfers between devices with their start and end apart: 29, of which 13 were waited for; matrix products, arithmetic and copies ran while one was open for 0% of the time, Pallas kernels for 5%

profile of v5, /device:TPU:1, one launch (start us, length us, event | category | flops | bytes accessed | tf_op | source)
XLA Modules:
  0.0 97.3 jit_solution(4476711391877494984)
XLA Ops:
  0.0 1.1 %fusion.10 = (bf16[16,8192]{1,0:T(8,128)(2,1)S(1)}, bf16[16,8192]{1,0:T(8,128)(2,1)S(1)}) fusion(bf16[32,8192]{1,0:T(8,128)(2,1)} %param.7), kind=kLoop, calls=%fused_computation.24 | loop fusion | bytes 1048576 | tf_op jit(solution)/shard_map/slice | solution.py:157
  1.1 6.5 %collective-permute-start.4 = (bf16[16,8192]{1,0:T(8,128)(2,1)S(1)}, bf16[16,8192]{1,0:T(8,128)(2,1)S(1)}, u32[]{:S(2)}, u32[]{:S(2)}) collective-permute-start(bf16[16,8192]{1,0:T(8,128)(2,1)S(1)} %get-tuple-element.19.refs_1_), channel_id=1, source_target_pairs={{0,16},{1,113},{16,32},{17,1},{32,48},{33,17},{48,64},{49,33},{64,... | collective-permute-start | bytes 786440 | tf_op jit(solution)/shard_map/ppermute | solution.py:26
  7.5 2.9 %collective-permute-start.8 = (bf16[16,8192]{1,0:T(8,128)(2,1)S(1)}, bf16[16,8192]{1,0:T(8,128)(2,1)S(1)}, u32[]{:S(2)}, u32[]{:S(2)}) collective-permute-start(bf16[16,8192]{1,0:T(8,128)(2,1)S(1)} %get-tuple-element.20.refs_0_), channel_id=1, source_target_pairs={{0,128},{1,129},{16,144},{17,145},{32,160},{33,161},{48,176},{49,1... | collective-permute-start | bytes 786440 | tf_op jit(solution)/shard_map/ppermute | solution.py:26
  10.5 2.7 %collective-permute-start = (bf16[16,8192]{1,0:T(8,128)(2,1)S(1)}, bf16[16,8192]{1,0:T(8,128)(2,1)S(1)}, u32[]{:S(2)}, u32[]{:S(2)}) collective-permute-start(bf16[16,8192]{1,0:T(8,128)(2,1)S(1)} %get-tuple-element.20.refs_0_), channel_id=1, source_target_pairs={{0,16},{1,113},{16,32},{17,1},{32,48},{33,17},{48,64},{49,33},{64,... | collective-permute-start | bytes 786440 | tf_op jit(solution)/shard_map/ppermute | solution.py:26
  13.2 3.4 %copy-done = bf16[512,8192]{1,0:T(8,128)(2,1)S(1)} copy-done((bf16[512,8192]{1,0:T(8,128)(2,1)S(1)}, bf16[512,8192]{1,0:T(8,128)(2,1)}, u32[]{:S(2)}) %copy-start) | copy-done | bytes 8388632
  16.7 1.5 %collective-permute-done.6.refs_7_ = bf16[16,8192]{1,0:T(8,128)(2,1)S(1)} collective-permute-done((bf16[16,8192]{1,0:T(8,128)(2,1)S(1)}, bf16[16,8192]{1,0:T(8,128)(2,1)S(1)}, u32[]{:S(2)}, u32[]{:S(2)}) %collective-permute-start.6) | collective-permute-done | bytes 262176 | tf_op jit(solution)/shard_map/ppermute | solution.py:26
  18.1 1.3 %collective-permute-start.9 = (bf16[16,8192]{1,0:T(8,128)(2,1)S(1)}, bf16[16,8192]{1,0:T(8,128)(2,1)S(1)}, u32[]{:S(2)}, u32[]{:S(2)}) collective-permute-start(bf16[16,8192]{1,0:T(8,128)(2,1)S(1)} %collective-permute-done.8.refs_2_), channel_id=1, source_target_pairs={{0,16},{1,113},{16,32},{17,1},{32,48},{33,17},{48,64},{49,33},{64,... | collective-permute-start | bytes 786440 | tf_op jit(solution)/shard_map/ppermute | solution.py:26
  19.4 3.3 %collective-permute-start.5 = (bf16[16,8192]{1,0:T(8,128)(2,1)S(1)}, bf16[16,8192]{1,0:T(8,128)(2,1)S(1)}, u32[]{:S(2)}, u32[]{:S(2)}) collective-permute-start(bf16[16,8192]{1,0:T(8,128)(2,1)S(1)} %collective-permute-done.4.refs_6_), channel_id=1, source_target_pairs={{0,16},{1,113},{16,32},{17,1},{32,48},{33,17},{48,64},{49,33},{64,... | collective-permute-start | bytes 786440 | tf_op jit(solution)/shard_map/ppermute | solution.py:26
  22.7 1.2 %collective-permute-done.15.refs_3_ = bf16[16,8192]{1,0:T(8,128)(2,1)S(1)} collective-permute-done((bf16[16,8192]{1,0:T(8,128)(2,1)S(1)}, bf16[16,8192]{1,0:T(8,128)(2,1)S(1)}, u32[]{:S(2)}, u32[]{:S(2)}) %collective-permute-start.15) | collective-permute-done | bytes 262176 | tf_op jit(solution)/shard_map/ppermute | solution.py:26
  24.1 7.1 %collective-permute-done.5.refs_2_ = bf16[16,8192]{1,0:T(8,128)(2,1)S(1)} collective-permute-done((bf16[16,8192]{1,0:T(8,128)(2,1)S(1)}, bf16[16,8192]{1,0:T(8,128)(2,1)S(1)}, u32[]{:S(2)}, u32[]{:S(2)}) %collective-permute-start.5) | collective-permute-done | bytes 262176 | tf_op jit(solution)/shard_map/ppermute | solution.py:26
  31.2 3.4 %collective-permute-start.1 = (bf16[16,8192]{1,0:T(8,128)(2,1)S(1)}, bf16[16,8192]{1,0:T(8,128)(2,1)S(1)}, u32[]{:S(2)}, u32[]{:S(2)}) collective-permute-start(bf16[16,8192]{1,0:T(8,128)(2,1)S(1)} %collective-permute-done.refs_4_), channel_id=1, source_target_pairs={{0,16},{1,113},{16,32},{17,1},{32,48},{33,17},{48,64},{49,33},{64,... | collective-permute-start | bytes 786440 | tf_op jit(solution)/shard_map/ppermute | solution.py:26
  34.7 2.7 %collective-permute-start.17 = (bf16[16,8192]{1,0:T(8,128)(2,1)S(1)}, bf16[16,8192]{1,0:T(8,128)(2,1)S(1)}, u32[]{:S(2)}, u32[]{:S(2)}) collective-permute-start(bf16[16,8192]{1,0:T(8,128)(2,1)S(1)} %collective-permute-done.5.refs_2_), channel_id=1, source_target_pairs={{0,16},{1,113},{16,32},{17,1},{32,48},{33,17},{48,64},{49,33},{64,... | collective-permute-start | bytes 786440 | tf_op jit(solution)/shard_map/ppermute | solution.py:26
  38.0 3.3 %collective-permute-start.13 = (bf16[32,8192]{1,0:T(8,128)(2,1)S(1)}, bf16[32,8192]{1,0:T(8,128)(2,1)S(1)}, u32[]{:S(2)}, u32[]{:S(2)}) collective-permute-start(bf16[32,8192]{1,0:T(8,128)(2,1)S(1)} %pad_maximum_fusion), channel_id=1, source_target_pairs={{0,128},{1,129},{16,144},{17,145},{32,160},{33,161},{48,176},{49,1... | collective-permute-start | bytes 1572872 | tf_op jit(solution)/shard_map/ppermute | solution.py:26
  41.3 2.6 %collective-permute-done.3.refs_1_ = bf16[16,8192]{1,0:T(8,128)(2,1)S(1)} collective-permute-done((bf16[16,8192]{1,0:T(8,128)(2,1)S(1)}, bf16[16,8192]{1,0:T(8,128)(2,1)S(1)}, u32[]{:S(2)}, u32[]{:S(2)}) %collective-permute-start.3) | collective-permute-done | bytes 262176 | tf_op jit(solution)/shard_map/ppermute | solution.py:26
  45.4 2.0 %collective-permute-start.14 = (bf16[16,8192]{1,0:T(8,128)(2,1)S(1)}, bf16[16,8192]{1,0:T(8,128)(2,1)S(1)}, u32[]{:S(2)}, u32[]{:S(2)}) collective-permute-start(bf16[16,8192]{1,0:T(8,128)(2,1)S(1)} %collective-permute-done.1.refs_0_), channel_id=1, source_target_pairs={{0,16},{1,113},{16,32},{17,1},{32,48},{33,17},{48,64},{49,33},{64,... | collective-permute-start | bytes 786440 | tf_op jit(solution)/shard_map/ppermute | solution.py:26
  47.4 2.2 %collective-permute-done.18.refs_12_ = bf16[16,8192]{1,0:T(8,128)(2,1)S(1)} collective-permute-done((bf16[16,8192]{1,0:T(8,128)(2,1)S(1)}, bf16[16,8192]{1,0:T(8,128)(2,1)S(1)}, u32[]{:S(2)}, u32[]{:S(2)}) %collective-permute-start.18) | collective-permute-done | bytes 262176 | tf_op jit(solution)/shard_map/ppermute | solution.py:26
  49.6 2.6 %shard_map.65 = (f32[512,192]{1,0:T(8,128)S(1)}, bf16[16,8192]{1,0:T(8,128)(2,1)S(1)}, bf16[16,8192]{1,0:T(8,128)(2,1)S(1)}) custom-call(s32[1]{0:T(128)} %bitcast.core_ref, bf16[512,8192]{1,0:T(8,128)(2,1)S(1)} %copy-done, bf16[16,8192]{1,0:T(8,128)(2,1)S(1)} %get-tuple-element.20.refs_0_, ...), custom_call_target="tpu_custom_call", output_to_operand_aliasing={{1}: (13, {}), {2}: (14, {})} | custom-call | flops 1610612736 | bytes 11534336 | tf_op jit(solution)/shard_map/pallas_call | solution.py:113
  52.2 2.8 %collective-permute-start.24 = (bf16[16,8192]{1,0:T(8,128)(2,1)S(1)}, bf16[16,8192]{1,0:T(8,128)(2,1)S(1)}, u32[]{:S(2)}, u32[]{:S(2)}) collective-permute-start(bf16[16,8192]{1,0:T(8,128)(2,1)S(1)} %get-tuple-element.14.refs_2_), channel_id=1, source_target_pairs={{0,16},{1,113},{16,32},{17,1},{32,48},{33,17},{48,64},{49,33},{64,... | collective-permute-start | bytes 786440 | tf_op jit(solution)/shard_map/ppermute | solution.py:26
  55.2 1.3 %collective-permute-start.22 = (bf16[32,8192]{1,0:T(8,128)(2,1)S(1)}, bf16[32,8192]{1,0:T(8,128)(2,1)S(1)}, u32[]{:S(2)}, u32[]{:S(2)}) collective-permute-start(bf16[32,8192]{1,0:T(8,128)(2,1)S(1)} %pad_maximum_fusion.2), channel_id=1, source_target_pairs={{0,128},{1,129},{16,144},{17,145},{32,160},{33,161},{48,176},{49,1... | collective-permute-start | bytes 1572872 | tf_op jit(solution)/shard_map/ppermute | solution.py:26
  56.5 1.7 %collective-permute-start.20 = (bf16[16,8192]{1,0:T(8,128)(2,1)S(1)}, bf16[16,8192]{1,0:T(8,128)(2,1)S(1)}, u32[]{:S(2)}, u32[]{:S(2)}) collective-permute-start(bf16[16,8192]{1,0:T(8,128)(2,1)S(1)} %collective-permute-done.10.refs_4_), channel_id=1, source_target_pairs={{0,16},{1,113},{16,32},{17,1},{32,48},{33,17},{48,64},{49,33},{64,... | collective-permute-start | bytes 786440 | tf_op jit(solution)/shard_map/ppermute | solution.py:26
  58.2 2.4 %shard_map.66 = (f32[512,320]{1,0:T(8,128)S(1)}, bf16[16,8192]{1,0:T(8,128)(2,1)S(1)}) custom-call(s32[1]{0:T(128)} %bitcast.core_ref, bf16[512,8192]{1,0:T(8,128)(2,1)S(1)} %copy-done, bf16[16,8192]{1,0:T(8,128)(2,1)S(1)} %collective-permute-done.1.refs_0_, bf16[16,8192]{1,0:T(8,128)(2,1)S(1)} %collective-permute-done.3.refs_1_, ...), custom_call_target="tpu_custom_call", output_to_operand_aliasing={{1}: (9, {})} | custom-call | flops 1073741824 | bytes 10485760 | tf_op jit(solution)/shard_map/pallas_call | solution.py:113
  60.8 2.6 %collective-permute-start.23 = (bf16[16,8192]{1,0:T(8,128)(2,1)S(1)}, bf16[16,8192]{1,0:T(8,128)(2,1)S(1)}, u32[]{:S(2)}, u32[]{:S(2)}) collective-permute-start(bf16[16,8192]{1,0:T(8,128)(2,1)S(1)} %get-tuple-element.13.refs_0_), channel_id=1, source_target_pairs={{0,16},{1,113},{16,32},{17,1},{32,48},{33,17},{48,64},{49,33},{64,... | collective-permute-start | bytes 786440 | tf_op jit(solution)/shard_map/ppermute | solution.py:26
  63.4 2.2 %collective-permute-start.26 = (bf16[16,8192]{1,0:T(8,128)(2,1)S(1)}, bf16[16,8192]{1,0:T(8,128)(2,1)S(1)}, u32[]{:S(2)}, u32[]{:S(2)}) collective-permute-start(bf16[16,8192]{1,0:T(8,128)(2,1)S(1)} %collective-permute-done.24.refs_8_), channel_id=1, source_target_pairs={{0,128},{1,129},{16,144},{17,145},{32,160},{33,161},{48,176},{49,1... | collective-permute-start | bytes 786440 | tf_op jit(solution)/shard_map/ppermute | solution.py:26
  65.6 1.1 %collective-permute-start.25 = (bf16[16,8192]{1,0:T(8,128)(2,1)S(1)}, bf16[16,8192]{1,0:T(8,128)(2,1)S(1)}, u32[]{:S(2)}, u32[]{:S(2)}) collective-permute-start(bf16[16,8192]{1,0:T(8,128)(2,1)S(1)} %collective-permute-done.20.refs_4_), channel_id=1, source_target_pairs={{0,16},{1,113},{16,32},{17,1},{32,48},{33,17},{48,64},{49,33},{64,... | collective-permute-start | bytes 786440 | tf_op jit(solution)/shard_map/ppermute | solution.py:26
  67.4 1.3 %collective-permute-done.22.refs_6_ = bf16[32,8192]{1,0:T(8,128)(2,1)S(1)} collective-permute-done((bf16[32,8192]{1,0:T(8,128)(2,1)S(1)}, bf16[32,8192]{1,0:T(8,128)(2,1)S(1)}, u32[]{:S(2)}, u32[]{:S(2)}) %collective-permute-start.22) | collective-permute-done | bytes 524320 | tf_op jit(solution)/shard_map/ppermute | solution.py:26
  68.8 5.6 %collective-permute-done.26.refs_10_ = bf16[16,8192]{1,0:T(8,128)(2,1)S(1)} collective-permute-done((bf16[16,8192]{1,0:T(8,128)(2,1)S(1)}, bf16[16,8192]{1,0:T(8,128)(2,1)S(1)}, u32[]{:S(2)}, u32[]{:S(2)}) %collective-permute-start.26) | collective-permute-done | bytes 262176 | tf_op jit(solution)/shard_map/ppermute | solution.py:26
  74.4 2.8 %shard_map.67 = (f32[256,512]{1,0:T(8,128)S(1)}, f32[256,512]{1,0:T(8,128)S(1)}) custom-call(s32[1]{0:T(128)} %bitcast.core_ref, bf16[512,8192]{1,0:T(8,128)(2,1)S(1)} %copy-done, bf16[16,8192]{1,0:T(8,128)(2,1)S(1)} %get-tuple-element.13.refs_0_, bf16[16,8192]{1,0:T(8,128)(2,1)S(1)} %collective-permute-done.19.refs_1_, ...), custom_call_target="tpu_custom_call" | custom-call | flops 1610612736 | bytes 11534336 | tf_op jit(solution)/shard_map/pallas_call | solution.py:113
  77.2 3.3 %collective-permute-start.27 = (f32[256,512]{1,0:T(8,128)S(1)}, f32[256,512]{1,0:T(8,128)S(1)}, u32[]{:S(2)}, u32[]{:S(2)}) collective-permute-start(f32[256,512]{1,0:T(8,128)S(1)} %get-tuple-element.18), channel_id=1, source_target_pairs={{0,1},{1,0},{16,17},{17,16},{32,33},{33,32},{48,49},{49,48},{64,65... | collective-permute-start | bytes 1572872 | tf_op jit(solution)/shard_map/ppermute | solution.py:26
  80.5 1.5 %collective-permute-done.27 = f32[256,512]{1,0:T(8,128)S(1)} collective-permute-done((f32[256,512]{1,0:T(8,128)S(1)}, f32[256,512]{1,0:T(8,128)S(1)}, u32[]{:S(2)}, u32[]{:S(2)}) %collective-permute-start.27) | collective-permute-done | bytes 524320 | tf_op jit(solution)/shard_map/ppermute | solution.py:26
  82.9 4.2 %all-to-all-start = ((f32[8,32,512]{2,1,0:T(8,128)}), f32[8,32,512]{2,1,0:T(8,128)S(1)}, u32[]{:S(2)}, u32[]{:S(2)}) async-start(f32[8,32,512]{2,1,0:T(8,128)} %bitcast.1), calls=%async_computation | async-start | bytes 1048576 | tf_op jit(solution)/shard_map/all_to_all | solution.py:191
  87.1 9.2 %all-to-all-done = f32[8,32,512]{2,1,0:T(8,128)S(1)} async-done(((f32[8,32,512]{2,1,0:T(8,128)}), f32[8,32,512]{2,1,0:T(8,128)S(1)}, u32[]{:S(2)}, u32[]{:S(2)}) %all-to-all-start) | async-done | bytes 524320 | tf_op jit(solution)/shard_map/all_to_all | solution.py:191
  96.4 1.0 convolution_convert_fusion
  (49 shorter events, 4.6 us)
Async XLA Ops:
  1.1 15.5 %collective-permute-start.4 = (bf16[16,8192]{1,0:T(8,128)(2,1)S(1)}, bf16[16,8192]{1,0:T(8,128)(2,1)S(1)}, u32[]{:S(2)}, u32[]{:S(2)}) collective-permute-start(bf16[16,8192]{1,0:T(8,128)(2,1)S(1)} %get-tuple-element.19.refs_1_), channel_id=1, source_target_pairs={{0,16},{1,113},{16,32},{17,1},{32,48},{33,17},{48,64},{49,33},{64,... | collective-permute-start | bytes 786440 | tf_op jit(solution)/shard_map/ppermute | solution.py:26
  7.5 9.1 %collective-permute-start.8 = (bf16[16,8192]{1,0:T(8,128)(2,1)S(1)}, bf16[16,8192]{1,0:T(8,128)(2,1)S(1)}, u32[]{:S(2)}, u32[]{:S(2)}) collective-permute-start(bf16[16,8192]{1,0:T(8,128)(2,1)S(1)} %get-tuple-element.20.refs_0_), channel_id=1, source_target_pairs={{0,128},{1,129},{16,144},{17,145},{32,160},{33,161},{48,176},{49,1... | collective-permute-start | bytes 786440 | tf_op jit(solution)/shard_map/ppermute | solution.py:26
  10.5 7.7 %collective-permute-start.6 = (bf16[16,8192]{1,0:T(8,128)(2,1)S(1)}, bf16[16,8192]{1,0:T(8,128)(2,1)S(1)}, u32[]{:S(2)}, u32[]{:S(2)}) collective-permute-start(bf16[16,8192]{1,0:T(8,128)(2,1)S(1)} %get-tuple-element.19.refs_1_), channel_id=1, source_target_pairs={{0,112},{1,17},{16,0},{17,33},{32,16},{33,49},{48,32},{49,65},{64,... | collective-permute-start | bytes 786440 | tf_op jit(solution)/shard_map/ppermute | solution.py:26
  10.5 9.0 %collective-permute-start = (bf16[16,8192]{1,0:T(8,128)(2,1)S(1)}, bf16[16,8192]{1,0:T(8,128)(2,1)S(1)}, u32[]{:S(2)}, u32[]{:S(2)}) collective-permute-start(bf16[16,8192]{1,0:T(8,128)(2,1)S(1)} %get-tuple-element.20.refs_0_), channel_id=1, source_target_pairs={{0,16},{1,113},{16,32},{17,1},{32,48},{33,17},{48,64},{49,33},{64,... | collective-permute-start | bytes 786440 | tf_op jit(solution)/shard_map/ppermute | solution.py:26
  13.1 9.6 %collective-permute-start.2 = (bf16[16,8192]{1,0:T(8,128)(2,1)S(1)}, bf16[16,8192]{1,0:T(8,128)(2,1)S(1)}, u32[]{:S(2)}, u32[]{:S(2)}) collective-permute-start(bf16[16,8192]{1,0:T(8,128)(2,1)S(1)} %get-tuple-element.20.refs_0_), channel_id=1, source_target_pairs={{0,112},{1,17},{16,0},{17,33},{32,16},{33,49},{48,32},{49,65},{64,... | collective-permute-start | bytes 786440 | tf_op jit(solution)/shard_map/ppermute | solution.py:26
  16.6 7.4 %collective-permute-start.15 = (bf16[16,8192]{1,0:T(8,128)(2,1)S(1)}, bf16[16,8192]{1,0:T(8,128)(2,1)S(1)}, u32[]{:S(2)}, u32[]{:S(2)}) collective-permute-start(bf16[16,8192]{1,0:T(8,128)(2,1)S(1)} %shard_map.64), channel_id=1, source_target_pairs={{0,128},{1,129},{16,144},{17,145},{32,160},{33,161},{48,176},{49,1... | collective-permute-start | bytes 786440 | tf_op jit(solution)/shard_map/ppermute | solution.py:26
  16.6 18.0 %collective-permute-start.11 = (bf16[16,8192]{1,0:T(8,128)(2,1)S(1)}, bf16[16,8192]{1,0:T(8,128)(2,1)S(1)}, u32[]{:S(2)}, u32[]{:S(2)}) collective-permute-start(bf16[16,8192]{1,0:T(8,128)(2,1)S(1)} %collective-permute-done.8.refs_2_), channel_id=1, source_target_pairs={{0,112},{1,17},{16,0},{17,33},{32,16},{33,49},{48,32},{49,65},{64,... | collective-permute-start | bytes 786440 | tf_op jit(solution)/shard_map/ppermute | solution.py:26
  18.1 19.2 %collective-permute-start.9 = (bf16[16,8192]{1,0:T(8,128)(2,1)S(1)}, bf16[16,8192]{1,0:T(8,128)(2,1)S(1)}, u32[]{:S(2)}, u32[]{:S(2)}) collective-permute-start(bf16[16,8192]{1,0:T(8,128)(2,1)S(1)} %collective-permute-done.8.refs_2_), channel_id=1, source_target_pairs={{0,16},{1,113},{16,32},{17,1},{32,48},{33,17},{48,64},{49,33},{64,... | collective-permute-start | bytes 786440 | tf_op jit(solution)/shard_map/ppermute | solution.py:26
  19.4 11.8 %collective-permute-start.5 = (bf16[16,8192]{1,0:T(8,128)(2,1)S(1)}, bf16[16,8192]{1,0:T(8,128)(2,1)S(1)}, u32[]{:S(2)}, u32[]{:S(2)}) collective-permute-start(bf16[16,8192]{1,0:T(8,128)(2,1)S(1)} %collective-permute-done.4.refs_6_), channel_id=1, source_target_pairs={{0,16},{1,113},{16,32},{17,1},{32,48},{33,17},{48,64},{49,33},{64,... | collective-permute-start | bytes 786440 | tf_op jit(solution)/shard_map/ppermute | solution.py:26
  22.7 11.9 %collective-permute-start.7 = (bf16[16,8192]{1,0:T(8,128)(2,1)S(1)}, bf16[16,8192]{1,0:T(8,128)(2,1)S(1)}, u32[]{:S(2)}, u32[]{:S(2)}) collective-permute-start(bf16[16,8192]{1,0:T(8,128)(2,1)S(1)} %collective-permute-done.6.refs_7_), channel_id=1, source_target_pairs={{0,112},{1,17},{16,0},{17,33},{32,16},{33,49},{48,32},{49,65},{64,... | collective-permute-start | bytes 786440 | tf_op jit(solution)/shard_map/ppermute | solution.py:26
  24.0 20.7 %collective-permute-start.16 = (bf16[32,8192]{1,0:T(8,128)(2,1)S(1)}, bf16[32,8192]{1,0:T(8,128)(2,1)S(1)}, u32[]{:S(2)}, u32[]{:S(2)}) collective-permute-start(bf16[32,8192]{1,0:T(8,128)(2,1)S(1)} %pad_maximum_fusion.1), channel_id=1, source_target_pairs={{0,128},{1,129},{16,144},{17,145},{32,160},{33,161},{48,176},{49,1... | collective-permute-start | bytes 1572872 | tf_op jit(solution)/shard_map/ppermute | solution.py:26
  31.2 6.7 %collective-permute-start.1 = (bf16[16,8192]{1,0:T(8,128)(2,1)S(1)}, bf16[16,8192]{1,0:T(8,128)(2,1)S(1)}, u32[]{:S(2)}, u32[]{:S(2)}) collective-permute-start(bf16[16,8192]{1,0:T(8,128)(2,1)S(1)} %collective-permute-done.refs_4_), channel_id=1, source_target_pairs={{0,16},{1,113},{16,32},{17,1},{32,48},{33,17},{48,64},{49,33},{64,... | collective-permute-start | bytes 786440 | tf_op jit(solution)/shard_map/ppermute | solution.py:26
  34.6 9.3 %collective-permute-start.3 = (bf16[16,8192]{1,0:T(8,128)(2,1)S(1)}, bf16[16,8192]{1,0:T(8,128)(2,1)S(1)}, u32[]{:S(2)}, u32[]{:S(2)}) collective-permute-start(bf16[16,8192]{1,0:T(8,128)(2,1)S(1)} %collective-permute-done.2.refs_5_), channel_id=1, source_target_pairs={{0,112},{1,17},{16,0},{17,33},{32,16},{33,49},{48,32},{49,65},{64,... | collective-permute-start | bytes 786440 | tf_op jit(solution)/shard_map/ppermute | solution.py:26
  34.7 10.8 %collective-permute-start.17 = (bf16[16,8192]{1,0:T(8,128)(2,1)S(1)}, bf16[16,8192]{1,0:T(8,128)(2,1)S(1)}, u32[]{:S(2)}, u32[]{:S(2)}) collective-permute-start(bf16[16,8192]{1,0:T(8,128)(2,1)S(1)} %collective-permute-done.5.refs_2_), channel_id=1, source_target_pairs={{0,16},{1,113},{16,32},{17,1},{32,48},{33,17},{48,64},{49,33},{64,... | collective-permute-start | bytes 786440 | tf_op jit(solution)/shard_map/ppermute | solution.py:26
  37.3 12.2 %collective-permute-start.18 = (bf16[16,8192]{1,0:T(8,128)(2,1)S(1)}, bf16[16,8192]{1,0:T(8,128)(2,1)S(1)}, u32[]{:S(2)}, u32[]{:S(2)}) collective-permute-start(bf16[16,8192]{1,0:T(8,128)(2,1)S(1)} %collective-permute-done.7.refs_3_), channel_id=1, source_target_pairs={{0,112},{1,17},{16,0},{17,33},{32,16},{33,49},{48,32},{49,65},{64,... | collective-permute-start | bytes 786440 | tf_op jit(solution)/shard_map/ppermute | solution.py:26
  38.0 20.2 %collective-permute-start.13 = (bf16[32,8192]{1,0:T(8,128)(2,1)S(1)}, bf16[32,8192]{1,0:T(8,128)(2,1)S(1)}, u32[]{:S(2)}, u32[]{:S(2)}) collective-permute-start(bf16[32,8192]{1,0:T(8,128)(2,1)S(1)} %pad_maximum_fusion), channel_id=1, source_target_pairs={{0,128},{1,129},{16,144},{17,145},{32,160},{33,161},{48,176},{49,1... | collective-permute-start | bytes 1572872 | tf_op jit(solution)/shard_map/ppermute | solution.py:26
  43.9 8.2 %collective-permute-start.10 = (bf16[16,8192]{1,0:T(8,128)(2,1)S(1)}, bf16[16,8192]{1,0:T(8,128)(2,1)S(1)}, u32[]{:S(2)}, u32[]{:S(2)}) collective-permute-start(bf16[16,8192]{1,0:T(8,128)(2,1)S(1)} %collective-permute-done.9.refs_8_), channel_id=1, source_target_pairs={{0,16},{1,113},{16,32},{17,1},{32,48},{33,17},{48,64},{49,33},{64,... | collective-permute-start | bytes 786440 | tf_op jit(solution)/shard_map/ppermute | solution.py:26
  44.7 10.5 %collective-permute-start.12 = (bf16[16,8192]{1,0:T(8,128)(2,1)S(1)}, bf16[16,8192]{1,0:T(8,128)(2,1)S(1)}, u32[]{:S(2)}, u32[]{:S(2)}) collective-permute-start(bf16[16,8192]{1,0:T(8,128)(2,1)S(1)} %collective-permute-done.11.refs_9_), channel_id=1, source_target_pairs={{0,112},{1,17},{16,0},{17,33},{32,16},{33,49},{48,32},{49,65},{64,... | collective-permute-start | bytes 786440 | tf_op jit(solution)/shard_map/ppermute | solution.py:26
  45.4 11.1 %collective-permute-start.14 = (bf16[16,8192]{1,0:T(8,128)(2,1)S(1)}, bf16[16,8192]{1,0:T(8,128)(2,1)S(1)}, u32[]{:S(2)}, u32[]{:S(2)}) collective-permute-start(bf16[16,8192]{1,0:T(8,128)(2,1)S(1)} %collective-permute-done.1.refs_0_), channel_id=1, source_target_pairs={{0,16},{1,113},{16,32},{17,1},{32,48},{33,17},{48,64},{49,33},{64,... | collective-permute-start | bytes 786440 | tf_op jit(solution)/shard_map/ppermute | solution.py:26
  49.6 11.2 %collective-permute-start.19 = (bf16[16,8192]{1,0:T(8,128)(2,1)S(1)}, bf16[16,8192]{1,0:T(8,128)(2,1)S(1)}, u32[]{:S(2)}, u32[]{:S(2)}) collective-permute-start(bf16[16,8192]{1,0:T(8,128)(2,1)S(1)} %collective-permute-done.3.refs_1_), channel_id=1, source_target_pairs={{0,112},{1,17},{16,0},{17,33},{32,16},{33,49},{48,32},{49,65},{64,... | collective-permute-start | bytes 786440 | tf_op jit(solution)/shard_map/ppermute | solution.py:26
  52.2 11.2 %collective-permute-start.24 = (bf16[16,8192]{1,0:T(8,128)(2,1)S(1)}, bf16[16,8192]{1,0:T(8,128)(2,1)S(1)}, u32[]{:S(2)}, u32[]{:S(2)}) collective-permute-start(bf16[16,8192]{1,0:T(8,128)(2,1)S(1)} %get-tuple-element.14.refs_2_), channel_id=1, source_target_pairs={{0,16},{1,113},{16,32},{17,1},{32,48},{33,17},{48,64},{49,33},{64,... | collective-permute-start | bytes 786440 | tf_op jit(solution)/shard_map/ppermute | solution.py:26
  55.2 13.6 %collective-permute-start.22 = (bf16[32,8192]{1,0:T(8,128)(2,1)S(1)}, bf16[32,8192]{1,0:T(8,128)(2,1)S(1)}, u32[]{:S(2)}, u32[]{:S(2)}) collective-permute-start(bf16[32,8192]{1,0:T(8,128)(2,1)S(1)} %pad_maximum_fusion.2), channel_id=1, source_target_pairs={{0,128},{1,129},{16,144},{17,145},{32,160},{33,161},{48,176},{49,1... | collective-permute-start | bytes 1572872 | tf_op jit(solution)/shard_map/ppermute | solution.py:26
  56.5 9.1 %collective-permute-start.20 = (bf16[16,8192]{1,0:T(8,128)(2,1)S(1)}, bf16[16,8192]{1,0:T(8,128)(2,1)S(1)}, u32[]{:S(2)}, u32[]{:S(2)}) collective-permute-start(bf16[16,8192]{1,0:T(8,128)(2,1)S(1)} %collective-permute-done.10.refs_4_), channel_id=1, source_target_pairs={{0,16},{1,113},{16,32},{17,1},{32,48},{33,17},{48,64},{49,33},{64,... | collective-permute-start | bytes 786440 | tf_op jit(solution)/shard_map/ppermute | solution.py:26
  58.2 9.3 %collective-permute-start.21 = (bf16[16,8192]{1,0:T(8,128)(2,1)S(1)}, bf16[16,8192]{1,0:T(8,128)(2,1)S(1)}, u32[]{:S(2)}, u32[]{:S(2)}) collective-permute-start(bf16[16,8192]{1,0:T(8,128)(2,1)S(1)} %collective-permute-done.12.refs_5_), channel_id=1, source_target_pairs={{0,112},{1,17},{16,0},{17,33},{32,16},{33,49},{48,32},{49,65},{64,... | collective-permute-start | bytes 786440 | tf_op jit(solution)/shard_map/ppermute | solution.py:26
  60.6 26.5 %copy-start.1 = (s32[512]{0:T(512)S(1)}, s32[512]{0:T(512)}, u32[]{:S(2)}) copy-start(s32[512]{0:T(512)} %constant.66.clone) | copy-start | bytes 6148
  60.6 26.5 %copy-start.2 = (s32[512]{0:T(512)S(1)}, s32[512]{0:T(512)}, u32[]{:S(2)}) copy-start(s32[512]{0:T(512)} %constant.67.clone) | copy-start | bytes 6148
  60.6 35.7 %copy-start.4 = (s32[512]{0:T(512)S(1)}, s32[512]{0:T(512)}, u32[]{:S(2)}) copy-start(s32[512]{0:T(512)} %param.8) | copy-start | bytes 6148
  60.8 8.0 %collective-permute-start.23 = (bf16[16,8192]{1,0:T(8,128)(2,1)S(1)}, bf16[16,8192]{1,0:T(8,128)(2,1)S(1)}, u32[]{:S(2)}, u32[]{:S(2)}) collective-permute-start(bf16[16,8192]{1,0:T(8,128)(2,1)S(1)} %get-tuple-element.13.refs_0_), channel_id=1, source_target_pairs={{0,16},{1,113},{16,32},{17,1},{32,48},{33,17},{48,64},{49,33},{64,... | collective-permute-start | bytes 786440 | tf_op jit(solution)/shard_map/ppermute | solution.py:26
  63.4 11.0 %collective-permute-start.26 = (bf16[16,8192]{1,0:T(8,128)(2,1)S(1)}, bf16[16,8192]{1,0:T(8,128)(2,1)S(1)}, u32[]{:S(2)}, u32[]{:S(2)}) collective-permute-start(bf16[16,8192]{1,0:T(8,128)(2,1)S(1)} %collective-permute-done.24.refs_8_), channel_id=1, source_target_pairs={{0,128},{1,129},{16,144},{17,145},{32,160},{33,161},{48,176},{49,1... | collective-permute-start | bytes 786440 | tf_op jit(solution)/shard_map/ppermute | solution.py:26
  65.6 8.8 %collective-permute-start.25 = (bf16[16,8192]{1,0:T(8,128)(2,1)S(1)}, bf16[16,8192]{1,0:T(8,128)(2,1)S(1)}, u32[]{:S(2)}, u32[]{:S(2)}) collective-permute-start(bf16[16,8192]{1,0:T(8,128)(2,1)S(1)} %collective-permute-done.20.refs_4_), channel_id=1, source_target_pairs={{0,16},{1,113},{16,32},{17,1},{32,48},{33,17},{48,64},{49,33},{64,... | collective-permute-start | bytes 786440 | tf_op jit(solution)/shard_map/ppermute | solution.py:26
  77.2 4.8 %collective-permute-start.27 = (f32[256,512]{1,0:T(8,128)S(1)}, f32[256,512]{1,0:T(8,128)S(1)}, u32[]{:S(2)}, u32[]{:S(2)}) collective-permute-start(f32[256,512]{1,0:T(8,128)S(1)} %get-tuple-element.18), channel_id=1, source_target_pairs={{0,1},{1,0},{16,17},{17,16},{32,33},{33,32},{48,49},{49,48},{64,65... | collective-permute-start | bytes 1572872 | tf_op jit(solution)/shard_map/ppermute | solution.py:26
  82.9 13.4 %all-to-all-start = ((f32[8,32,512]{2,1,0:T(8,128)}), f32[8,32,512]{2,1,0:T(8,128)S(1)}, u32[]{:S(2)}, u32[]{:S(2)}) async-start(f32[8,32,512]{2,1,0:T(8,128)} %bitcast.1), calls=%async_computation | async-start | bytes 1048576 | tf_op jit(solution)/shard_map/all_to_all | solution.py:191
  (2 other events, 29.9 us)
